TPU v7x, 32 devices: a whole 2x2x4 slice. The times are simulated.
32 devices in a mesh: seq: 8 (over z, x), ch: 4 (over y, core).
Axes of the slice: x: 2, y: 2, z: 4, core: 2. Of those that a mesh axis runs over, the one named last changes fastest.
Arguments:
- token_ids: int32 [16, 2048], P(None, 'seq'), may hold values from 0 to 255
- counts: int32 [16], replicated, may hold values from 1024 to 2048, as said below
- embedding: bfloat16 [256, 512], replicated, may hold values from -6 to 6
- gain_one: float32 [512], replicated, may hold values from 0.5 to 1.5
- ema_rate: float32 [512, 16], P('ch'), may hold values from 4.8828126e-05 to 0.05
- ema_beta: float32 [512, 16], P('ch'), may hold values from -6 to 6
- ema_eta: float32 [512, 16], P('ch'), may hold values from -3 to 3
- ema_omega: float32 [512], P('ch'), may hold values from -5 to 5
- w_value: bfloat16 [512, 1024], P(None, 'ch'), may hold values from -0.25 to 0.25
- w_reset: bfloat16 [512, 1024], P(None, 'ch'), may hold values from -0.25 to 0.25
- w_z: bfloat16 [512, 128], replicated, may hold values from -0.25 to 0.25
- z_scale: float32 [2, 128], replicated, may hold values from -6 to 6
- z_offset: float32 [2, 128], replicated, may hold values from -3 to 3
- position_bias: float32 [255], replicated, may hold values from -3 to 3
- w_update: bfloat16 [512, 512], P(None, 'ch'), may hold values from -0.25 to 0.25
- w_cand: bfloat16 [512, 512], P(None, 'ch'), may hold values from -0.25 to 0.25
- w_out: bfloat16 [1024, 512], P('ch'), may hold values from -0.375 to 0.375
- gain_two: float32 [512], replicated, may hold values from 0.5 to 1.5
- w_up: bfloat16 [512, 1024], P(None, 'ch'), may hold values from -0.25 to 0.25
- w_down: bfloat16 [1024, 512], P('ch'), may hold values from -0.1875 to 0.1875
- cotangent: bfloat16 [16, 2048, 512], P(None, 'seq'), may hold values from -6 to 6
Outputs:
- output: float32 [16, 2048, 512], P(None, 'seq')
- input_grad: float32 [16, 2048, 512], P(None, 'seq')
- grad_embedding: float32 [256, 512], replicated
- grad_gain_one: float32 [512], replicated
- grad_ema_rate: float32 [512, 16], P('ch')
- grad_ema_beta: float32 [512, 16], P('ch')
- grad_ema_eta: float32 [512, 16], P('ch')
- grad_ema_omega: float32 [512], P('ch')
- grad_w_value: float32 [512, 1024], P(None, 'ch')
- grad_w_reset: float32 [512, 1024], P(None, 'ch')
- grad_w_z: float32 [512, 128], replicated
- grad_z_scale: float32 [2, 128], replicated
- grad_z_offset: float32 [2, 128], replicated
- grad_position_bias: float32 [255], replicated
- grad_w_update: float32 [512, 512], P(None, 'ch')
- grad_w_cand: float32 [512, 512], P(None, 'ch')
- grad_w_out: float32 [1024, 512], P('ch')
- grad_gain_two: float32 [512], replicated
- grad_w_up: float32 [512, 1024], P(None, 'ch')
- grad_w_down: float32 [1024, 512], P('ch')
Inputs may be any that keep to these rules, and one draw needn't show every extreme that they name: Valid positions of each sequence; positions from counts on are padding; some sequence is full.
All inputs are finite; a program needn't handle non-finite values.
Results may differ from a plain program's by a relative error of at most 0.024.
Values may be sent and summed in bfloat16 or wider, within the bound.
No kernel may reach another device: no remote copies, remote signals or barrier semaphores. Data moves between devices by JAX's collectives and lax.ppermute only.
A program may use at most 320 MiB of HBM per device.

v0:
```python
import jax
import jax.numpy as jnp
from jax import lax
from jax.sharding import PartitionSpec as P

C = 128


EPS = 1e-05


def prefix(value, axis, join, neutral, backward):
    count, mine = (lax.axis_size(axis), lax.axis_index(axis))
    pieces = jax.tree.map(lambda part: lax.all_gather(part, axis), value)
    if backward:
        pieces = jax.tree.map(lambda part: part[::-1], pieces)
        mine = count - 1 - mine
    total = jax.tree.map(
        lambda part, zero: jnp.full_like(part, 0) + jnp.asarray(zero, part.dtype), value, neutral
    )

    def step(position, total):
        longer = join(total, jax.tree.map(lambda part: part[position], pieces))
        return jax.tree.map(lambda new, old: jnp.where(position < mine, new, old), longer, total)

    return lax.fori_loop(0, count - 1, step, total)


def silu_slope(values):
    sigmoid_val = jax.nn.sigmoid(values)
    return sigmoid_val * (1.0 + values * (1.0 - sigmoid_val))


def norm_forward(values, gain):
    inverse = lax.rsqrt(jnp.mean(values * values, axis=-1, keepdims=True) + EPS)
    unit_val = values * inverse
    return (unit_val * gain, unit_val, inverse)


def norm_backward(grad_after, gain, unit_val, inverse):
    scaled = grad_after * gain
    grad_before = inverse * (
        scaled - unit_val * jnp.mean(scaled * unit_val, axis=-1, keepdims=True)
    )
    return (grad_before, jnp.sum(grad_after * unit_val, axis=0))


def pair_chain(earlier, later):
    return (earlier[0] * later[0], later[0] * earlier[1] + later[1])


def ema_tables(ema_rate, ema_beta, ema_eta, span):
    rate_t = ema_rate.T
    decay = jnp.exp(-rate_t)
    lags = jnp.arange(span, dtype=jnp.float32)
    powers = jnp.exp(-rate_t[None] * lags[:, None, None])
    coeff = (1.0 - decay) * ema_beta.T
    kernel = jnp.sum(ema_eta.T[None] * coeff[None] * powers, axis=1)
    steps_idx = jnp.arange(span, dtype=jnp.int32)
    lag_idx = steps_idx[:, None] - steps_idx[None, :]
    toeplitz = jnp.where((lag_idx >= 0)[:, :, None], kernel[jnp.maximum(lag_idx, 0)], 0.0)
    return (toeplitz, powers, coeff, decay)


def local_leaving(inputs, ema_rate, ema_beta, ema_eta):
    span = inputs.shape[1]
    _, powers, coeff, _ = ema_tables(ema_rate, ema_beta, ema_eta, span)
    return jnp.einsum(
        "sjc,bsc->bjc", powers[::-1] * coeff[None], inputs, precision=lax.Precision.HIGHEST
    )


def whole_ema(inputs, entering, ema_rate, ema_beta, ema_eta, ema_omega):
    span = inputs.shape[1]
    toeplitz, powers, coeff, decay = ema_tables(ema_rate, ema_beta, ema_eta, span)
    inside = jnp.einsum("tsc,bsc->btc", toeplitz, inputs, precision=lax.Precision.HIGHEST)
    later_powers = powers * decay[None]
    carried = jnp.einsum(
        "tjc,bjc->btc", later_powers * ema_eta.T[None], entering, precision=lax.Precision.HIGHEST
    )
    ema_sum = inside + carried + ema_omega * inputs
    leaving = (
        jnp.einsum(
            "sjc,bsc->bjc", powers[::-1] * coeff[None], inputs, precision=lax.Precision.HIGHEST
        )
        + later_powers[-1][None] * entering
    )
    return (ema_sum, leaving)


def bias_matrix(position_bias, span):
    padded = jnp.concatenate([position_bias, jnp.zeros((1,), jnp.float32)])
    tiled = jnp.tile(padded, span)[span - 1 : span - 1 + span * (2 * span - 1)]
    return tiled.reshape(span, 2 * span - 1)[:, :span]


def bias_gradient(summed, span):
    flipped = summed[::-1]
    padded = jnp.concatenate([flipped, jnp.zeros((span, span), jnp.float32)], axis=1)
    skewed = padded.reshape(-1)[: span * (2 * span - 1)].reshape(span, 2 * span - 1)
    return jnp.sum(skewed, axis=0)


def local(
    token_ids,
    counts,
    embedding,
    gain_one,
    ema_rate,
    ema_beta,
    ema_eta,
    ema_omega,
    w_value,
    w_reset,
    w_z,
    z_scale,
    z_offset,
    position_bias,
    w_update,
    w_cand,
    w_out,
    gain_two,
    w_up,
    w_down,
    cotangent,
):
    batch, seg_len = token_ids.shape
    vocab, width = embedding.shape
    channels = ema_rate.shape[0]
    z_width = w_z.shape[1]
    rows = batch * seg_len
    blocks = rows // C
    position = lax.axis_index("seq")
    column = lax.axis_index("ch") * channels
    places = position * seg_len + jnp.arange(seg_len, dtype=jnp.int32)
    present = (places[None, :] < counts[:, None]).astype(jnp.float32).reshape(rows, 1)
    one_hot = (token_ids.reshape(rows, 1) == jnp.arange(vocab, dtype=jnp.int32)[None, :]).astype(
        jnp.bfloat16
    )
    embedded = jnp.dot(one_hot, embedding, preferred_element_type=jnp.float32) * present
    normed, unit_one, inverse_one = norm_forward(embedded, gain_one)
    ema_in = lax.dynamic_slice_in_dim(normed, column, channels, 1).reshape(batch, seg_len, channels)
    leaving = local_leaving(ema_in, ema_rate, ema_beta, ema_eta)
    rate_span = ema_rate.T * seg_len
    transfer = jnp.broadcast_to(jnp.exp(-rate_span), leaving.shape)
    nothing = jnp.zeros_like(leaving)
    entering = prefix(
        (transfer, leaving), "seq", pair_chain, (jnp.ones_like(leaving), nothing), False
    )[1]

    def ema_map(inputs, rate_arg, beta_arg, eta_arg, omega_arg):
        return whole_ema(inputs, entering, rate_arg, beta_arg, eta_arg, omega_arg)

    (ema_sum, _), ema_pull = jax.vjp(ema_map, ema_in, ema_rate, ema_beta, ema_eta, ema_omega)
    ema_act = jax.nn.silu(ema_sum).astype(jnp.bfloat16).reshape(rows, channels)
    ema_full = lax.all_gather(ema_act, "ch", axis=1, tiled=True)
    normed_low = normed.astype(jnp.bfloat16)
    value_pre = jnp.dot(normed_low, w_value, preferred_element_type=jnp.float32)
    values = jax.nn.silu(value_pre).astype(jnp.bfloat16)
    reset_pre = jnp.dot(ema_full, w_reset, preferred_element_type=jnp.float32)
    reset = jax.nn.silu(reset_pre)
    z_pre = jnp.dot(ema_full, w_z, preferred_element_type=jnp.float32)
    z_act = jax.nn.silu(z_pre)
    query = (z_act * z_scale[0] + z_offset[0]).astype(jnp.bfloat16).reshape(blocks, C, z_width)
    keys = (z_act * z_scale[1] + z_offset[1]).astype(jnp.bfloat16).reshape(blocks, C, z_width)
    factor = z_width ** (-0.5)
    causal = jnp.arange(C)[:, None] >= jnp.arange(C)[None, :]
    bias_table = bias_matrix(position_bias, C)
    scores = jnp.einsum("kqz,kpz->kqp", query, keys, preferred_element_type=jnp.float32) * factor
    scores = jnp.where(causal[None], scores + bias_table[None], -1e30)
    shifted = jnp.exp(scores - jnp.max(scores, axis=-1, keepdims=True))
    weights_soft = shifted / jnp.sum(shifted, axis=-1, keepdims=True)
    weights_low = weights_soft.astype(jnp.bfloat16)
    value_blocks = values.reshape(blocks, C, -1)
    mixed = jnp.einsum(
        "kqp,kpv->kqv", weights_low, value_blocks, preferred_element_type=jnp.float32
    ).reshape(rows, -1)
    gated = (reset * mixed).astype(jnp.bfloat16)
    recurrent = lax.psum_scatter(
        jnp.dot(gated, w_out, preferred_element_type=jnp.float32),
        "ch",
        scatter_dimension=1,
        tiled=True,
    )
    update = jax.nn.sigmoid(jnp.dot(ema_full, w_update, preferred_element_type=jnp.float32))
    cand_pre = jnp.dot(ema_full, w_cand, preferred_element_type=jnp.float32) + recurrent
    cand = jax.nn.silu(cand_pre)
    embedded_own = lax.dynamic_slice_in_dim(embedded, column, channels, 1)
    resid_own = update * cand + (1.0 - update) * embedded_own
    resid = lax.all_gather(resid_own, "ch", axis=1, tiled=True)
    ff_norm, unit_two, inverse_two = norm_forward(resid, gain_two)
    ff_in = ff_norm.astype(jnp.bfloat16)
    up_pre = jnp.dot(ff_in, w_up, preferred_element_type=jnp.float32)
    hidden = jax.nn.silu(up_pre).astype(jnp.bfloat16)
    output = resid + lax.psum(
        jnp.dot(hidden, w_down, preferred_element_type=jnp.float32).astype(jnp.bfloat16), "ch"
    ).astype(jnp.float32)
    grad_out = cotangent.reshape(rows, width).astype(jnp.float32) * present
    grad_low = grad_out.astype(jnp.bfloat16)
    grad_hidden = jnp.dot(grad_low, w_down.T, preferred_element_type=jnp.float32)
    grad_up = (grad_hidden * silu_slope(up_pre)).astype(jnp.bfloat16)
    grad_w_down = jnp.dot(hidden.T, grad_low, preferred_element_type=jnp.float32)
    grad_w_up = jnp.dot(ff_in.T, grad_up, preferred_element_type=jnp.float32)
    grad_ff_norm = lax.psum(jnp.dot(grad_up, w_up.T, preferred_element_type=jnp.float32), "ch")
    grad_part, grad_gain_two = norm_backward(grad_ff_norm, gain_two, unit_two, inverse_two)
    grad_resid = grad_out + grad_part
    resid_own_grad = lax.dynamic_slice_in_dim(grad_resid, column, channels, 1)
    grad_cand_pre = (resid_own_grad * update * silu_slope(cand_pre)).astype(jnp.bfloat16)
    grad_update_pre = (resid_own_grad * (cand - embedded_own) * update * (1.0 - update)).astype(
        jnp.bfloat16
    )
    direct_own = resid_own_grad * (1.0 - update)
    grad_w_cand = jnp.dot(ema_full.T, grad_cand_pre, preferred_element_type=jnp.float32)
    grad_w_update = jnp.dot(ema_full.T, grad_update_pre, preferred_element_type=jnp.float32)
    cand_full = lax.all_gather(grad_cand_pre, "ch", axis=1, tiled=True)
    grad_w_out = jnp.dot(gated.T, cand_full, preferred_element_type=jnp.float32)
    grad_gated = jnp.dot(cand_full, w_out.T, preferred_element_type=jnp.float32)
    grad_mixed = (grad_gated * reset).astype(jnp.bfloat16).reshape(blocks, C, -1)
    grad_reset_pre = (grad_gated * mixed * silu_slope(reset_pre)).astype(jnp.bfloat16)
    grad_w_reset = jnp.dot(ema_full.T, grad_reset_pre, preferred_element_type=jnp.float32)
    grad_values = jnp.einsum(
        "kqp,kqv->kpv", weights_low, grad_mixed, preferred_element_type=jnp.float32
    ).reshape(rows, -1)
    grad_value_pre = (grad_values * silu_slope(value_pre)).astype(jnp.bfloat16)
    grad_weights = lax.psum(
        jnp.einsum("kqv,kpv->kqp", grad_mixed, value_blocks, preferred_element_type=jnp.float32),
        "ch",
    )
    grad_scores_full = weights_soft * (
        grad_weights - jnp.sum(weights_soft * grad_weights, axis=-1, keepdims=True)
    )
    grad_position_bias = bias_gradient(jnp.sum(grad_scores_full, axis=0), C)
    grad_scores = grad_scores_full.astype(jnp.bfloat16)
    grad_query = (
        jnp.einsum("kqp,kpz->kqz", grad_scores, keys, preferred_element_type=jnp.float32) * factor
    ).reshape(rows, z_width)
    grad_keys = (
        jnp.einsum("kqp,kqz->kpz", grad_scores, query, preferred_element_type=jnp.float32) * factor
    ).reshape(rows, z_width)
    grad_z_scale = jnp.stack(
        [jnp.sum(z_act * grad_query, axis=0), jnp.sum(z_act * grad_keys, axis=0)]
    )
    grad_z_offset = jnp.stack([jnp.sum(grad_query, axis=0), jnp.sum(grad_keys, axis=0)])
    grad_z_pre = ((grad_query * z_scale[0] + grad_keys * z_scale[1]) * silu_slope(z_pre)).astype(
        jnp.bfloat16
    )
    grad_w_z = jnp.dot(ema_full.T, grad_z_pre, preferred_element_type=jnp.float32)
    gate_partial = (
        jnp.dot(grad_reset_pre, w_reset.T, preferred_element_type=jnp.float32)
        + jnp.dot(grad_update_pre, w_update.T, preferred_element_type=jnp.float32)
        + jnp.dot(grad_cand_pre, w_cand.T, preferred_element_type=jnp.float32)
    )
    own_z_rows = lax.dynamic_slice_in_dim(w_z, column, channels, 0)
    grad_ema_act = lax.psum_scatter(gate_partial, "ch", scatter_dimension=1, tiled=True) + jnp.dot(
        grad_z_pre, own_z_rows.T, preferred_element_type=jnp.float32
    )
    grad_ema_sum = grad_ema_act.reshape(batch, seg_len, channels) * silu_slope(ema_sum)
    rate_t = ema_rate.T
    counted = jnp.arange(1, seg_len + 1, dtype=jnp.float32)
    powers = jnp.exp(-rate_t[None] * counted[:, None, None])
    local_back = ema_eta.T * jnp.einsum(
        "btc,tjc->bjc", grad_ema_sum, powers, precision=lax.Precision.HIGHEST
    )
    arriving = prefix(
        (transfer, local_back), "seq", pair_chain, (jnp.ones_like(leaving), nothing), True
    )[1]
    grad_ema_in, grad_ema_rate, grad_ema_beta, grad_ema_eta, grad_ema_omega = ema_pull(
        (grad_ema_sum, arriving)
    )
    input_part = jnp.dot(grad_value_pre, w_value.T, preferred_element_type=jnp.float32)
    own_cols = lax.dynamic_slice_in_dim(input_part, column, channels, 1) + grad_ema_in.reshape(
        rows, channels
    )
    input_part = lax.dynamic_update_slice_in_dim(input_part, own_cols, column, 1)
    before_part, gain_part = norm_backward(input_part, gain_one, unit_one, inverse_one)
    own_before = lax.dynamic_slice_in_dim(before_part, column, channels, 1) + direct_own
    before_part = lax.dynamic_update_slice_in_dim(before_part, own_before, column, 1)
    grad_embedded, grad_gain_one = (
        lax.psum(before_part.astype(jnp.bfloat16), "ch").astype(jnp.float32),
        lax.psum(gain_part.astype(jnp.bfloat16), "ch").astype(jnp.float32),
    )
    input_grad = grad_embedded * present
    grad_embedding = jnp.dot(
        one_hot.astype(jnp.float32).T, input_grad, precision=lax.Precision.HIGHEST
    )
    grad_w_value = jnp.dot(normed_low.T, grad_value_pre, preferred_element_type=jnp.float32)
    summed = lax.psum(
        (
            grad_embedding,
            grad_gain_one,
            grad_ema_rate,
            grad_ema_beta,
            grad_ema_eta,
            grad_ema_omega,
            grad_w_value,
            grad_w_reset,
            grad_w_z,
            grad_z_scale,
            grad_z_offset,
            grad_position_bias,
            grad_w_update,
            grad_w_cand,
            grad_w_out,
            grad_gain_two,
            grad_w_up,
            grad_w_down,
        ),
        "seq",
    )
    return (
        output.reshape(batch, seg_len, width),
        input_grad.reshape(batch, seg_len, width),
        summed[0],
        summed[1],
        summed[2],
        summed[3],
        summed[4],
        summed[5],
        summed[6],
        summed[7],
        summed[8],
        summed[9],
        summed[10],
        summed[11],
        summed[12],
        summed[13],
        summed[14],
        summed[15],
        summed[16],
        summed[17],
    )


def solution(mesh):
    return jax.shard_map(
        local,
        mesh=mesh,
        in_specs=(
            P(None, "seq"),
            P(),
            P(),
            P(),
            P("ch", None),
            P("ch", None),
            P("ch", None),
            P("ch"),
            P(None, "ch"),
            P(None, "ch"),
            P(),
            P(),
            P(),
            P(),
            P(None, "ch"),
            P(None, "ch"),
            P("ch", None),
            P(),
            P(None, "ch"),
            P("ch", None),
            P(None, "seq", None),
        ),
        out_specs=(
            P(None, "seq", None),
            P(None, "seq", None),
            P(),
            P(),
            P("ch", None),
            P("ch", None),
            P("ch", None),
            P("ch"),
            P(None, "ch"),
            P(None, "ch"),
            P(),
            P(),
            P(),
            P(),
            P(None, "ch"),
            P(None, "ch"),
            P("ch", None),
            P(),
            P(None, "ch"),
            P("ch", None),
        ),
        check_vma=False,
    )
```

profile of v0, /device:TPU:0, one launch (start us, length us, event | category | flops | bytes accessed | tf_op | source)
XLA Modules:
  0.0 1708.7 jit_solution(18154287288477452802)
XLA Ops:
  36.6 215.9 %gather_fusion = f32[65536,128]{1,0:T(8,128)} fusion(f32[256,128]{1,0:T(8,128)S(1)} %copy.207, s32[65536]{0:T(1024)S(1)} %broadcast_clamp_fusion), kind=kCustom, calls=%fused_computation | custom fusion | bytes 67371008 | tf_op jit(solution)/shard_map/jvp()/gather | solution.py:61
  252.5 33.5 %copy.208 = f32[256,256,128]{1,0,2:T(8,128)} copy(f32[256,256,128]{2,1,0:T(8,128)} %bitcast.250) | data formatting | bytes 67108864 | tf_op jit(solution)/shard_map/jvp()/gather | solution.py:61
  285.9 33.8 %all-gather = f32[128,128]{1,0:T(8,128)} all-gather(f32[16,128]{1,0:T(8,128)S(1)} %get-tuple-element.408), channel_id=3, replica_groups=mesh['seq'=8,'ch'=4] {'seq'}, dimensions={0}, use_global_device_ids=true | all-gather | bytes 73728 | tf_op jit(solution)/shard_map/all_gather | solution.py:14
  319.8 35.2 %fusion.5 = f32[128,16,256]{2,1,0:T(8,128)} fusion(f32[16,256,128]{1,0,2:T(8,128)S(1)} %copy.209, f32[256,256,128]{1,0,2:T(8,128)} %copy.208, pred[256,256]{1,0:T(8,128)(4,1)S(1)} %subtract_compare_fusion), kind=kOutput, calls=%fused_computation.12 | convolution fusion | flops 1619001344 | bytes 37814272 | tf_op jit(solution)/shard_map/jvp(tsc,bsc->btc)/dot_general | solution.py:76
  355.1 7.6 copy.212
  363.6 7.2 while.28
  380.6 7.4 multiply_convert_fusion.3
  388.0 27.3 %all-gather.9.cloned.1.call-done = bf16[4096,512]{0,1:T(8,128)(2,1)} async-done(((bf16[4096,128]{0,1:T(8,128)(2,1)}), bf16[4096,512]{0,1:T(8,128)(2,1)}) %all-gather.9.cloned.1.call-update) | async-done | bytes 4194320 | tf_op jit(solution)/shard_map/all_gather | solution.py:156
  436.9 71.4 %reduce-scatter.3.cloned.1.call-done = f32[4096,128]{1,0:T(8,128)} async-done(((f32[4096,512]{1,0:T(8,128)}), f32[4096,128]{1,0:T(8,128)}) %reduce-scatter.3.cloned.1.call-update) | async-done | bytes 2097168 | tf_op jit(solution)/shard_map/reduce_scatter | solution.py:179
  523.8 53.6 %all-gather.11.cloned.1.call-done = f32[4096,512]{1,0:T(8,128)} async-done(((f32[4096,128]{1,0:T(8,128)}), f32[4096,512]{1,0:T(8,128)}) %all-gather.11.cloned.1.call-update) | async-done | bytes 8388624 | tf_op jit(solution)/shard_map/all_gather | solution.py:190
  597.7 153.0 %all-reduce.10.cloned.1.call-done = f32[4096,512]{1,0:T(8,128)} async-done(((f32[4096,512]{1,0:T(8,128)}), f32[4096,512]{1,0:T(8,128)}) %all-reduce.10.cloned.1.call-update) | async-done | bytes 8388624 | tf_op jit(solution)/shard_map/psum | solution.py:204
  750.7 7.8 multiply_reduce_fusion
  773.2 29.6 %all-gather.13.cloned.1.call-done = bf16[4096,512]{1,0:T(8,128)(2,1)} async-done(((bf16[4096,128]{1,0:T(8,128)(2,1)}), bf16[4096,512]{1,0:T(8,128)(2,1)}) %all-gather.13.cloned.1.call-update) | async-done | bytes 4194320 | tf_op jit(solution)/shard_map/all_gather | solution.py:215
  802.8 7.1 fusion.18
  816.1 8.3 add_add_fusion
  843.7 21.1 %all-reduce.12.cloned.1.call-done = f32[32,128,128]{1,2,0:T(8,128)} async-done(((f32[32,128,128]{1,2,0:T(8,128)}), f32[32,128,128]{1,2,0:T(8,128)}) %all-reduce.12.cloned.1.call-update) | async-done | bytes 2097168 | tf_op jit(solution)/shard_map/psum | solution.py:225
  885.3 54.0 %reduce-scatter.5.cloned.1.call-done = f32[4096,128]{1,0:T(8,128)} async-done(((f32[4096,512]{1,0:T(8,128)}), f32[4096,128]{1,0:T(8,128)}) %reduce-scatter.5.cloned.1.call-update) | async-done | bytes 2097168 | tf_op jit(solution)/shard_map/reduce_scatter | solution.py:254
  963.3 22.5 %fusion.3 = f32[128,16,256]{2,1,0:T(8,128)} fusion(f32[256,256,128]{1,0,2:T(8,128)} %copy.208, pred[256,256]{1,0:T(8,128)(4,1)S(1)} %copy-done.47, f32[16,256,128]{1,0,2:T(8,128)} %copy-done.10), kind=kOutput, calls=%fused_computation.10 | convolution fusion | flops 1619001344 | bytes 37814272 | tf_op jit(solution)/shard_map/transpose(jvp(tsc,bsc->btc))/dot_general | solution.py:76
  985.8 11.5 all-gather.17.cloned.1.call-done
  999.6 7.7 while.29
  1008.7 6.9 bitcast_add_fusion.3
  1022.4 7.6 multiply_reduce_fusion.1
  1039.8 6.2 fusion.61
  1068.6 31.3 %select_bitcast_fusion = f32[256,256,128]{1,0,2:T(8,128)} fusion(pred[256,256]{1,0:T(8,128)(4,1)S(1)} %copy-done.47, f32[16,256,128]{1,0,2:T(8,128)S(1)} %copy-done.9, f32[16,256,128]{1,0,2:T(8,128)S(1)} %copy-done.11), kind=kOutput, calls=%fused_computation.9 | convolution fusion | flops 1619001344 | bytes 37814272 | tf_op jit(solution)/shard_map/transpose(jvp(tsc,bsc->btc))/dot_general | solution.py:76
  1099.9 34.2 %copy.250 = f32[256,256,128]{2,1,0:T(8,128)} copy(f32[256,256,128]{1,0,2:T(8,128)} %select_bitcast_fusion) | data formatting | bytes 67108864 | tf_op jit(solution)/shard_map/transpose(jvp(jit(_where)))/select_n | solution.py:61
  1134.1 396.5 %scatter_custom_fusion = f32[256,128]{1,0:T(8,128)S(1)} fusion(s32[65536]{0:T(1024)} %bitcast.274, f32[65536,128]{1,0:T(8,128)} %bitcast.253, f32[]{:T(128)} %constant.93.clone.1), kind=kCustom, calls=%fused_computation.160 | custom fusion | flops 8388608 | bytes 131584 | tf_op jit(solution)/shard_map/transpose(jvp())/scatter-add | solution.py:61
  1531.4 8.7 fusion.20
  1554.3 6.2 multiply_reduce_fusion.9
  1564.2 6.2 psum.166
  1570.5 37.4 %all-reduce.2 = (f32[512]{0:T(512)}, f32[128,16]{0,1:T(8,128)}, f32[128,16]{0,1:T(8,128)}, f32[128,16]{0,1:T(8,128)}, f32[128]{0:T(128)}, /*index=5*/f32[2,128]{...) all-reduce(bf16[512]{0:T(512)(128)(2,1)S(1)} %psum.166, ...), channel_id=1, replica_groups=mesh['seq'=8,'ch'=4] {'seq'}, use_global_device_ids=true, to_apply=%region_21.22 | all-reduce | flops 8063 | bytes 63480 | tf_op jit(solution)/shard_map/psum | solution.py:287
  1613.4 8.2 convert_add_fusion
  1621.6 70.8 %all-reduce.14.cloned.1.call-done = (f32[256,512]{1,0:T(8,128)}, f32[512,256]{1,0:T(8,128)}, f32[512,256]{1,0:T(8,128)}, f32[512,128]{1,0:T(8,128)}, f32[512,128...) async-done(((f32[256,512]{1,0:T(8,128)}, f32[512,256]{1,0:T(8,128)}, f32[512,256]{1,0:T(8,128)}, ...) | async-done | bytes 3932176 | tf_op jit(solution)/shard_map/psum | solution.py:287
  (389 shorter events, 271.9 us)
Async XLA Ops:
  7.2 424.7 %copy-start = (bf16[256,512]{1,0:T(8,128)(2,1)S(1)}, bf16[256,512]{1,0:T(8,128)(2,1)}, u32[]{:S(2)}) copy-start(bf16[256,512]{1,0:T(8,128)(2,1)} %param.41) | copy-start | bytes 786436
  7.2 347.9 %all-gather.15.cloned.1.call-start = ((), (), s32[]{:S(2)}) async-start(), calls=%async_computation.9 | async-start | bytes 9437184 | tf_op jit(solution)/shard_map/all_gather | solution.py:14
  10.6 17.9 %copy-start.49 = (f32[16,128]{0,1:T(8,128)}, f32[16,128]{0,1:T(8,128)S(1)}, u32[]{:S(2)}) copy-start(f32[16,128]{0,1:T(8,128)S(1)} %copy.210) | copy-start | bytes 24580
  28.5 343.8 %copy-start.8 = (f32[16,256,128]{1,0,2:T(8,128)}, f32[16,256,128]{1,0,2:T(8,128)S(1)}, u32[]{:S(2)}) copy-start(f32[16,256,128]{1,0,2:T(8,128)S(1)} %copy.209) | copy-start | bytes 6291460
  34.0 381.2 %all-gather.9.cloned.1.call-start = ((), (), s32[]{:S(2)}) async-start(), calls=%async_computation.2 | async-start | bytes 5242880 | tf_op jit(solution)/shard_map/all_gather | solution.py:156
  319.8 35.3 %copy-start.46 = (pred[256,256]{1,0:T(8,128)(4,1)}, pred[256,256]{1,0:T(8,128)(4,1)S(1)}, u32[]{:S(2)}) copy-start(pred[256,256]{1,0:T(8,128)(4,1)S(1)} %subtract_compare_fusion) | copy-start | bytes 196612
  355.1 8.5 copy-start.34
  363.6 8.6 copy-start.103
  379.7 128.6 %reduce-scatter.3.cloned.1.call-start = ((), (), s32[]{:S(2)}) async-start(), calls=%async_computation.3 | async-start | bytes 10485760 | tf_op jit(solution)/shard_map/reduce_scatter | solution.py:179
  380.6 34.7 %copy-start.96 = (f32[128]{0:T(128)}, f32[128]{0:T(128)S(1)}, u32[]{:S(2)}) copy-start(f32[128]{0:T(128)S(1)} %get-tuple-element.431) | copy-start | bytes 1540
  380.6 34.7 %copy-start.98 = (f32[128]{0:T(128)}, f32[128]{0:T(128)S(1)}, u32[]{:S(2)}) copy-start(f32[128]{0:T(128)S(1)} %get-tuple-element.432) | copy-start | bytes 1540
  380.6 34.7 %copy-start.94 = (bf16[512,128]{1,0:T(8,128)(2,1)S(1)}, bf16[512,128]{1,0:T(8,128)(2,1)}, u32[]{:S(2)}) copy-start(bf16[512,128]{1,0:T(8,128)(2,1)} %param.35) | copy-start | bytes 393220
  436.4 71.9 %copy-start.58 = (bf16[512,128]{1,0:T(8,128)(2,1)S(1)}, bf16[512,128]{1,0:T(8,128)(2,1)}, u32[]{:S(2)}) copy-start(bf16[512,128]{1,0:T(8,128)(2,1)} %param.40) | copy-start | bytes 393220
  436.4 76.2 %copy-start.79 = (bf16[512,128]{1,0:T(8,128)(2,1)S(1)}, bf16[512,128]{1,0:T(8,128)(2,1)}, u32[]{:S(2)}) copy-start(bf16[512,128]{1,0:T(8,128)(2,1)} %param.39) | copy-start | bytes 393220
  436.5 140.9 %all-gather.11.cloned.1.call-start = ((), (), s32[]{:S(2)}) async-start(), calls=%async_computation.4 | async-start | bytes 10485760 | tf_op jit(solution)/shard_map/all_gather | solution.py:190
  517.8 232.9 %all-reduce.10.cloned.1.call-start = ((), (), s32[]{:S(2)}) async-start(), calls=%async_computation.5 | async-start | bytes 16777216 | tf_op jit(solution)/shard_map/psum | solution.py:204
  597.7 205.1 %all-gather.13.cloned.1.call-start = ((), (), s32[]{:S(2)}) async-start(), calls=%async_computation.6 | async-start | bytes 5242880 | tf_op jit(solution)/shard_map/all_gather | solution.py:215
  767.4 97.4 %all-reduce.12.cloned.1.call-start = ((), (), s32[]{:S(2)}) async-start(), calls=%async_computation.8 | async-start | bytes 4194304 | tf_op jit(solution)/shard_map/psum | solution.py:225
  813.3 125.9 %reduce-scatter.5.cloned.1.call-start = ((), (), s32[]{:S(2)}) async-start(), calls=%async_computation.7 | async-start | bytes 10485760 | tf_op jit(solution)/shard_map/reduce_scatter | solution.py:254
  824.5 172.9 %all-gather.17.cloned.1.call-start = ((), (), s32[]{:S(2)}) async-start(), calls=%async_computation.10 | async-start | bytes 1179648 | tf_op jit(solution)/shard_map/all_gather | solution.py:14
  885.3 57.4 %copy-start.26 = (bf16[4096,128]{1,0:T(8,128)(2,1)}, bf16[4096,128]{1,0:T(8,128)(2,1)S(1)}, u32[]{:S(2)}) copy-start(bf16[4096,128]{1,0:T(8,128)(2,1)S(1)} %get-tuple-element.395) | copy-start | bytes 3145732
  957.0 574.4 %all-reduce.16.cloned.1.call-start = ((), (), s32[]{:S(2)}) async-start(), calls=%async_computation.12 | async-start | bytes 16777216 | tf_op jit(solution)/shard_map/psum | solution.py:195
  999.6 9.1 copy-start.50
  999.6 9.1 copy-start.104
  1039.5 652.9 %all-reduce.14.cloned.1.call-start = ((), (), s32[]{:S(2)}) async-start(), calls=%async_computation.11 | async-start | bytes 7864320 | tf_op jit(solution)/shard_map/psum | solution.py:287
  1055.3 9.0 copy-start.27
  1099.9 431.5 %copy-start.78 = (f32[2,2,8,128]{3,1,2,0:T(2,128)S(1)}, f32[2,2,8,128]{3,1,2,0:T(2,128)}, u32[]{:S(2)}) copy-start(f32[2,2,8,128]{3,1,2,0:T(2,128)} %copy-done.76) | copy-start | bytes 49156
  1099.9 431.5 %copy-start.93 = (s32[2,2,8,128]{3,1,2,0:T(2,128)S(1)}, s32[2,2,8,128]{3,1,2,0:T(2,128)}, u32[]{:S(2)}) copy-start(s32[2,2,8,128]{3,1,2,0:T(2,128)} %copy-done.92) | copy-start | bytes 49156
  1554.3 16.1 copy-start.83
  1554.3 16.1 copy-start.85
  1554.3 16.1 copy-start.88
  1554.3 16.1 copy-start.89
  (93 other events, 357.4 us)
Sparse Core Ops, SparseCore 0:
  34.1 128.0 all-gather.14
  379.8 35.3 all-gather.8
  436.6 71.7 reduce-scatter.2
  517.9 59.4 all-gather.10
  597.8 152.8 all-reduce.9
  767.6 35.1 all-gather.12
  813.4 51.3 all-reduce.11
  867.4 71.7 reduce-scatter.4
  957.1 40.1 all-gather.16
  1039.6 152.1 all-reduce.15
  1540.3 152.0 all-reduce.13
where the time goes:
time: 1720 us; the launch traced here: 1710 us
  other arithmetic  497 us (29%)
  waiting for transfers between devices  492 us (29%)
  local copies, waits for them, and re-layouts  375 us (22%)
  matrix products  250 us (15%)
  blocking collectives  77.5 us (5%)
    scatter-add x1, other arithmetic, ema_tables(): kernel[jnp.maximum(lag_idx, 0)]  397 us
    gather x2, local copies, waits for them, and re-layouts, ema_tables(): kernel[jnp.maximum(lag_idx, 0)]  249 us
    psum x1, waiting for transfers between devices, local(): lax.psum(jnp.dot(grad_up, w_up.T, preferred_element_type=jnp.float32), 'ch')  153 us
    dot_general x3, matrix products, whole_ema(): jnp.einsum('tsc,bsc->btc', toeplitz, inputs, precision=lax.Precision.HIGH...  89 us
    reduce_scatter x1, waiting for transfers between devices, local(): lax.psum_scatter(jnp.dot(gated, w_out, preferred_element_type=jnp.float32...  71.4 us
    psum x1, waiting for transfers between devices, local(): lax.psum((grad_embedding, grad_gain_one, grad_ema_rate, grad_ema_beta, gr...  70.8 us
    reduce_scatter x1, waiting for transfers between devices, local(): lax.psum_scatter(gate_partial, 'ch', scatter_dimension=1, tiled=True)  54 us
    all_gather x1, waiting for transfers between devices, local(): resid = lax.all_gather(resid_own, 'ch', axis=1, tiled=True)  53.6 us
  transfers between devices with their start and end apart: 11, of which 9 were waited for; matrix products, arithmetic and copies ran while one was open for 53% of the time, Pallas kernels for 0%

commit v1 on v0

v1 whole, which is shorter than its diff:
```python
import functools

import jax
import jax.numpy as jnp
from jax import lax
from jax.experimental import pallas as pl
from jax.experimental.pallas import tpu as pltpu
from jax.sharding import PartitionSpec as P

C = 128
BLK = 256
LANES = 8
STEP = BLK // LANES
EPS = 1e-05
BF = jnp.bfloat16
F32 = jnp.float32
VMEM = 60 * 1024 * 1024


def cost(us):
    return pl.CostEstimate(flops=us * 10**9, bytes_accessed=10**5, transcendentals=0)


def sig(v):
    return 0.5 * jnp.tanh(0.5 * v) + 0.5


def mm(a, b):
    return jnp.dot(a, b, preferred_element_type=F32)


def mm_nt(a, b):
    return lax.dot_general(a, b, (((1,), (1,)), ((), ())), preferred_element_type=F32)


def mm_tn(a, b):
    return lax.dot_general(a, b, (((0,), (0,)), ((), ())), preferred_element_type=F32)


def slope(v, s):
    return s * (1.0 + v * (1.0 - s))


def wide(row):
    return jnp.broadcast_to(row, (LANES, 128))


def lane_iota():
    return lax.broadcasted_iota(jnp.int32, (LANES, 128), 0)


def shift_down(v, k, row):
    return jnp.where(row >= k, pltpu.roll(v, k, axis=0), 0.0)


def shift_up(v, k, row):
    return jnp.where(row < LANES - k, pltpu.roll(v, LANES - k, axis=0), 0.0)


def chain(values, rates, row, shift):
    for k in (1, 2, 4):
        values = [
            v + jnp.exp(r * (-float(STEP * k))) * shift(v, k, row) for v, r in zip(values, rates)
        ]
    return values


def at(t):
    return pl.ds(pl.multiple_of(t * LANES, LANES), LANES)


def one_hot_t(ids, vocab):
    hit = lax.broadcasted_iota(jnp.int32, (vocab, BLK), 0) == ids
    return jnp.where(hit, 1.0, 0.0).astype(BF)


def one_less_exp(rate):
    near = rate * (1.0 - rate * (0.5 - rate * (1.0 / 6.0 - rate * (1.0 / 24.0))))
    return jnp.where(rate < 0.02, near, 1.0 - jnp.exp(-rate))


def prep_kernel(rate_ref, beta_ref, eta_ref, omega_ref, out_ref):
    dims = rate_ref.shape[0]
    rate, beta, eta = rate_ref[...], beta_ref[...], eta_ref[...]
    decay, rise = jnp.exp(-rate), one_less_exp(rate)
    for k, v in enumerate((rate, eta * rise * beta, rise * beta, eta * rise, -decay * eta * beta)):
        out_ref[k * dims : (k + 1) * dims, :] = v
    out_ref[5 * dims :, :] = jnp.broadcast_to(omega_ref[...], (8, omega_ref.shape[1]))


def split3(v):
    parts = []
    for _ in range(3):
        parts.append(v.astype(BF))
        v = v - parts[-1].astype(F32)
    return parts


def skew(v, sign):
    row = lax.broadcasted_iota(jnp.int32, v.shape, 0)
    for b in range(7):
        k = 1 << b
        v = jnp.where((row & k) != 0, pltpu.roll(v, k if sign > 0 else 256 - k, axis=1), v)
    return v


def table_kernel(bias_ref, out_ref):
    v = jnp.broadcast_to(bias_ref[...], (C, 256))
    v = skew(pltpu.roll(v, 256 - (C - 1), axis=1), 1)[:, :C]
    off = jnp.zeros((C, C), F32)
    v = jnp.concatenate(
        [jnp.concatenate([v, off], axis=1), jnp.concatenate([off, v], axis=1)], axis=0
    )
    perm = to_natural(None)
    v = sum(mm_tn(perm, p) for p in split3(v))
    v = sum(mm(p, perm) for p in split3(v))
    r = lax.broadcasted_iota(jnp.int32, (BLK, BLK), 0)
    c = lax.broadcasted_iota(jnp.int32, (BLK, BLK), 1)
    query = (r & (LANES - 1)) * STEP + (r >> 3)
    key = (c & (LANES - 1)) * STEP + (c >> 3)
    seen = jnp.logical_and(key <= query, key >= (query & C))
    out_ref[...] = jnp.where(seen, v, -1e30)


def embed_kernel(ids_ref, tab_ref, gain_ref, x_ref, emb_ref):
    emb = mm_tn(one_hot_t(ids_ref[0], tab_ref.shape[0]), tab_ref[...])
    inv = lax.rsqrt(jnp.mean(emb * emb, axis=-1, keepdims=True) + EPS)
    x_ref[0] = emb * inv * gain_ref[...]
    emb_ref[0] = emb.astype(BF)


def enter_kernel(x_ref, par_ref, ex_ref, lv_ref):
    dims, width = lv_ref.shape[1:]

    row = lane_iota()
    for c0 in range(0, width, 128):
        sl = pl.ds(c0, 128)
        rates = [wide(par_ref[pl.ds(j, 1), sl]) for j in range(dims)]
        decay = [jnp.exp(-r) for r in rates]

        def body(t, s):
            xt = x_ref[0, at(t), sl]
            return tuple(d * v + xt for d, v in zip(decay, s))

        s = lax.fori_loop(
            0, STEP, body, tuple(jnp.zeros((LANES, 128), F32) for _ in range(dims)), unroll=8
        )
        s = chain(list(s), rates, row, shift_down)
        for j in range(dims):
            ex_ref[0, j, :, sl] = shift_down(s[j], 1, row)
            lv_ref[0, pl.ds(j, 1), sl] = s[j][LANES - 1 :, :]


def run_kernel(x_ref, ex_ref, se_ref, par_ref, out_ref):
    dims, width = se_ref.shape[1:]
    place = lane_iota().astype(F32)
    for c0 in range(0, width, 128):
        sl = pl.ds(c0, 128)
        rates = [wide(par_ref[pl.ds(j, 1), sl]) for j in range(dims)]
        decay = [jnp.exp(-r) for r in rates]
        ws = [wide(par_ref[pl.ds(dims + j, 1), sl]) for j in range(dims)]
        omega = wide(par_ref[pl.ds(5 * dims, 1), sl])
        start = tuple(
            ex_ref[0, j, :, sl]
            + jnp.exp(rates[j] * place * (-float(STEP))) * wide(se_ref[0, pl.ds(j, 1), sl])
            for j in range(dims)
        )

        def body(t, s):
            xt = x_ref[0, at(t), sl]
            s = tuple(d * v + xt for d, v in zip(decay, s))
            parts = [w * v for w, v in zip(ws, s)]
            while len(parts) > 1:
                parts = [a + b for a, b in zip(parts[::2], parts[1::2])]
            out_ref[0, at(t), sl] = parts[0] + omega * xt
            return s

        lax.fori_loop(0, STEP, body, start, unroll=4)


def to_natural(mask_row):
    q = lax.broadcasted_iota(jnp.int32, (BLK, BLK), 0)
    r = lax.broadcasted_iota(jnp.int32, (BLK, BLK), 1)
    hit = q == (r & (LANES - 1)) * STEP + (r >> 3)
    if mask_row is not None:
        hit = jnp.logical_and(hit, mask_row >= 0)
    return jnp.where(hit, 1.0, 0.0).astype(BF)


def from_natural(mask_row):
    r = lax.broadcasted_iota(jnp.int32, (BLK, BLK), 0)
    q = lax.broadcasted_iota(jnp.int32, (BLK, BLK), 1)
    hit = q == (r & (LANES - 1)) * STEP + (r >> 3)
    if mask_row is not None:
        hit = jnp.logical_and(hit, mask_row >= 0)
    return jnp.where(hit, 1.0, 0.0).astype(BF)


def fill(refs, rows, to_ref):
    for r, ref in enumerate(refs):
        to_ref[:, pl.ds(r * 256, 256)] = ref[rows : rows + 512, :]


def fill_rows(refs, rows, to_ref):
    for r, ref in enumerate(refs):
        to_ref[pl.ds(r * 256, 256), 0:256] = ref[rows : rows + 256, :]
        to_ref[pl.ds(r * 256, 256), 256:512] = ref[rows + 256 : rows + 512, :]


def fill_gates(me, refs, wu_ref, wc_ref):
    for r, ref in enumerate(refs):
        own = pl.ds(pl.multiple_of((me ^ r) * 128, 128), 128)
        wu_ref[:, own] = ref[0:512, 0:128]
        wc_ref[:, own] = ref[0:512, 128:256]


def slots(keep_ref, send_ref):
    return ((keep_ref, 0), (send_ref, 0), (keep_ref, 1), (send_ref, 1))


def softmax_rows(query, keys, bias, factor):
    scores = mm_nt(query, keys) * factor + bias
    shifted = jnp.exp(scores - jnp.max(scores, axis=-1, keepdims=True))
    return shifted / jnp.sum(shifted, axis=-1, keepdims=True)


def forward_kernel(me_ref, es_ref, x_ref, emb_ref, bias_ref, wz_ref, zs_ref, zo_ref, *rest):
    packs, rest = rest[:8], rest[8:]
    (vp_ref, rp_ref, mix_ref, zp_ref, up_ref, cp_ref, res_ref) = rest[:7]
    (wv_ref, wr_ref, wu_ref, wc_ref, wo_ref) = rest[7:]

    @pl.when(pl.program_id(0) == 0)
    def _():
        fill(packs[0:4], 0, wv_ref)
        fill(packs[0:4], 512, wr_ref)
        fill_gates(me_ref[0], packs[4:8], wu_ref, wc_ref)
        fill_rows(packs[4:8], 512, wo_ref)

    es = es_ref[0]
    e = (es * sig(es)).astype(BF)
    zp = mm(e, wz_ref[...])
    zp_ref[0] = zp
    za = zp * sig(zp)
    query = (za * zs_ref[0:1, :] + zo_ref[0:1, :]).astype(BF)
    keys = (za * zs_ref[1:2, :] + zo_ref[1:2, :]).astype(BF)
    weights = softmax_rows(query, keys, bias_ref[...], zp.shape[-1] ** -0.5).astype(BF)
    vp = mm(x_ref[0].astype(BF), wv_ref[...])
    vp_ref[0] = vp.astype(BF)
    values = (vp * sig(vp)).astype(BF)
    mixed = mm(weights, values)
    mix_ref[0] = mixed.astype(BF)
    rp = mm(e, wr_ref[...])
    rp_ref[0] = rp.astype(BF)
    gated = (rp * sig(rp) * mixed).astype(BF)
    up = mm(e, wu_ref[...])
    up_ref[0] = up.astype(BF)
    cp = mm(e, wc_ref[...]) + mm(gated, wo_ref[...])
    cp_ref[0] = cp.astype(BF)
    emb = emb_ref[0].astype(F32)
    res_ref[0] = emb + sig(up) * (cp * sig(cp) - emb)


def ff_kernel(me_ref, nat_ref, cot_ref, res_ref, gain_ref, *rest):
    packs, rest = rest[:4], rest[4:]
    out_ref, gr_ref, keep_ref, send_ref, gg_ref, w_up_ref, w_down_ref, au_ref, ad_ref = rest
    step = pl.program_id(0)

    @pl.when(step == 0)
    def _():
        fill(packs, 0, w_up_ref)
        fill_rows(packs, 512, w_down_ref)
        au_ref[...] = jnp.zeros_like(au_ref)
        ad_ref[...] = jnp.zeros_like(ad_ref)
        gg_ref[...] = jnp.zeros_like(gg_ref)

    resid = res_ref[0]
    inv = lax.rsqrt(jnp.mean(resid * resid, axis=-1, keepdims=True) + EPS)
    unit = resid * inv
    gain = gain_ref[...]
    ff_in = (unit * gain).astype(BF)
    hp = mm(ff_in, w_up_ref[...])
    s = sig(hp)
    hidden = (hp * s).astype(BF)
    out = resid + mm(hidden, w_down_ref[...])
    out_ref[0] = mm(to_natural(None), out.astype(BF)).astype(BF)
    grad_out = mm(from_natural(nat_ref[0]), cot_ref[0])
    grad_low = grad_out.astype(BF)
    ad_ref[...] += mm_tn(hidden, grad_low)
    grad_up = (mm_nt(grad_low, w_down_ref[...]) * slope(hp, s)).astype(BF)
    au_ref[...] += mm_tn(ff_in, grad_up)
    grad_norm = mm_nt(grad_up, w_up_ref[...])
    gain_part = jnp.sum(grad_norm * unit, axis=0, keepdims=True)
    for k in range(4):
        gg_ref[k : k + 1, :] += gain_part[:, k * 128 : (k + 1) * 128]
    scaled = grad_norm * gain
    gr_ref[0] = grad_out + inv * (
        scaled - unit * jnp.mean(scaled * unit, axis=-1, keepdims=True)
    )

    @pl.when(step == pl.num_programs(0) - 1)
    def _():
        for r, (ref, slot) in enumerate(slots(keep_ref, send_ref)):
            ref[slot, 0:512, :] = au_ref[:, r * 256 : r * 256 + 256].astype(BF)
            ref[slot, 512:768, :] = ad_ref[r * 256 : r * 256 + 256, 0:256].astype(BF)
            ref[slot, 768:1024, :] = ad_ref[r * 256 : r * 256 + 256, 256:512].astype(BF)


def gates_back_kernel(me_ref, es_ref, emb_ref, rp_ref, mix_ref, up_ref, cp_ref, gr_ref, *rest):
    packs, rest = rest[:8], rest[8:]
    (gm_ref, ge_ref, dir_ref, keep_ref, send_ref) = rest[:5]
    (wr_ref, wu_ref, wc_ref, wo_ref, ar_ref, au_ref, ac_ref, ao_ref) = rest[5:]
    me = me_ref[0]
    step = pl.program_id(0)

    @pl.when(step == 0)
    def _():
        fill(packs[0:4], 0, wr_ref)
        fill_gates(me, packs[4:8], wu_ref, wc_ref)
        fill_rows(packs[4:8], 512, wo_ref)
        for ref in (ar_ref, au_ref, ac_ref, ao_ref):
            ref[...] = jnp.zeros_like(ref)

    es = es_ref[0]
    e_t = (es * sig(es)).astype(BF).T
    emb = emb_ref[0].astype(F32)
    grad_resid = gr_ref[0]
    up = sig(up_ref[0].astype(F32))
    cp = cp_ref[0].astype(F32)
    cs = sig(cp)
    gcp = (grad_resid * up * slope(cp, cs)).astype(BF)
    gup = (grad_resid * (cp * cs - emb) * up * (1.0 - up)).astype(BF)
    dir_ref[0] = (grad_resid * (1.0 - up)).astype(BF)
    ac_ref[...] += mm(e_t, gcp)
    au_ref[...] += mm(e_t, gup)
    rp = rp_ref[0].astype(F32)
    rs = sig(rp)
    reset = rp * rs
    mixed = mix_ref[0].astype(F32)
    ao_ref[...] += mm_tn((reset * mixed).astype(BF), gcp)
    grad_gated = mm_nt(gcp, wo_ref[...])
    gm_ref[0] = (grad_gated * reset).astype(BF)
    grp = (grad_gated * mixed * slope(rp, rs)).astype(BF)
    ar_ref[...] += mm(e_t, grp)
    ge_ref[0] = mm_nt(grp, wr_ref[...]) + mm_nt(gup, wu_ref[...]) + mm_nt(gcp, wc_ref[...])

    @pl.when(step == pl.num_programs(0) - 1)
    def _():
        for r, (ref, slot) in enumerate(slots(keep_ref, send_ref)):
            units = pl.ds(r * 256, 256)
            own = pl.ds(pl.multiple_of((me ^ r) * 128, 128), 128)
            ref[slot, 0:512, :] = ar_ref[:, units].astype(BF)
            ref[slot, 512:1024, 0:128] = au_ref[:, own].astype(BF)
            ref[slot, 512:1024, 128:256] = ac_ref[:, own].astype(BF)
            ref[slot, 1024:1280, :] = ao_ref[units, 0:256].astype(BF)
            ref[slot, 1280:1536, :] = ao_ref[units, 256:512].astype(BF)


def mix_back_kernel(
    es_ref, x_ref, vp_ref, zp_ref, gm_ref, ge_ref,
    bias_ref, wz_ref, zs_ref, zo_ref, par_ref, gg_ref, *rest,
):
    packs, rest = rest[:4], rest[4:]
    (g_ref, gnv_ref, ae_ref, lb_ref, keep_ref, send_ref) = rest[:6]
    (wv_ref, av_ref, az_ref, gz_ref, gb_ref) = rest[6:]
    step = pl.program_id(0)

    @pl.when(step == 0)
    def _():
        fill(packs, 0, wv_ref)
        for ref in (av_ref, az_ref, gz_ref, gb_ref):
            ref[...] = jnp.zeros_like(ref)

    es = es_ref[0]
    es_sig = sig(es)
    e_t = (es * es_sig).astype(BF).T
    gm = gm_ref[0]
    zp = zp_ref[0]
    zsig = sig(zp)
    za = zp * zsig
    factor = zp.shape[-1] ** -0.5
    s0, s1 = zs_ref[0:1, :], zs_ref[1:2, :]
    query = (za * s0 + zo_ref[0:1, :]).astype(BF)
    keys = (za * s1 + zo_ref[1:2, :]).astype(BF)
    weights = softmax_rows(query, keys, bias_ref[...], factor)
    vp = vp_ref[0].astype(F32)
    vs = sig(vp)
    values = (vp * vs).astype(BF)
    gvp = (mm_tn(weights.astype(BF), gm) * slope(vp, vs)).astype(BF)
    gnv_ref[0] = mm_nt(gvp, wv_ref[...]).astype(BF)
    av_ref[...] += mm_tn(x_ref[0].astype(BF), gvp)
    gw = mm_nt(gm, values)
    gsf = weights * (gw - jnp.sum(weights * gw, axis=-1, keepdims=True))
    gb_ref[...] += gsf
    gs = gsf.astype(BF)
    gq = mm(gs, keys) * factor
    gk = mm_tn(gs, query) * factor
    gz_ref[0:1, :] += jnp.sum(za * gq, axis=0, keepdims=True)
    gz_ref[1:2, :] += jnp.sum(za * gk, axis=0, keepdims=True)
    gz_ref[2:3, :] += jnp.sum(gq, axis=0, keepdims=True)
    gz_ref[3:4, :] += jnp.sum(gk, axis=0, keepdims=True)
    gzp = ((gq * s0 + gk * s1) * slope(zp, zsig)).astype(BF)
    az_ref[...] += mm(e_t, gzp)
    g_ref[0] = (ge_ref[0] + mm_nt(gzp, wz_ref[...])) * slope(es, es_sig)

    dims, width = lb_ref.shape[1:]
    row = lane_iota()
    for c0 in range(0, width, 128):
        sl = pl.ds(c0, 128)
        rates = [wide(par_ref[pl.ds(j, 1), sl]) for j in range(dims)]
        decay = [jnp.exp(-r) for r in rates]

        def body(t, a):
            gt = g_ref[0, at(STEP - 1 - t), sl]
            return tuple(d * v + gt for d, v in zip(decay, a))

        a = lax.fori_loop(
            0, STEP, body, tuple(jnp.zeros((LANES, 128), F32) for _ in range(dims)), unroll=8
        )
        a = chain(list(a), rates, row, shift_up)
        for j in range(dims):
            ae_ref[0, j, :, sl] = shift_up(a[j], 1, row)
            lb_ref[0, pl.ds(j, 1), sl] = a[j][0:1, :]

    @pl.when(step == pl.num_programs(0) - 1)
    def _():
        perm = to_natural(None)
        v = sum(mm(perm, p) for p in split3(gb_ref[...]))
        v = sum(mm_nt(p, perm) for p in split3(v))
        v = v[:C, :C] + v[C:, C:]
        v = jnp.concatenate([v, jnp.zeros((C, C), F32)], axis=1)
        bias = jnp.sum(pltpu.roll(skew(v, -1), C - 1, axis=1), axis=0, keepdims=True)
        zero = jnp.zeros((6, 128), F32)
        small = jnp.concatenate(
            [gz_ref[0:4, :], bias[:, :128], bias[:, 128:], gg_ref[...], zero], axis=0
        )
        for r, (ref, slot) in enumerate(slots(keep_ref, send_ref)):
            ref[slot, 0:512, :] = av_ref[:, r * 256 : r * 256 + 256].astype(BF)
            ref[slot, 512:768, 0:128] = az_ref[0:256, :].astype(BF)
            ref[slot, 512:768, 128:256] = az_ref[256:512, :].astype(BF)
            ref[slot, 768:896, :] = jnp.zeros((128, 256), BF)
            ref[slot, 768:784, 0:128] = small.astype(BF)


def leave_kernel(
    me_ref, ids_ref, emb_ref, x_ref, g_ref, ae_ref, ar_ref, ex_ref, se_ref, dir_ref, gnv_ref,
    par_ref, gain_ref, ig_ref, keep_ref, send_ref,
    gn_ref, m_ref, n_ref, ge_ref, go_ref, gg_ref, sum_ref,
):
    step = pl.program_id(0)
    dims, width = se_ref.shape[1:]

    @pl.when(step == 0)
    def _():
        for ref in (ge_ref, go_ref, gg_ref, m_ref, n_ref):
            ref[...] = jnp.zeros_like(ref)

    place = lane_iota().astype(F32)
    half = 8
    for c0 in range(0, width, 128):
        sl = pl.ds(c0, 128)
        omega = wide(par_ref[pl.ds(5 * dims, 1), sl])
        for j0 in range(0, dims, half):
            js = range(j0, j0 + half)
            rates = [wide(par_ref[pl.ds(j, 1), sl]) for j in js]
            decay = [jnp.exp(-r) for r in rates]
            ws = [wide(par_ref[pl.ds(dims + j, 1), sl]) for j in js]
            a_end = [
                ae_ref[0, j, :, sl]
                + jnp.exp(r * (LANES - 1.0 - place) * (-float(STEP)))
                * wide(ar_ref[0, pl.ds(j, 1), sl])
                for j, r in zip(js, rates)
            ]

            def emit(t, a, gt):
                parts = [w * v for w, v in zip(ws, a)]
                while len(parts) > 1:
                    parts = [p + q for p, q in zip(parts[::2], parts[1::2])]
                if j0 == 0:
                    gn_ref[at(t), sl] = parts[0] + omega * gt
                else:
                    gn_ref[at(t), sl] += parts[0]

            gt = g_ref[0, at(STEP - 1), sl]
            xt = x_ref[0, at(STEP - 1), sl]
            a = tuple(gt + d * v for d, v in zip(decay, a_end))
            emit(STEP - 1, a, gt)
            m = tuple(xt * v for v in a)
            zero = tuple(jnp.zeros((LANES, 128), F32) for _ in js)

            def body(i, carry):
                a, b, m, n = carry
                t = STEP - 2 - i
                gt = g_ref[0, at(t), sl]
                xt = x_ref[0, at(t), sl]
                b = tuple(u + d * v for d, u, v in zip(decay, a, b))
                a = tuple(gt + d * v for d, v in zip(decay, a))
                emit(t, a, gt)
                m = tuple(u + xt * v for u, v in zip(m, a))
                n = tuple(u + xt * v for u, v in zip(n, b))
                return a, b, m, n

            a, b, m, n = lax.fori_loop(0, STEP - 1, body, (a, zero, m, zero))
            for k, j in enumerate(js):
                start = ex_ref[0, j, :, sl] + jnp.exp(rates[k] * place * (-float(STEP))) * wide(
                    se_ref[0, pl.ds(j, 1), sl]
                )
                m_ref[j, :, sl] += m[k]
                n_ref[j, :, sl] += n[k] + start * (a[k] + decay[k] * b[k])

    go_ref[...] += jnp.sum(g_ref[0] * x_ref[0], axis=0, keepdims=True)
    emb = emb_ref[0].astype(F32)
    inv = lax.rsqrt(jnp.mean(emb * emb, axis=-1, keepdims=True) + EPS)
    unit = emb * inv
    gn = gn_ref[...] + gnv_ref[0].astype(F32)
    gg_ref[...] += jnp.sum(gn * unit, axis=0, keepdims=True)
    scaled = gn * gain_ref[...]
    ig = dir_ref[0].astype(F32) + inv * (
        scaled - unit * jnp.mean(scaled * unit, axis=-1, keepdims=True)
    )
    ig = ig.astype(BF)
    ids = ids_ref[0]
    ig_ref[0] = mm(to_natural(ids), ig).astype(BF)
    ge_ref[...] += mm(one_hot_t(ids, ge_ref.shape[0]), ig)

    @pl.when(step == pl.num_programs(0) - 1)
    def _():
        for j in range(dims):
            sum_ref[pl.ds(j, 1), :] = jnp.sum(m_ref[j], axis=0, keepdims=True)
            sum_ref[pl.ds(dims + j, 1), :] = jnp.sum(n_ref[j], axis=0, keepdims=True)
        m, n = sum_ref[0:dims, :], sum_ref[dims : 2 * dims, :]
        rb, er, eb = (par_ref[k * dims : (k + 1) * dims, :] for k in (2, 3, 4))
        rise = one_less_exp(par_ref[0:dims, :])
        sum_ref[0:dims, :] = eb * (rise * n - m)
        sum_ref[dims : 2 * dims, :] = er * m
        sum_ref[2 * dims : 3 * dims, :] = rb * m
        pad = jnp.zeros((8, 128), F32)
        gains = [gg_ref[:, k * 128 : (k + 1) * 128] for k in range(4)]
        for r, (ref, slot) in enumerate(slots(keep_ref, send_ref)):
            own = pl.ds(pl.multiple_of((me_ref[0] ^ r) * 128, 128), 128)
            part = pl.ds(pl.multiple_of((me_ref[0] ^ r) * 64, 64), 64)
            ref[slot, 0:64, :] = ge_ref[part, 0:256].astype(BF)
            ref[slot, 64:128, :] = ge_ref[part, 256:512].astype(BF)
            ref[slot, 128:256, :] = jnp.zeros((128, 256), BF)
            ref[slot, 128:144, 0:128] = sum_ref[0:dims, own].astype(BF)
            ref[slot, 128:144, 128:256] = sum_ref[dims : 2 * dims, own].astype(BF)
            ref[slot, 144:160, 0:128] = sum_ref[2 * dims : 3 * dims, own].astype(BF)
            ref[slot, 160:176, 0:128] = jnp.concatenate(
                [jnp.broadcast_to(go_ref[:, own], (4, 128)), *gains, pad], axis=0
            ).astype(BF)


def add_kernel(n, *refs):
    acc = refs[0][...].astype(F32)
    for ref in refs[1:n]:
        acc = acc + ref[...].astype(F32)
    refs[n][...] = acc[0].astype(BF)
    refs[n + 1][...] = acc[1].astype(BF)


def cut_kernel(bit, at_ref, near_ref, far_ref, keep_ref, send_ref, sum_ref):
    rows = keep_ref.shape[0]
    sum_ref[...] = near_ref[...].astype(F32) + far_ref[...].astype(F32)
    upper = (at_ref[0] // bit) % 2
    keep_ref[...] = sum_ref[pl.ds(pl.multiple_of(upper * rows, rows), rows), :].astype(BF)
    send_ref[...] = sum_ref[pl.ds(pl.multiple_of((1 - upper) * rows, rows), rows), :].astype(BF)


def sum_kernel(*refs):
    refs[-1][...] = total([ref[...] for ref in refs[:-1]]).astype(BF)


def join_kernel(put, at_ref, *refs):
    ins, outs, whole = refs[:2], refs[2:-1], refs[-1]
    rows = whole.shape[0] // 8
    slots = (0, 4, 2, 6, 1, 5, 3, 7)
    for k, slot in enumerate(slots):
        of = at_ref[0] ^ slot
        place = (of % 2) * 4 + ((of // 2) % 2) * 2 + of // 4
        piece = ins[k // 4][(k % 4) * rows : (k % 4 + 1) * rows, :]
        whole[pl.ds(pl.multiple_of(place * rows, rows), rows), :] = piece.astype(F32)
    put(whole, *outs)


def widen_kernel(me_ref, *refs):
    for r, ref in enumerate(refs[:4]):

        @pl.when(pl.program_id(0) == r)
        def _(ref=ref):
            refs[-1][...] = ref[...].astype(F32)


def pairs(axis, bit):
    return [(i, i ^ bit) for i in range(lax.axis_size(axis))]


def swap(v, axis, bit):
    return lax.ppermute(v, axis, pairs(axis, bit))


def gather_pack(v):
    far = swap(v, "ch", 2)
    return [v, swap(v, "ch", 1), far, swap(far, "ch", 1)]


def exclusive(total, rate, span, backward):
    count, mine = lax.axis_size("seq"), lax.axis_index("seq")
    out = jnp.zeros_like(total)
    bit = 1
    while bit < count:
        recv = swap(total, "seq", bit)
        upper = (mine & bit) != 0
        inside = mine & (bit - 1)
        decay = jnp.exp(rate * (-float(bit * span)))
        gap = bit - 1 - inside if backward else inside
        near = jnp.exp(-rate * (gap * span).astype(F32))
        first = jnp.logical_not(upper) if backward else upper
        out = jnp.where(first, out + recv * near, out)
        total = jnp.where(first, total + decay * recv, recv + decay * total)
        bit *= 2
    return out


def block_states(local, rate, span, backward):
    per = span // BLK
    local = local.reshape((-1, per) + local.shape[1:])
    decay = jnp.exp(rate * (-float(BLK)))
    order = range(per)[::-1] if backward else range(per)
    total = 0.0
    for k in order:
        total = total * decay + local[:, k]
    state = exclusive(total, rate, span, backward)
    states = [None] * per
    for k in order:
        states[k] = state
        state = state * decay + local[:, k]
    return jnp.stack(states, axis=1).reshape((-1,) + rate.shape)


def total(parts):
    acc = parts[0].astype(F32)
    for p in parts[1:]:
        acc = acc + p.astype(F32)
    return acc


def small_call(kernel, name, scalars, args, outs, scratch=(), after=()):
    vmem = pl.BlockSpec(memory_space=pltpu.VMEM)
    smem = pl.BlockSpec(memory_space=pltpu.SMEM)
    n = len(scalars) + len(args)

    def body(*refs):
        kernel(*refs[:n], *refs[n + len(after) :])

    return pl.pallas_call(
        body,
        in_specs=[smem] * len(scalars)
        + [vmem] * len(args)
        + [pl.BlockSpec(memory_space=pl.ANY)] * len(after),
        out_specs=[vmem] * len(outs),
        out_shape=[jax.ShapeDtypeStruct(s, t) for s, t in outs],
        scratch_shapes=[pltpu.VMEM(s, t) for s, t in scratch],
        compiler_params=pltpu.CompilerParams(vmem_limit_bytes=VMEM),
        cost_estimate=cost(2),
        name=name,
    )(*scalars, *args, *after)


class Reduction:
    def __init__(self, name, at, keeps, sends):
        self.name, self.at = name, at
        self.args = list(keeps) + [swap(s, "ch", 1) for s in sends]
        self.rows = keeps[0].shape[1]
        self.wide = lax.axis_size("seq") != 8

    def shards(self):
        shape = (self.rows, 256)
        near, far = small_call(
            functools.partial(add_kernel, len(self.args)), self.name + "_add", [], self.args,
            [(shape, BF), (shape, BF)],
        )
        self.near, self.far = near, swap(far, "ch", 2)
        return near

    def whole_seq(self):
        self.whole = lax.psum(total([self.near, self.far]).astype(BF), "seq").astype(F32)

    def scatter(self, bit):
        if self.wide:
            if bit == 1:
                self.whole_seq()
            return self.whole
        rows = self.near.shape[0]
        near, far = small_call(
            functools.partial(cut_kernel, bit), self.name + "_cut", [self.at], [self.near, self.far],
            [((rows // 2, 256), BF)] * 2, [((rows, 256), F32)],
        )
        self.near, self.far = near, swap(far, "seq", bit)
        return near

    def sums(self):
        if self.wide:
            return self.whole
        shape = self.near.shape
        (self.near,) = small_call(
            sum_kernel, self.name + "_sum", [], [self.near, self.far], [(shape, BF)]
        )
        self.far = swap(self.near, "seq", 4)
        return self.near

    def grow(self, bit):
        if self.wide:
            return self.whole
        self.near = jnp.concatenate([self.near, self.far], axis=0)
        self.far = swap(self.near, "seq", bit)
        return self.near

    def join(self, put, outs):
        if self.wide:
            return small_call(put, self.name + "_join", [], [self.whole], outs)
        return small_call(
            functools.partial(join_kernel, put), self.name + "_join", [self.at],
            [self.near, self.far], outs, [((self.rows, 256), F32)],
        )

    def rest(self, put, outs, scatters=()):
        for bit in scatters:
            self.scatter(bit)
        self.sums()
        self.grow(2)
        self.grow(1)
        return self.join(put, outs)


def put_ff(whole, up_ref, down_ref):
    up_ref[...] = whole[0:512, :]
    down_ref[:, 0:256] = whole[512:768, :]
    down_ref[:, 256:512] = whole[768:1024, :]


def put_gates(whole, reset_ref, update_ref, cand_ref, out_ref):
    reset_ref[...] = whole[0:512, :]
    update_ref[...] = whole[512:1024, 0:128]
    cand_ref[...] = whole[512:1024, 128:256]
    out_ref[:, 0:256] = whole[1024:1280, :]
    out_ref[:, 256:512] = whole[1280:1536, :]


def put_mix(whole, value_ref, z_ref, small_ref):
    value_ref[...] = whole[0:512, :]
    z_ref[0:256, :] = whole[512:768, 0:128]
    z_ref[256:512, :] = whole[512:768, 128:256]
    small_ref[...] = whole[768:784, 0:128]


def put_late(whole, emb_ref, rate_ref, beta_ref, eta_ref, small_ref):
    emb_ref[:, 0:256] = whole[0:64, :].astype(BF)
    emb_ref[:, 256:512] = whole[64:128, :].astype(BF)
    rate_ref[...] = whole[128:144, 0:128]
    beta_ref[...] = whole[128:144, 128:256]
    eta_ref[...] = whole[144:160, 0:128]
    small_ref[...] = whole[160:176, 0:128]


def spread(v, me, base, first, blocks):
    far = swap(v, "ch", 2)
    near = swap(v, "ch", 1)
    parts = [v, near, far, swap(far, "ch", 1)]
    n, _, width = v.shape
    step = n if blocks % n == 0 and first % n == 0 else 1
    inner = n // step

    def held(k):
        return lambda r, b, me_ref: (jnp.where(r == k, b, jnp.where(r > k, inner - 1, 0)), 0, 0)

    extra = [] if base is None else [base]
    return pl.pallas_call(
        widen_kernel,
        grid_spec=pltpu.PrefetchScalarGridSpec(
            num_scalar_prefetch=1,
            grid=(4, inner),
            in_specs=[pl.BlockSpec((step, BLK, width), held(k)) for k in range(4)]
            + [pl.BlockSpec(memory_space=pl.ANY)] * len(extra),
            out_specs=pl.BlockSpec(
                (step, BLK, width),
                lambda r, b, me_ref: (((me_ref[0] ^ r) * blocks + first) // step + b, 0, 0),
            ),
        ),
        out_shape=jax.ShapeDtypeStruct((4 * blocks, BLK, width), F32),
        input_output_aliases={5: 0} if extra else {},
        compiler_params=pltpu.CompilerParams(
            dimension_semantics=("arbitrary", "arbitrary"), vmem_limit_bytes=VMEM
        ),
        cost_estimate=cost(4),
        name="widen",
    )(me, *parts, *extra)


def row_block(shape, first=0):
    zeros = (0,) * (len(shape) - 1)
    return pl.BlockSpec((1,) + tuple(shape[1:]), lambda i, *_: (i + first,) + zeros)


def whole_block(shape):
    zeros = (0,) * len(shape)
    return pl.BlockSpec(tuple(shape), lambda i, *_: zeros)


def call(kernel, name, span, us, scalars, rows, fixed, row_outs, fixed_outs, scratch, specs=None, after=()):
    first, count = span
    if specs is None:
        specs = [row_block(v.shape, first if v.shape[0] > count else 0) for v in rows]
    specs = specs + [v[1] if isinstance(v, tuple) else whole_block(v.shape) for v in fixed]
    specs = specs + [pl.BlockSpec(memory_space=pl.ANY)] * len(after)
    fixed = [v[0] if isinstance(v, tuple) else v for v in fixed]
    n = len(scalars) + len(rows) + len(fixed)

    def body(*refs):
        kernel(*refs[:n], *refs[n + len(after) :])

    row_outs = [((count,) + s[1:], t) for s, t in row_outs]
    return pl.pallas_call(
        body,
        grid_spec=pltpu.PrefetchScalarGridSpec(
            num_scalar_prefetch=len(scalars),
            grid=(count,),
            in_specs=specs,
            out_specs=[row_block(s) for s, _ in row_outs] + [whole_block(s) for s, _ in fixed_outs],
            scratch_shapes=[pltpu.VMEM(s, t) for s, t in scratch],
        ),
        out_shape=[jax.ShapeDtypeStruct(s, t) for s, t in row_outs + fixed_outs],
        compiler_params=pltpu.CompilerParams(
            dimension_semantics=("arbitrary",), vmem_limit_bytes=VMEM
        ),
        cost_estimate=cost(us),
        name=name,
    )(*scalars, *rows, *fixed, *after)


def local(
    token_ids, counts, embedding, gain_one, ema_rate, ema_beta, ema_eta, ema_omega, w_value, w_reset,
    w_z, z_scale, z_offset, position_bias, w_update, w_cand, w_out, gain_two, w_up, w_down, cotangent,
):
    batch, span = token_ids.shape
    vocab, width = embedding.shape
    group = lax.axis_size("ch")
    mine = lax.axis_index("ch")
    channels, dims = ema_rate.shape
    z_width = w_z.shape[1]
    units = w_value.shape[1] * group
    seqs = batch // group
    blocks = seqs * span // BLK
    rows = blocks * BLK
    me = mine.astype(jnp.int32).reshape(1)

    pack1 = gather_pack(jnp.concatenate([w_value, w_reset], axis=0))
    halves = width // 2
    pack2 = gather_pack(
        jnp.concatenate(
            [jnp.concatenate([w_update, w_cand], axis=1), w_out[:, :halves], w_out[:, halves:]], axis=0
        )
    )
    pack3 = gather_pack(
        jnp.concatenate([w_up, w_down[:, :halves], w_down[:, halves:]], axis=0)
    )

    par = pl.pallas_call(
        prep_kernel, out_shape=jax.ShapeDtypeStruct((5 * dims + 8, channels), F32), name="prep"
    )(ema_rate.T, ema_beta.T, ema_eta.T, ema_omega[None])
    par = lax.all_gather(par, "ch", axis=1, tiled=True)
    rate = par[:dims]
    g_one, g_two = gain_one[None], gain_two[None]

    ids = lax.dynamic_slice_in_dim(token_ids, mine * seqs, seqs, 0)
    own_counts = lax.dynamic_slice_in_dim(counts, mine * seqs, seqs, 0)
    places = lax.axis_index("seq") * span + jnp.arange(span, dtype=jnp.int32)
    ids = jnp.where(places[None, :] < own_counts[:, None], ids, -1)
    ids_nat = ids.reshape(blocks, 1, BLK)
    ids_tm = ids.reshape(blocks, LANES, STEP).transpose(0, 2, 1).reshape(blocks, 1, BLK)

    bias = jnp.concatenate([position_bias, jnp.zeros((1,), F32)])[None]
    (bias,) = small_call(table_kernel, "table", [], [bias], [((BLK, BLK), F32)])

    row = (blocks, BLK, width)
    row_v = (blocks, BLK, units)
    states = (blocks, dims, LANES, width)
    edge = (blocks, dims, width)
    every = (0, blocks)
    x, emb = call(
        embed_kernel, "embed", every, 4, [], [ids_tm], [embedding, g_one], [(row, F32), (row, BF)], [], []
    )
    ex, lv = call(
        enter_kernel, "enter", every, 6, [], [x], [par], [(states, F32), (edge, F32)], [], []
    )
    se = block_states(lv, rate, span, False)
    (es,) = call(run_kernel, "run", every, 7, [], [x, ex, se], [par], [(row, F32)], [], [])
    vp, rp, mix, zp, up, cp, res = call(
        forward_kernel, "forward", every, 12, [me], [es, x, emb],
        [bias, w_z, z_scale, z_offset, *pack1, *pack2],
        [(row_v, BF), (row_v, BF), (row_v, BF), ((blocks, BLK, z_width), F32), (row, BF), (row, BF),
         (row, F32)],
        [],
        [((width, units), BF), ((width, units), BF), ((width, width), BF), ((width, width), BF),
         ((units, width), BF)],
    )
    at_seq = lax.axis_index("seq").astype(jnp.int32).reshape(1)
    cot = cotangent.reshape(batch * span // BLK, BLK, width)

    def pack_outs(rows):
        return [((2, rows, 256), BF), ((2, rows, 256), BF)]

    out, gr, keep3, send3, gg2 = call(
        ff_kernel, "ff", every, 14, [me], [ids_nat, cot, res], [g_two, *pack3],
        [(row, BF), (row, F32)],
        pack_outs(1024) + [((4, 128), F32)],
        [((width, units), BF), ((units, width), BF), ((width, units), F32), ((units, width), F32)],
        specs=[
            row_block(ids_nat.shape),
            pl.BlockSpec((1, BLK, width), lambda i, me_ref: (me_ref[0] * blocks + i, 0, 0)),
            row_block(res.shape),
        ],
    )
    sum3 = Reduction("ff", at_seq, [keep3], [send3])
    output = spread(out, me, None, 0, blocks).reshape(batch, span, width)

    def half_of(pack, k):
        return [(v, pl.BlockSpec((512, 256), lambda i, *_: (k, 0))) for v in pack]

    gm, ge, direct, keep2, send2 = call(
        gates_back_kernel, "gates_back", every, 17, [me], [es, emb, rp, mix, up, cp, gr],
        [*half_of(pack1, 1), *pack2],
        [(row_v, BF), (row, F32), (row, BF)],
        pack_outs(1536),
        [((width, units), BF), ((width, width), BF), ((width, width), BF), ((units, width), BF),
         ((width, units), F32), ((width, width), F32), ((width, width), F32), ((units, width), F32)],
    )
    sum2 = Reduction("gates", at_seq, [keep2], [send2])
    g, gnv, ae, lb, keep1, send1 = call(
        mix_back_kernel, "mix_back", every, 24, [], [es, x, vp, zp, gm, ge],
        [bias, w_z, z_scale, z_offset, par, gg2, *half_of(pack1, 0)],
        [(row, F32), (row, BF), (states, F32), (edge, F32)],
        pack_outs(896),
        [((width, units), BF), ((width, units), F32), ((width, z_width), F32),
         ((8, z_width), F32), ((BLK, BLK), F32)],
        after=[sum3.shards()],
    )
    sum1 = Reduction("mix", at_seq, [keep1], [send1])
    ar = block_states(lb, rate, span, True)
    sum3.whole_seq()
    pins = [[sum2.shards(), sum1.shards()], [sum2.scatter(1)]]
    parts = [(0, blocks // 2), (blocks // 2, blocks // 2)]
    keep, send = [], []
    input_grad = None
    for part, pin in zip(parts, pins):
        ig, kept, sent = call(
            leave_kernel, "leave", part, 15, [me],
            [ids_tm, emb, x, g, ae, ar, ex, se, direct, gnv],
            [par, g_one],
            [(row, BF)],
            pack_outs(256),
            [((BLK, width), F32), ((dims, LANES, width), F32), ((dims, LANES, width), F32),
             ((vocab, width), F32), ((1, width), F32), ((1, width), F32), ((3 * dims, width), F32)],
            after=pin,
        )
        keep.append(kept)
        send.append(sent)
        input_grad = spread(ig, me, input_grad, part[0], blocks)
    input_grad = input_grad.reshape(batch, span, width)
    last = Reduction("late", at_seq, keep, send)
    last.shards()
    emb_part, grad_rate, grad_beta, grad_eta, late = last.rest(
        put_late,
        [((64, width), BF), ((dims, channels), F32), ((dims, channels), F32),
         ((dims, channels), F32), ((16, 128), F32)],
        (1, 2, 4),
    )
    ge = lax.all_gather(emb_part, "ch", axis=0, tiled=True).astype(F32)
    grad_up, grad_down = small_call(
        put_ff, "ff_join", [], [sum3.whole], [((width, 256), F32), ((256, width), F32)]
    )
    grad_reset, grad_update, grad_cand, grad_out = sum2.rest(
        put_gates,
        [((width, 256), F32), ((width, 128), F32), ((width, 128), F32), ((256, width), F32)],
        (2, 4),
    )
    grad_value, grad_z, small = sum1.rest(
        put_mix, [((width, 256), F32), ((width, z_width), F32), ((16, 128), F32)], (1, 2, 4)
    )
    return (
        output,
        input_grad,
        ge,
        late[4:8].reshape(-1),
        grad_rate.T,
        grad_beta.T,
        grad_eta.T,
        late[0],
        grad_value,
        grad_reset,
        grad_z,
        small[0:2],
        small[2:4],
        small[4:6].reshape(-1)[:-1],
        grad_update,
        grad_cand,
        grad_out,
        small[6:10].reshape(-1),
        grad_up,
        grad_down,
    )


def solution(mesh):
    return jax.shard_map(
        local,
        mesh=mesh,
        in_specs=(
            P(None, "seq"), P(), P(), P(), P("ch", None), P("ch", None), P("ch", None), P("ch"),
            P(None, "ch"), P(None, "ch"), P(), P(), P(), P(), P(None, "ch"), P(None, "ch"),
            P("ch", None), P(), P(None, "ch"), P("ch", None), P(None, "seq", None),
        ),
        out_specs=(
            P(None, "seq", None), P(None, "seq", None), P(), P(), P("ch", None), P("ch", None),
            P("ch", None), P("ch"), P(None, "ch"), P(None, "ch"), P(), P(), P(), P(), P(None, "ch"),
            P(None, "ch"), P("ch", None), P(), P(None, "ch"), P("ch", None),
        ),
        check_vma=False,
    )
```

time: 1720 us -> 355 us (0.21)
  other arithmetic: 497 us -> 13.3 us
  waiting for transfers between devices: 492 us -> 74.4 us
  local copies, waits for them, and re-layouts: 375 us -> 17.6 us
  matrix products: 250 us -> 0 us
  Pallas kernels: 0 us -> 166 us
  blocking collectives: 77.5 us -> 16.5 us
  starting transfers between devices: 1.21 us -> 51.2 us
    scatter-add x1 -> x0, other arithmetic: 397 us -> none  [ema_tables(): kernel[jnp.maximum(lag_idx, 0)]]
    gather x2 -> x0, local copies, waits for them, and re-layouts: 249 us -> none  [ema_tables(): kernel[jnp.maximum(lag_idx, 0)]]
    dot_general x40 -> x0, matrix products: 247 us -> none  [the longest x3 89 us: whole_ema(): jnp.einsum('tsc,bsc->btc', toeplitz, inputs, precision=lax.Precision.HIGH...]
    psum x4 -> x1, waiting for transfers between devices: 245 us -> 23.7 us  [whole_seq(): lax.psum(total([self.near, self.far]).astype(BF), 'seq').astype(F32)]
    pallas_call x0 -> x34, Pallas kernels: none -> 166 us  [the longest x9 109 us: call(): pl.pallas_call(body, grid_spec=pltpu.PrefetchScalarGridSpec(num_scalar_pr...]
    reduce_scatter x2 -> x0, waiting for transfers between devices: 125 us -> none  [the longest x1 71.4 us: local(): lax.psum_scatter(jnp.dot(gated, w_out, preferred_element_type=jnp.float32...]
    all_gather x5 -> x0, waiting for transfers between devices: 122 us -> none  [the longest x1 53.6 us: local(): resid = lax.all_gather(resid_own, 'ch', axis=1, tiled=True)]
    ppermute x0 -> x51, starting transfers between devices: none -> 51.2 us  [swap(): return lax.ppermute(v, axis, pairs(axis, bit))]
  transfers between devices with their start and end apart: 11 -> 52, of which waited for: 9 -> 22; matrix products, arithmetic and copies ran while one was open for 53% -> 6% of each run, Pallas kernels for 0% -> 42%
where the time goes in v1:
time: 355 us; the launch traced here: 354 us
  Pallas kernels  166 us (47%)
  waiting for transfers between devices  74.4 us (21%)
  starting transfers between devices  51.2 us (14%)
  local copies, waits for them, and re-layouts  17.6 us (5%)
  blocking collectives  16.5 us (5%)
  between operations  14.6 us (4%)
  other arithmetic  13.3 us (4%)
    pallas_call x9, Pallas kernels, call(): pl.pallas_call(body, grid_spec=pltpu.PrefetchScalarGridSpec(num_scalar_pr...  109 us
    ppermute x51, starting transfers between devices, swap(): return lax.ppermute(v, axis, pairs(axis, bit))  51.2 us
    ppermute x51, waiting for transfers between devices, swap(): return lax.ppermute(v, axis, pairs(axis, bit))  50.7 us
    pallas_call x21, Pallas kernels, small_call(): pl.pallas_call(body, in_specs=[smem] * len(scalars) + [vmem] * len(args)...  42.2 us
    psum x1, waiting for transfers between devices, whole_seq(): lax.psum(total([self.near, self.far]).astype(BF), 'seq').astype(F32)  23.7 us
    pallas_call x3, Pallas kernels, spread(): pl.pallas_call(widen_kernel, grid_spec=pltpu.PrefetchScalarGridSpec(num_s...  13.7 us
    all_gather x1, blocking collectives, local(): par = lax.all_gather(par, 'ch', axis=1, tiled=True)  10.5 us
    unnamed x99, local copies, waits for them, and re-layouts  9.33 us
  transfers between devices with their start and end apart: 52, of which 22 were waited for; matrix products, arithmetic and copies ran while one was open for 6% of the time, Pallas kernels for 42%

profile of v1, /device:TPU:0, one launch (start us, length us, event | category | flops | bytes accessed | tf_op | source)
XLA Modules:
  0.0 353.5 jit_solution(13555702819567034223)
XLA Ops:
  9.3 3.0 collective-permute-start.7
  16.0 10.5 %all_gather.6.refs_1_.refs_3_.refs_10_.refs_11_ = f32[88,512]{1,0:T(8,128)} all-gather(f32[88,128]{1,0:T(8,128)} %prep.1), channel_id=1, replica_groups=mesh['seq'=8,'ch'=4] {'ch'}, dimensions={1}, use_global_device_ids=true | all-gather | bytes 225280 | tf_op jit(solution)/shard_map/all_gather | solution.py:869
  26.5 3.9 %embed.1 = (f32[4,256,512]{2,1,0:T(8,128)}, bf16[4,256,512]{2,1,0:T(8,128)(2,1)}) custom-call(s32[4,1,256]{2,1,0:T(1,128)} %reshape.85.refs_0_.refs_1_, bf16[256,512]{1,0:T(8,128)(2,1)} %refs_1_.1, f32[1,512]{1,0:T(1,128)} %bitcast.30), custom_call_target="tpu_custom_call" | custom-call | flops 4000000000 | bytes 100000 | tf_op jit(solution)/shard_map/embed/pallas_call | solution.py:821
  30.4 5.7 %enter.1 = (f32[4,16,8,512]{3,2,1,0:T(8,128)}, f32[4,16,512]{2,1,0:T(8,128)}) custom-call(f32[4,256,512]{2,1,0:T(8,128)} %get-tuple-element.93.refs_0_.refs_2_.refs_1_.refs_3_, f32[88,512]{1,0:T(8,128)} %all_gather.6.refs_1_.refs_3_.refs_10_.refs_11_), custom_call_target="tpu_custom_call" | custom-call | flops 6000000000 | bytes 100000 | tf_op jit(solution)/shard_map/enter/pallas_call | solution.py:821
  47.2 2.5 collective-permute-done.1
  49.8 2.8 collective-permute-start.2
  52.6 2.6 table.1.refs_4_.refs_6_
  60.7 7.6 %run.1.refs_1_.refs_0_ = f32[4,256,512]{2,1,0:T(8,128)} custom-call(f32[4,256,512]{2,1,0:T(8,128)} %get-tuple-element.93.refs_0_.refs_2_.refs_1_.refs_3_, f32[4,16,8,512]{3,2,1,0:T(8,128)} %get-tuple-element.94.refs_1_.refs_7_, f32[4,16,512]{2,1,0:T(8,128)} %add_select_fusion.2.refs_2_.refs_8_, f32[88,512]{1,0:T(8,128)} %all_gather.6.refs_1_.refs_3_.refs_10_.refs_11_), custom_call_target="tpu_custom_call" | custom-call | flops 7000000000 | bytes 100000 | tf_op jit(solution)/shard_map/run/pallas_call | solution.py:821
  70.3 11.7 %forward.1 = (bf16[4,256,1024]{2,1,0:T(8,128)(2,1)}, bf16[4,256,1024]{2,1,0:T(8,128)(2,1)}, bf16[4,256,1024]{2,1,0:T(8,128)(2,1)}, f32[4,256,128]{2,1,0:T(8,128)...) custom-call(s32[1]{0:T(128)} %bitcast.refs_0_.me_ref, ...), custom_call_target="tpu_custom_call" | custom-call | flops 12000000000 | bytes 100000 | tf_op jit(solution)/shard_map/forward/pallas_call | solution.py:821
  82.8 14.1 %ff.1 = (bf16[4,256,512]{2,1,0:T(8,128)(2,1)}, f32[4,256,512]{2,1,0:T(8,128)}, bf16[2,1024,256]{2,1,0:T(8,128)(2,1)}, bf16[2,1024,256]{2,1,0:T(8,128)(2,1)}, f32[4,128]{1,0:T(4,128)}) custom-call(s32[1]{0:T(128)} %bitcast.refs_0_.me_ref, s32[4,1,256]{2,1,0:T(1,128)} %reshape.78.refs_1_, bf16[16,256,512]{2,1,0:T(8,128)(2,1)} %refs_2_.1, ...), custom_call_target="tpu_custom_call" | custom-call | flops 14000000000 | bytes 100000 | tf_op jit(solution)/shard_map/ff/pallas_call | solution.py:821
  97.5 16.7 %gates_back.1 = (bf16[4,256,1024]{2,1,0:T(8,128)(2,1)}, f32[4,256,512]{2,1,0:T(8,128)}, bf16[4,256,512]{2,1,0:T(8,128)(2,1)}, bf16[2,1536,256]{2,1,0:T(8,128)(2,1)}, bf16[2,1536,256]{2,1,0:T(8,128)(2,1)}) custom-call(s32[1]{0:T(128)} %bitcast.refs_0_.me_ref, f32[4,256,512]{2,1,0:T(8,128)} %run.1.refs_1_.refs_0_, ...), custom_call_target="tpu_custom_call" | custom-call | flops 16999999488 | bytes 100000 | tf_op jit(solution)/shard_map/gates_back/pallas_call | solution.py:821
  117.0 2.6 ff_add.1
  119.6 18.8 %mix_back.1 = (f32[4,256,512]{2,1,0:T(8,128)}, bf16[4,256,512]{2,1,0:T(8,128)(2,1)}, f32[4,16,8,512]{3,2,1,0:T(8,128)}, f32[4,16,512]{2,1,0:T(8,128)}, bf16[2,89...) custom-call(f32[4,256,512]{2,1,0:T(8,128)} %run.1.refs_1_.refs_0_, ...), custom_call_target="tpu_custom_call" | custom-call | flops 24000000000 | bytes 100000 | tf_op jit(solution)/shard_map/mix_back/pallas_call | solution.py:821
  141.0 4.0 %collective-permute-done.16 = f32[4,16,512]{2,1,0:T(8,128)S(1)} collective-permute-done((f32[4,16,512]{2,1,0:T(8,128)S(1)}, f32[4,16,512]{2,1,0:T(8,128)S(1)}, u32[]{:S(2)}, u32[]{:S(2)}) %collective-permute-start.16) | collective-permute-done | bytes 131104 | tf_op jit(solution)/shard_map/ppermute | solution.py:597
  148.8 2.5 collective-permute-done.17
  151.3 3.5 collective-permute-start.18
  154.8 4.9 %collective-permute-done.18 = f32[4,16,512]{2,1,0:T(8,128)S(1)} collective-permute-done((f32[4,16,512]{2,1,0:T(8,128)S(1)}, f32[4,16,512]{2,1,0:T(8,128)S(1)}, u32[]{:S(2)}, u32[]{:S(2)}) %collective-permute-start.18) | collective-permute-done | bytes 131104 | tf_op jit(solution)/shard_map/ppermute | solution.py:597
  163.5 3.2 gates_add.1
  167.2 2.6 mix_add.1
  169.8 15.0 %leave.3 = (bf16[2,256,512]{2,1,0:T(8,128)(2,1)}, bf16[2,256,256]{2,1,0:T(8,128)(2,1)}, bf16[2,256,256]{2,1,0:T(8,128)(2,1)}) custom-call(s32[1]{0:T(128)} %bitcast.refs_0_.me_ref, s32[4,1,256]{2,1,0:T(1,128)} %reshape.85.refs_0_.refs_1_, bf16[4,256,512]{2,1,0:T(8,128)(2,1)} %get-tuple-element.96.refs_3_.refs_2_, ...), custom_call_target="tpu_custom_call" | custom-call | flops 15000000512 | bytes 100000 | tf_op jit(solution)/shard_map/leave/pallas_call | solution.py:821
  187.3 2.6 gates_cut.3
  189.9 15.1 %leave.2 = (bf16[2,256,512]{2,1,0:T(8,128)(2,1)}, bf16[2,256,256]{2,1,0:T(8,128)(2,1)}, bf16[2,256,256]{2,1,0:T(8,128)(2,1)}) custom-call(s32[1]{0:T(128)} %bitcast.refs_0_.me_ref, s32[4,1,256]{2,1,0:T(1,128)} %reshape.85.refs_0_.refs_1_, bf16[4,256,512]{2,1,0:T(8,128)(2,1)} %get-tuple-element.96.refs_3_.refs_2_, ...), custom_call_target="tpu_custom_call" | custom-call | flops 15000000512 | bytes 100000 | tf_op jit(solution)/shard_map/leave/pallas_call | solution.py:821
  205.6 5.8 %widen.3 = f32[16,256,512]{2,1,0:T(8,128)} custom-call(s32[1]{0:T(128)} %bitcast.refs_0_.me_ref, bf16[4,256,512]{2,1,0:T(8,128)(2,1)} %get-tuple-element.98.refs_0_, bf16[4,256,512]{2,1,0:T(8,128)(2,1)} %collective-permute-done.12.refs_1_, bf16[4,256,512]{2,1,0:T(8,128)(2,1)} %collective-permute-done.13.refs_2_, ...), custom_call_target="tpu_custom_call" | custom-call | flops 4000000000 | bytes 100000 | tf_op jit(solution)/shard_map/widen/pallas_call | solution.py:776
  211.4 23.7 %all-reduce.2.cloned.1.call-done = bf16[1024,256]{1,0:T(8,128)(2,1)} async-done(((bf16[1024,256]{1,0:T(8,128)(2,1)}), bf16[1024,256]{1,0:T(8,128)(2,1)}) %all-reduce.2.cloned.1.call-update) | async-done | bytes 524304 | tf_op jit(solution)/shard_map/psum | solution.py:685
  275.3 2.6 collective-permute-done.40.refs_1_
  284.1 3.9 %collective-permute-done.41 = bf16[112,256]{1,0:T(8,128)(2,1)S(1)} collective-permute-done((bf16[112,256]{1,0:T(8,128)(2,1)}, bf16[112,256]{1,0:T(8,128)(2,1)S(1)}, u32[]{:S(2)}, u32[]{:S(2)}) %collective-permute-start.41) | collective-permute-done | bytes 57376 | tf_op jit(solution)/shard_map/ppermute | solution.py:597
  299.6 6.0 %all_gather.7 = bf16[256,512]{1,0:T(8,128)(2,1)S(1)} all-gather(bf16[64,512]{1,0:T(8,128)(2,1)} %get-tuple-element.139), channel_id=1, replica_groups=mesh['seq'=8,'ch'=4] {'ch'}, dimensions={0}, use_global_device_ids=true | all-gather | bytes 327680 | tf_op jit(solution)/shard_map/all_gather | solution.py:976
  311.0 6.0 %collective-permute-done.46.refs_1_ = bf16[192,256]{1,0:T(8,128)(2,1)S(1)} collective-permute-done((bf16[192,256]{1,0:T(8,128)(2,1)S(1)}, bf16[192,256]{1,0:T(8,128)(2,1)S(1)}, u32[]{:S(2)}, u32[]{:S(2)}) %collective-permute-start.46) | collective-permute-done | bytes 98336 | tf_op jit(solution)/shard_map/ppermute | solution.py:597
  320.5 4.0 %widen.4.refs_4_ = f32[16,256,512]{2,1,0:T(8,128)} custom-call(s32[1]{0:T(128)} %bitcast.refs_0_.me_ref, bf16[2,256,512]{2,1,0:T(8,128)(2,1)} %get-tuple-element.126.refs_0_, bf16[2,256,512]{2,1,0:T(8,128)(2,1)} %copy-done.23, bf16[2,256,512]{2,1,0:T(8,128)(2,1)} %copy-done.22, bf16[2,256,512]{2,1,0:T(8,128)(2,1)} %collective-permute-done.27.refs_3_), custom_call_target="tpu_custom_call" | custom-call | flops 4000000000 | bytes 100000 | tf_op jit(solution)/shard_map/widen/pallas_call | solution.py:776
  324.5 2.6 collective-permute-done.47
  331.1 2.5 collective-permute-done.48
  337.9 4.0 %widen.5 = f32[16,256,512]{2,1,0:T(8,128)} custom-call(s32[1]{0:T(128)} %bitcast.refs_0_.me_ref, bf16[2,256,512]{2,1,0:T(8,128)(2,1)} %get-tuple-element.122.refs_0_, bf16[2,256,512]{2,1,0:T(8,128)(2,1)} %copy-done.2, bf16[2,256,512]{2,1,0:T(8,128)(2,1)} %copy-done.1, bf16[2,256,512]{2,1,0:T(8,128)(2,1)} %copy-done.3, ...), custom_call_target="tpu_custom_call", output_to_operand_aliasing={{}: (5, {})} | custom-call | flops 4000000000 | bytes 100000 | tf_op jit(solution)/shard_map/widen/pallas_call | solution.py:776
  (243 shorter events, 122.1 us)
Async XLA Ops:
  7.2 228.0 %all-reduce.2.cloned.1.call-start = ((), (), s32[]{:S(2)}) async-start(), calls=%async_computation | async-start | bytes 1048576 | tf_op jit(solution)/shard_map/psum | solution.py:685
  9.3 50.9 %collective-permute-start.7 = (bf16[1024,256]{1,0:T(8,128)(2,1)S(1)}, bf16[1024,256]{1,0:T(8,128)(2,1)S(1)}, u32[]{:S(2)}, u32[]{:S(2)}) collective-permute-start(bf16[1024,256]{1,0:T(8,128)(2,1)S(1)} %pad_maximum_fusion.refs_12_), channel_id=1, source_target_pairs={{0,2},{1,3},{2,0},{3,1},{4,6},{5,7},{6,4},{7,5},{8,10},{9,11},{10,... | collective-permute-start | bytes 1572872 | tf_op jit(solution)/shard_map/ppermute | solution.py:597
  12.3 56.0 %collective-permute-start.6 = (bf16[1024,256]{1,0:T(8,128)(2,1)S(1)}, bf16[1024,256]{1,0:T(8,128)(2,1)S(1)}, u32[]{:S(2)}, u32[]{:S(2)}) collective-permute-start(bf16[1024,256]{1,0:T(8,128)(2,1)S(1)} %pad_maximum_fusion.refs_12_), channel_id=1, source_target_pairs={{0,1},{1,0},{2,3},{3,2},{4,5},{5,4},{6,7},{7,6},{8,9},{9,8},{10,11... | collective-permute-start | bytes 1572872 | tf_op jit(solution)/shard_map/ppermute | solution.py:597
  39.8 20.4 %collective-permute-start.4 = (bf16[1024,256]{1,0:T(8,128)(2,1)S(1)}, bf16[1024,256]{1,0:T(8,128)(2,1)}, u32[]{:S(2)}, u32[]{:S(2)}) collective-permute-start(bf16[1024,256]{1,0:T(8,128)(2,1)S(1)} %constant_dynamic-update-slice_fusion.refs_8_.refs_12_), channel_id=1, source_target_pairs={{0,2},{1,3},{2,0},{3,1},{4,6},{5,7},{6,4},{7,5},{8,10},{9,11},{10,... | collective-permute-start | bytes 1572872 | tf_op jit(solution)/shard_map/ppermute | solution.py:597
  41.4 27.9 %collective-permute-start.3 = (bf16[1024,256]{1,0:T(8,128)(2,1)S(1)}, bf16[1024,256]{1,0:T(8,128)(2,1)}, u32[]{:S(2)}, u32[]{:S(2)}) collective-permute-start(bf16[1024,256]{1,0:T(8,128)(2,1)S(1)} %constant_dynamic-update-slice_fusion.refs_8_.refs_12_), channel_id=1, source_target_pairs={{0,1},{1,0},{2,3},{3,2},{4,5},{5,4},{6,7},{7,6},{8,9},{9,8},{10,11... | collective-permute-start | bytes 1572872 | tf_op jit(solution)/shard_map/ppermute | solution.py:597
  57.9 11.4 %collective-permute-start.10 = (bf16[1024,256]{1,0:T(8,128)(2,1)S(1)}, bf16[1024,256]{1,0:T(8,128)(2,1)}, u32[]{:S(2)}, u32[]{:S(2)}) collective-permute-start(bf16[1024,256]{1,0:T(8,128)(2,1)S(1)} %pad_maximum_fusion.1.refs_5_), channel_id=1, source_target_pairs={{0,2},{1,3},{2,0},{3,1},{4,6},{5,7},{6,4},{7,5},{8,10},{9,11},{10,... | collective-permute-start | bytes 1572872 | tf_op jit(solution)/shard_map/ppermute | solution.py:597
  68.3 13.7 %collective-permute-start.9 = (bf16[1024,256]{1,0:T(8,128)(2,1)S(1)}, bf16[1024,256]{1,0:T(8,128)(2,1)S(1)}, u32[]{:S(2)}, u32[]{:S(2)}) collective-permute-start(bf16[1024,256]{1,0:T(8,128)(2,1)S(1)} %pad_maximum_fusion.1.refs_5_), channel_id=1, source_target_pairs={{0,1},{1,0},{2,3},{3,2},{4,5},{5,4},{6,7},{7,6},{8,9},{9,8},{10,11... | collective-permute-start | bytes 1572872 | tf_op jit(solution)/shard_map/ppermute | solution.py:597
  69.3 12.7 %collective-permute-start.11 = (bf16[1024,256]{1,0:T(8,128)(2,1)}, bf16[1024,256]{1,0:T(8,128)(2,1)}, u32[]{:S(2)}, u32[]{:S(2)}) collective-permute-start(bf16[1024,256]{1,0:T(8,128)(2,1)} %collective-permute-done.10.refs_7_), channel_id=1, source_target_pairs={{0,1},{1,0},{2,3},{3,2},{4,5},{5,4},{6,7},{7,6},{8,9},{9,8},{10,11... | collective-permute-start | bytes 1572872 | tf_op jit(solution)/shard_map/ppermute | solution.py:597
  96.9 19.1 %collective-permute-start.15 = (bf16[2,1024,256]{2,1,0:T(8,128)(2,1)}, bf16[2,1024,256]{2,1,0:T(8,128)(2,1)S(1)}, u32[]{:S(2)}, u32[]{:S(2)}) collective-permute-start(bf16[2,1024,256]{2,1,0:T(8,128)(2,1)} %get-tuple-element.110), channel_id=1, source_target_pairs={{0,1},{1,0},{2,3},{3,2},{4,5},{5,4},{6,7},{7,6},{8,9},{9,8},{10,11... | collective-permute-start | bytes 3145736 | tf_op jit(solution)/shard_map/ppermute | solution.py:597
  114.2 48.1 %collective-permute-start.19 = (bf16[2,1536,256]{2,1,0:T(8,128)(2,1)}, bf16[2,1536,256]{2,1,0:T(8,128)(2,1)S(1)}, u32[]{:S(2)}, u32[]{:S(2)}) collective-permute-start(bf16[2,1536,256]{2,1,0:T(8,128)(2,1)} %get-tuple-element.118), channel_id=1, source_target_pairs={{0,1},{1,0},{2,3},{3,2},{4,5},{5,4},{6,7},{7,6},{8,9},{9,8},{10,11... | collective-permute-start | bytes 4718600 | tf_op jit(solution)/shard_map/ppermute | solution.py:597
  114.3 40.5 %collective-permute-start.13 = (bf16[4,256,512]{2,1,0:T(8,128)(2,1)}, bf16[4,256,512]{2,1,0:T(8,128)(2,1)}, u32[]{:S(2)}, u32[]{:S(2)}) collective-permute-start(bf16[4,256,512]{2,1,0:T(8,128)(2,1)} %get-tuple-element.98.refs_0_), channel_id=1, source_target_pairs={{0,2},{1,3},{2,0},{3,1},{4,6},{5,7},{6,4},{7,5},{8,10},{9,11},{10,... | collective-permute-start | bytes 3145736 | tf_op jit(solution)/shard_map/ppermute | solution.py:597
  148.3 13.1 %collective-permute-start.50 = (bf16[1024,256]{1,0:T(8,128)(2,1)}, bf16[1024,256]{1,0:T(8,128)(2,1)S(1)}, u32[]{:S(2)}, u32[]{:S(2)}) collective-permute-start(bf16[1024,256]{1,0:T(8,128)(2,1)} %get-tuple-element.163), channel_id=1, source_target_pairs={{0,2},{1,3},{2,0},{3,1},{4,6},{5,7},{6,4},{7,5},{8,10},{9,11},{10,... | collective-permute-start | bytes 1572872 | tf_op jit(solution)/shard_map/ppermute | solution.py:597
  148.8 18.4 %collective-permute-start.24 = (bf16[2,896,256]{2,1,0:T(8,128)(2,1)}, bf16[2,896,256]{2,1,0:T(8,128)(2,1)}, u32[]{:S(2)}, u32[]{:S(2)}) collective-permute-start(bf16[2,896,256]{2,1,0:T(8,128)(2,1)} %get-tuple-element.124), channel_id=1, source_target_pairs={{0,1},{1,0},{2,3},{3,2},{4,5},{5,4},{6,7},{7,6},{8,9},{9,8},{10,11... | collective-permute-start | bytes 2752520 | tf_op jit(solution)/shard_map/ppermute | solution.py:597
  154.8 50.2 %collective-permute-start.12 = (bf16[4,256,512]{2,1,0:T(8,128)(2,1)}, bf16[4,256,512]{2,1,0:T(8,128)(2,1)}, u32[]{:S(2)}, u32[]{:S(2)}) collective-permute-start(bf16[4,256,512]{2,1,0:T(8,128)(2,1)} %get-tuple-element.98.refs_0_), channel_id=1, source_target_pairs={{0,1},{1,0},{2,3},{3,2},{4,5},{5,4},{6,7},{7,6},{8,9},{9,8},{10,11... | collective-permute-start | bytes 3145736 | tf_op jit(solution)/shard_map/ppermute | solution.py:597
  159.7 45.9 %collective-permute-start.14 = (bf16[4,256,512]{2,1,0:T(8,128)(2,1)}, bf16[4,256,512]{2,1,0:T(8,128)(2,1)}, u32[]{:S(2)}, u32[]{:S(2)}) collective-permute-start(bf16[4,256,512]{2,1,0:T(8,128)(2,1)} %collective-permute-done.13.refs_2_), channel_id=1, source_target_pairs={{0,1},{1,0},{2,3},{3,2},{4,5},{5,4},{6,7},{7,6},{8,9},{9,8},{10,11... | collective-permute-start | bytes 3145736 | tf_op jit(solution)/shard_map/ppermute | solution.py:597
  166.7 19.7 %collective-permute-start.20 = (bf16[1536,256]{1,0:T(8,128)(2,1)}, bf16[1536,256]{1,0:T(8,128)(2,1)S(1)}, u32[]{:S(2)}, u32[]{:S(2)}) collective-permute-start(bf16[1536,256]{1,0:T(8,128)(2,1)} %get-tuple-element.120), channel_id=1, source_target_pairs={{0,2},{1,3},{2,0},{3,1},{4,6},{5,7},{6,4},{7,5},{8,10},{9,11},{10,... | collective-permute-start | bytes 2359304 | tf_op jit(solution)/shard_map/ppermute | solution.py:597
  184.9 105.4 %collective-permute-start.26 = (bf16[2,256,512]{2,1,0:T(8,128)(2,1)}, bf16[2,256,512]{2,1,0:T(8,128)(2,1)S(1)}, u32[]{:S(2)}, u32[]{:S(2)}) collective-permute-start(bf16[2,256,512]{2,1,0:T(8,128)(2,1)} %get-tuple-element.126.refs_0_), channel_id=1, source_target_pairs={{0,2},{1,3},{2,0},{3,1},{4,6},{5,7},{6,4},{7,5},{8,10},{9,11},{10,... | collective-permute-start | bytes 1572872 | tf_op jit(solution)/shard_map/ppermute | solution.py:597
  186.4 133.3 %collective-permute-start.25 = (bf16[2,256,512]{2,1,0:T(8,128)(2,1)}, bf16[2,256,512]{2,1,0:T(8,128)(2,1)S(1)}, u32[]{:S(2)}, u32[]{:S(2)}) collective-permute-start(bf16[2,256,512]{2,1,0:T(8,128)(2,1)} %get-tuple-element.126.refs_0_), channel_id=1, source_target_pairs={{0,1},{1,0},{2,3},{3,2},{4,5},{5,4},{6,7},{7,6},{8,9},{9,8},{10,11... | collective-permute-start | bytes 1572872 | tf_op jit(solution)/shard_map/ppermute | solution.py:597
  186.4 50.8 %collective-permute-start.37 = (bf16[896,256]{1,0:T(8,128)(2,1)S(1)}, bf16[896,256]{1,0:T(8,128)(2,1)S(1)}, u32[]{:S(2)}, u32[]{:S(2)}) collective-permute-start(bf16[896,256]{1,0:T(8,128)(2,1)S(1)} %copy-done.29), channel_id=1, source_target_pairs={{0,2},{1,3},{2,0},{3,1},{4,6},{5,7},{6,4},{7,5},{8,10},{9,11},{10,... | collective-permute-start | bytes 1376264 | tf_op jit(solution)/shard_map/ppermute | solution.py:597
  205.0 36.1 %collective-permute-start.28 = (bf16[2,256,256]{2,1,0:T(8,128)(2,1)S(1)}, bf16[2,256,256]{2,1,0:T(8,128)(2,1)S(1)}, u32[]{:S(2)}, u32[]{:S(2)}) collective-permute-start(bf16[2,256,256]{2,1,0:T(8,128)(2,1)S(1)} %copy-done.34), channel_id=1, source_target_pairs={{0,1},{1,0},{2,3},{3,2},{4,5},{5,4},{6,7},{7,6},{8,9},{9,8},{10,11... | collective-permute-start | bytes 786440 | tf_op jit(solution)/shard_map/ppermute | solution.py:597
  205.6 35.5 %collective-permute-start.29 = (bf16[2,256,256]{2,1,0:T(8,128)(2,1)}, bf16[2,256,256]{2,1,0:T(8,128)(2,1)S(1)}, u32[]{:S(2)}, u32[]{:S(2)}) collective-permute-start(bf16[2,256,256]{2,1,0:T(8,128)(2,1)} %get-tuple-element.130), channel_id=1, source_target_pairs={{0,1},{1,0},{2,3},{3,2},{4,5},{5,4},{6,7},{7,6},{8,9},{9,8},{10,11... | collective-permute-start | bytes 786440 | tf_op jit(solution)/shard_map/ppermute | solution.py:597
  240.2 12.4 %collective-permute-start.38 = (bf16[448,256]{1,0:T(8,128)(2,1)}, bf16[448,256]{1,0:T(8,128)(2,1)S(1)}, u32[]{:S(2)}, u32[]{:S(2)}) collective-permute-start(bf16[448,256]{1,0:T(8,128)(2,1)} %get-tuple-element.146), channel_id=1, source_target_pairs={{0,4},{4,0},{8,12},{12,8},{16,20},{20,16},{24,28},{28,24},{1,5},{5... | collective-permute-start | bytes 688136 | tf_op jit(solution)/shard_map/ppermute | solution.py:597
  247.6 13.6 %collective-permute-start.44 = (bf16[768,256]{1,0:T(8,128)(2,1)S(1)}, bf16[768,256]{1,0:T(8,128)(2,1)S(1)}, u32[]{:S(2)}, u32[]{:S(2)}) collective-permute-start(bf16[768,256]{1,0:T(8,128)(2,1)S(1)} %copy-done.31), channel_id=1, source_target_pairs={{0,4},{4,0},{8,12},{12,8},{16,20},{20,16},{24,28},{28,24},{1,5},{5... | collective-permute-start | bytes 1179656 | tf_op jit(solution)/shard_map/ppermute | solution.py:597
  249.4 41.0 %collective-permute-start.22 = (bf16[2,256,512]{2,1,0:T(8,128)(2,1)S(1)}, bf16[2,256,512]{2,1,0:T(8,128)(2,1)S(1)}, u32[]{:S(2)}, u32[]{:S(2)}) collective-permute-start(bf16[2,256,512]{2,1,0:T(8,128)(2,1)S(1)} %copy-done), channel_id=1, source_target_pairs={{0,2},{1,3},{2,0},{3,1},{4,6},{5,7},{6,4},{7,5},{8,10},{9,11},{10,... | collective-permute-start | bytes 1572872 | tf_op jit(solution)/shard_map/ppermute | solution.py:597
  257.6 10.1 %collective-permute-start.39 = (bf16[224,256]{1,0:T(8,128)(2,1)}, bf16[224,256]{1,0:T(8,128)(2,1)S(1)}, u32[]{:S(2)}, u32[]{:S(2)}) collective-permute-start(bf16[224,256]{1,0:T(8,128)(2,1)} %get-tuple-element.148), channel_id=1, source_target_pairs={{0,8},{4,12},{8,0},{12,4},{16,24},{20,28},{24,16},{28,20},{1,9},{5... | collective-permute-start | bytes 344072 | tf_op jit(solution)/shard_map/ppermute | solution.py:597
  265.7 26.3 %collective-permute-start.45 = (bf16[384,256]{1,0:T(8,128)(2,1)}, bf16[384,256]{1,0:T(8,128)(2,1)S(1)}, u32[]{:S(2)}, u32[]{:S(2)}) collective-permute-start(bf16[384,256]{1,0:T(8,128)(2,1)} %get-tuple-element.154), channel_id=1, source_target_pairs={{0,8},{4,12},{8,0},{12,4},{16,24},{20,28},{24,16},{28,20},{1,9},{5... | collective-permute-start | bytes 589832 | tf_op jit(solution)/shard_map/ppermute | solution.py:597
  290.3 46.0 %collective-permute-start.21 = (bf16[2,256,512]{2,1,0:T(8,128)(2,1)S(1)}, bf16[2,256,512]{2,1,0:T(8,128)(2,1)S(1)}, u32[]{:S(2)}, u32[]{:S(2)}) collective-permute-start(bf16[2,256,512]{2,1,0:T(8,128)(2,1)S(1)} %copy-done), channel_id=1, source_target_pairs={{0,1},{1,0},{2,3},{3,2},{4,5},{5,4},{6,7},{7,6},{8,9},{9,8},{10,11... | collective-permute-start | bytes 1572872 | tf_op jit(solution)/shard_map/ppermute | solution.py:597
  290.4 30.0 %collective-permute-start.27 = (bf16[2,256,512]{2,1,0:T(8,128)(2,1)S(1)}, bf16[2,256,512]{2,1,0:T(8,128)(2,1)}, u32[]{:S(2)}, u32[]{:S(2)}) collective-permute-start(bf16[2,256,512]{2,1,0:T(8,128)(2,1)S(1)} %collective-permute-done.26.refs_2_), channel_id=1, source_target_pairs={{0,1},{1,0},{2,3},{3,2},{4,5},{5,4},{6,7},{7,6},{8,9},{9,8},{10,11... | collective-permute-start | bytes 1572872 | tf_op jit(solution)/shard_map/ppermute | solution.py:597
  291.9 44.4 %collective-permute-start.23 = (bf16[2,256,512]{2,1,0:T(8,128)(2,1)S(1)}, bf16[2,256,512]{2,1,0:T(8,128)(2,1)S(1)}, u32[]{:S(2)}, u32[]{:S(2)}) collective-permute-start(bf16[2,256,512]{2,1,0:T(8,128)(2,1)S(1)} %collective-permute-done.22.refs_2_), channel_id=1, source_target_pairs={{0,1},{1,0},{2,3},{3,2},{4,5},{5,4},{6,7},{7,6},{8,9},{9,8},{10,11... | collective-permute-start | bytes 1572872 | tf_op jit(solution)/shard_map/ppermute | solution.py:597
  296.5 12.3 %collective-permute-start.42 = (bf16[224,256]{1,0:T(8,128)(2,1)S(1)}, bf16[224,256]{1,0:T(8,128)(2,1)S(1)}, u32[]{:S(2)}, u32[]{:S(2)}) collective-permute-start(bf16[224,256]{1,0:T(8,128)(2,1)S(1)} %pad_maximum_fusion.5), channel_id=1, source_target_pairs={{0,8},{4,12},{8,0},{12,4},{16,24},{20,28},{24,16},{28,20},{1,9},{5... | collective-permute-start | bytes 344072 | tf_op jit(solution)/shard_map/ppermute | solution.py:597
  316.9 10.2 %collective-permute-start.43 = (bf16[448,256]{1,0:T(8,128)(2,1)S(1)}, bf16[448,256]{1,0:T(8,128)(2,1)S(1)}, u32[]{:S(2)}, u32[]{:S(2)}) collective-permute-start(bf16[448,256]{1,0:T(8,128)(2,1)S(1)} %pad_maximum_fusion.3.refs_1_), channel_id=1, source_target_pairs={{0,4},{4,0},{8,12},{12,8},{16,20},{20,16},{24,28},{28,24},{1,5},{5... | collective-permute-start | bytes 688136 | tf_op jit(solution)/shard_map/ppermute | solution.py:597
  333.7 9.9 %collective-permute-start.49 = (bf16[768,256]{1,0:T(8,128)(2,1)S(1)}, bf16[768,256]{1,0:T(8,128)(2,1)S(1)}, u32[]{:S(2)}, u32[]{:S(2)}) collective-permute-start(bf16[768,256]{1,0:T(8,128)(2,1)S(1)} %pad_maximum_fusion.2.refs_1_), channel_id=1, source_target_pairs={{0,4},{4,0},{8,12},{12,8},{16,20},{20,16},{24,28},{28,24},{1,5},{5... | collective-permute-start | bytes 1179656 | tf_op jit(solution)/shard_map/ppermute | solution.py:597
  (69 other events, 383.2 us)
Sparse Core Ops, SparseCore 0:
  162.5 72.6 all-reduce.1

commit v2 on v1

--- a/solution.py
+++ b/solution.py
@@ -17,8 +17,29 @@
 VMEM = 60 * 1024 * 1024
 
 
+SCALE = 10**9
+
+ORDER = []
+LANDED = []
+
+
+def before():
+    ready = ORDER[-1:] + LANDED
+    LANDED.clear()
+    return ready
+
+
+def land(*arrays):
+    LANDED.extend(arrays)
+
+
+def done(outs):
+    ORDER.append(outs[0] if isinstance(outs, (list, tuple)) else outs)
+    return outs
+
+
 def cost(us):
-    return pl.CostEstimate(flops=us * 10**9, bytes_accessed=10**5, transcendentals=0)
+    return pl.CostEstimate(flops=us * SCALE, bytes_accessed=10**5, transcendentals=0)
 
 
 def sig(v):
@@ -122,6 +143,18 @@
     out_ref[...] = jnp.where(seen, v, -1e30)
 
 
+def pack_kernel(wv_ref, wr_ref, wu_ref, wc_ref, wo_ref, up_ref, down_ref, p1_ref, p2_ref, p3_ref):
+    p1_ref[0:512, :] = wv_ref[...]
+    p1_ref[512:1024, :] = wr_ref[...]
+    p2_ref[0:512, 0:128] = wu_ref[...]
+    p2_ref[0:512, 128:256] = wc_ref[...]
+    p2_ref[512:768, :] = wo_ref[:, 0:256]
+    p2_ref[768:1024, :] = wo_ref[:, 256:512]
+    p3_ref[0:512, :] = up_ref[...]
+    p3_ref[512:768, :] = down_ref[:, 0:256]
+    p3_ref[768:1024, :] = down_ref[:, 256:512]
+
+
 def embed_kernel(ids_ref, tab_ref, gain_ref, x_ref, emb_ref):
     emb = mm_tn(one_hot_t(ids_ref[0], tab_ref.shape[0]), tab_ref[...])
     inv = lax.rsqrt(jnp.mean(emb * emb, axis=-1, keepdims=True) + EPS)
@@ -129,8 +162,36 @@
     emb_ref[0] = emb.astype(BF)
 
 
-def enter_kernel(x_ref, par_ref, ex_ref, lv_ref):
+def slope_kernel(x_ref, par_ref, e_ref, f_ref):
+    dims, width = e_ref.shape[1], e_ref.shape[3]
+    half = 8
+    for c0 in range(0, width, 128):
+        sl = pl.ds(c0, 128)
+        for j0 in range(0, dims, half):
+            decay = [jnp.exp(-wide(par_ref[pl.ds(j, 1), sl])) for j in range(j0, j0 + half)]
+
+            def body(t, carry):
+                e, f = carry
+                xt = x_ref[0, at(t), sl]
+                f = tuple(d * v + u for d, v, u in zip(decay, f, e))
+                e = tuple(d * v + xt for d, v in zip(decay, e))
+                return e, f
+
+            zero = x_ref[0, at(0), sl] * 0.0
+            e, f = lax.fori_loop(0, STEP, body, ((zero,) * half, (zero,) * half), unroll=4)
+            for k in range(half):
+                e_ref[0, j0 + k, :, sl] = e[k]
+                f_ref[0, j0 + k, :, sl] = f[k]
+
+
+def enter_kernel(me_ref, x_ref, p0_ref, p1_ref, p2_ref, p3_ref, ex_ref, lv_ref, par_ref):
     dims, width = lv_ref.shape[1:]
+
+    @pl.when(pl.program_id(0) == 0)
+    def _():
+        for r, ref in enumerate((p0_ref, p1_ref, p2_ref, p3_ref)):
+            own = pl.ds(pl.multiple_of((me_ref[0] ^ r) * 128, 128), 128)
+            par_ref[:, own] = ref[...]
 
     row = lane_iota()
     for c0 in range(0, width, 128):
@@ -245,12 +306,12 @@
     keys = (za * zs_ref[1:2, :] + zo_ref[1:2, :]).astype(BF)
     weights = softmax_rows(query, keys, bias_ref[...], zp.shape[-1] ** -0.5).astype(BF)
     vp = mm(x_ref[0].astype(BF), wv_ref[...])
-    vp_ref[0] = vp.astype(BF)
+    vp_ref[0] = vp
     values = (vp * sig(vp)).astype(BF)
     mixed = mm(weights, values)
     mix_ref[0] = mixed.astype(BF)
     rp = mm(e, wr_ref[...])
-    rp_ref[0] = rp.astype(BF)
+    rp_ref[0] = rp
     gated = (rp * sig(rp) * mixed).astype(BF)
     up = mm(e, wu_ref[...])
     up_ref[0] = up.astype(BF)
@@ -332,7 +393,7 @@
     dir_ref[0] = (grad_resid * (1.0 - up)).astype(BF)
     ac_ref[...] += mm(e_t, gcp)
     au_ref[...] += mm(e_t, gup)
-    rp = rp_ref[0].astype(F32)
+    rp = rp_ref[0]
     rs = sig(rp)
     reset = rp * rs
     mixed = mix_ref[0].astype(F32)
@@ -361,7 +422,7 @@
 ):
     packs, rest = rest[:4], rest[4:]
     (g_ref, gnv_ref, ae_ref, lb_ref, keep_ref, send_ref) = rest[:6]
-    (wv_ref, av_ref, az_ref, gz_ref, gb_ref) = rest[6:]
+    (wv_ref, av_ref, az_ref, gz_ref, gb_ref, as_ref) = rest[6:]
     step = pl.program_id(0)
 
     @pl.when(step == 0)
@@ -382,7 +443,7 @@
     query = (za * s0 + zo_ref[0:1, :]).astype(BF)
     keys = (za * s1 + zo_ref[1:2, :]).astype(BF)
     weights = softmax_rows(query, keys, bias_ref[...], factor)
-    vp = vp_ref[0].astype(F32)
+    vp = vp_ref[0]
     vs = sig(vp)
     values = (vp * vs).astype(BF)
     gvp = (mm_tn(weights.astype(BF), gm) * slope(vp, vs)).astype(BF)
@@ -433,27 +494,20 @@
         small = jnp.concatenate(
             [gz_ref[0:4, :], bias[:, :128], bias[:, 128:], gg_ref[...], zero], axis=0
         )
+        high = small.astype(BF)
+        low = (small - high.astype(F32)).astype(BF)
+        small = jnp.concatenate([high, low], axis=1)
+        as_ref[512:768, 0:128] = az_ref[0:256, :].astype(BF)
+        as_ref[512:768, 128:256] = az_ref[256:512, :].astype(BF)
         for r, (ref, slot) in enumerate(slots(keep_ref, send_ref)):
-            ref[slot, 0:512, :] = av_ref[:, r * 256 : r * 256 + 256].astype(BF)
-            ref[slot, 512:768, 0:128] = az_ref[0:256, :].astype(BF)
-            ref[slot, 512:768, 128:256] = az_ref[256:512, :].astype(BF)
-            ref[slot, 768:896, :] = jnp.zeros((128, 256), BF)
-            ref[slot, 768:784, 0:128] = small.astype(BF)
-
-
-def leave_kernel(
-    me_ref, ids_ref, emb_ref, x_ref, g_ref, ae_ref, ar_ref, ex_ref, se_ref, dir_ref, gnv_ref,
-    par_ref, gain_ref, ig_ref, keep_ref, send_ref,
-    gn_ref, m_ref, n_ref, ge_ref, go_ref, gg_ref, sum_ref,
-):
-    step = pl.program_id(0)
+            as_ref[0:512, :] = av_ref[:, r * 256 : r * 256 + 256].astype(BF)
+            for k in range(8):
+                ref[slot, k * 112 : k * 112 + 96, :] = as_ref[k * 96 : k * 96 + 96, :]
+                ref[slot, k * 112 + 96 : k * 112 + 112, :] = small
+
+
+def adjoint_kernel(x_ref, g_ref, ae_ref, ex_ref, se_ref, par_ref, gn_ref, mn_ref):
     dims, width = se_ref.shape[1:]
-
-    @pl.when(step == 0)
-    def _():
-        for ref in (ge_ref, go_ref, gg_ref, m_ref, n_ref):
-            ref[...] = jnp.zeros_like(ref)
-
     place = lane_iota().astype(F32)
     half = 8
     for c0 in range(0, width, 128):
@@ -464,25 +518,19 @@
             rates = [wide(par_ref[pl.ds(j, 1), sl]) for j in js]
             decay = [jnp.exp(-r) for r in rates]
             ws = [wide(par_ref[pl.ds(dims + j, 1), sl]) for j in js]
-            a_end = [
-                ae_ref[0, j, :, sl]
-                + jnp.exp(r * (LANES - 1.0 - place) * (-float(STEP)))
-                * wide(ar_ref[0, pl.ds(j, 1), sl])
-                for j, r in zip(js, rates)
-            ]
 
             def emit(t, a, gt):
                 parts = [w * v for w, v in zip(ws, a)]
                 while len(parts) > 1:
                     parts = [p + q for p, q in zip(parts[::2], parts[1::2])]
                 if j0 == 0:
-                    gn_ref[at(t), sl] = parts[0] + omega * gt
+                    gn_ref[0, at(t), sl] = parts[0] + omega * gt
                 else:
-                    gn_ref[at(t), sl] += parts[0]
+                    gn_ref[0, at(t), sl] += parts[0]
 
             gt = g_ref[0, at(STEP - 1), sl]
             xt = x_ref[0, at(STEP - 1), sl]
-            a = tuple(gt + d * v for d, v in zip(decay, a_end))
+            a = tuple(gt + d * ae_ref[0, j, :, sl] for j, d in zip(js, decay))
             emit(STEP - 1, a, gt)
             m = tuple(xt * v for v in a)
             zero = tuple(jnp.zeros((LANES, 128), F32) for _ in js)
@@ -499,13 +547,70 @@
                 n = tuple(u + xt * v for u, v in zip(n, b))
                 return a, b, m, n
 
-            a, b, m, n = lax.fori_loop(0, STEP - 1, body, (a, zero, m, zero))
+            carry = (a, zero, m, zero)
+            for i in range(3):
+                carry = body(i, carry)
+            a, b, m, n = lax.fori_loop(3, STEP - 1, body, carry, unroll=4)
             for k, j in enumerate(js):
                 start = ex_ref[0, j, :, sl] + jnp.exp(rates[k] * place * (-float(STEP))) * wide(
                     se_ref[0, pl.ds(j, 1), sl]
                 )
-                m_ref[j, :, sl] += m[k]
-                n_ref[j, :, sl] += n[k] + start * (a[k] + decay[k] * b[k])
+                mn_ref[0, pl.ds(j, 1), sl] = jnp.sum(m[k], axis=0, keepdims=True)
+                mn_ref[0, pl.ds(dims + j, 1), sl] = jnp.sum(
+                    n[k] + start * (a[k] + decay[k] * b[k]), axis=0, keepdims=True
+                )
+
+
+def leave_kernel(n_parts, me_ref, ids_ref, emb_ref, x_ref, g_ref, ar_ref, ex_ref, se_ref, el_ref, ed_ref,
+                 dir_ref, gnv_ref, *rest):
+    locals_, rest = rest[: 2 * n_parts], rest[2 * n_parts :]
+    par_ref, gain_ref, ig_ref, keep_ref, send_ref = rest[:5]
+    gn_ref, ge_ref, go_ref, gg_ref, sum_ref = rest[5:]
+    step = pl.program_id(0)
+    dims, width = se_ref.shape[1:]
+
+    @pl.when(step == 0)
+    def _():
+        for ref in (ge_ref, go_ref, gg_ref, sum_ref):
+            ref[...] = jnp.zeros_like(ref)
+
+    for k in range(n_parts):
+
+        @pl.when(step == k)
+        def _(k=k):
+            gn_ref[...] = locals_[2 * k][0]
+            sum_ref[0 : 2 * dims, :] += locals_[2 * k + 1][0]
+
+    place = lane_iota().astype(F32)
+    for c0 in range(0, width, 128):
+        sl = pl.ds(c0, 128)
+        rates = [wide(par_ref[pl.ds(j, 1), sl]) for j in range(dims)]
+        decay = [jnp.exp(-r) for r in rates]
+        ws = [wide(par_ref[pl.ds(dims + j, 1), sl]) for j in range(dims)]
+        far = [
+            jnp.exp(r * (LANES - 1.0 - place) * (-float(STEP))) * wide(ar_ref[0, pl.ds(j, 1), sl])
+            for j, r in enumerate(rates)
+        ]
+        for j in range(dims):
+            start = ex_ref[0, j, :, sl] + jnp.exp(rates[j] * place * (-float(STEP))) * wide(
+                se_ref[0, pl.ds(j, 1), sl]
+            )
+            whole = jnp.exp(rates[j] * (-float(STEP)))
+            more_m = far[j] * decay[j] * el_ref[0, j, :, sl]
+            more_n = far[j] * (decay[j] * ed_ref[0, j, :, sl] + float(STEP) * whole * start)
+            sum_ref[pl.ds(j, 1), sl] += jnp.sum(more_m, axis=0, keepdims=True)
+            sum_ref[pl.ds(dims + j, 1), sl] += jnp.sum(more_n, axis=0, keepdims=True)
+
+        def body(i, c):
+            t = STEP - 1 - i
+            c = tuple(d * v for d, v in zip(decay, c))
+            parts = [w * v for w, v in zip(ws, c)]
+            while len(parts) > 1:
+                parts = [p + q for p, q in zip(parts[::2], parts[1::2])]
+            gn_ref[at(t), sl] += parts[0]
+            return c
+
+        lax.fori_loop(0, STEP, body, tuple(far), unroll=4)
 
     go_ref[...] += jnp.sum(g_ref[0] * x_ref[0], axis=0, keepdims=True)
     emb = emb_ref[0].astype(F32)
@@ -524,9 +629,6 @@
 
     @pl.when(step == pl.num_programs(0) - 1)
     def _():
-        for j in range(dims):
-            sum_ref[pl.ds(j, 1), :] = jnp.sum(m_ref[j], axis=0, keepdims=True)
-            sum_ref[pl.ds(dims + j, 1), :] = jnp.sum(n_ref[j], axis=0, keepdims=True)
         m, n = sum_ref[0:dims, :], sum_ref[dims : 2 * dims, :]
         rb, er, eb = (par_ref[k * dims : (k + 1) * dims, :] for k in (2, 3, 4))
         rise = one_less_exp(par_ref[0:dims, :])
@@ -540,45 +642,58 @@
             part = pl.ds(pl.multiple_of((me_ref[0] ^ r) * 64, 64), 64)
             ref[slot, 0:64, :] = ge_ref[part, 0:256].astype(BF)
             ref[slot, 64:128, :] = ge_ref[part, 256:512].astype(BF)
-            ref[slot, 128:256, :] = jnp.zeros((128, 256), BF)
             ref[slot, 128:144, 0:128] = sum_ref[0:dims, own].astype(BF)
             ref[slot, 128:144, 128:256] = sum_ref[dims : 2 * dims, own].astype(BF)
             ref[slot, 144:160, 0:128] = sum_ref[2 * dims : 3 * dims, own].astype(BF)
-            ref[slot, 160:176, 0:128] = jnp.concatenate(
+            ref[slot, 144:160, 128:256] = jnp.concatenate(
                 [jnp.broadcast_to(go_ref[:, own], (4, 128)), *gains, pad], axis=0
             ).astype(BF)
 
 
-def add_kernel(n, *refs):
+def repair(v):
+    out = []
+    for k in range(0, v.shape[0], 112):
+        both = v[k + 96 : k + 112, 0:128] + v[k + 96 : k + 112, 128:256]
+        high = both.astype(BF)
+        low = (both - high.astype(F32)).astype(BF)
+        out += [v[k : k + 96].astype(BF), jnp.concatenate([high, low], axis=1)]
+    return jnp.concatenate(out, axis=0)
+
+
+def plain(v):
+    return v.astype(BF)
+
+
+def add_kernel(n, fix, *refs):
     acc = refs[0][...].astype(F32)
     for ref in refs[1:n]:
         acc = acc + ref[...].astype(F32)
-    refs[n][...] = acc[0].astype(BF)
-    refs[n + 1][...] = acc[1].astype(BF)
-
-
-def cut_kernel(bit, at_ref, near_ref, far_ref, keep_ref, send_ref, sum_ref):
+    refs[n][...] = fix(acc[0])
+    refs[n + 1][...] = fix(acc[1])
+
+
+def cut_kernel(bit, fix, at_ref, near_ref, far_ref, keep_ref, send_ref, sum_ref):
     rows = keep_ref.shape[0]
     sum_ref[...] = near_ref[...].astype(F32) + far_ref[...].astype(F32)
     upper = (at_ref[0] // bit) % 2
-    keep_ref[...] = sum_ref[pl.ds(pl.multiple_of(upper * rows, rows), rows), :].astype(BF)
-    send_ref[...] = sum_ref[pl.ds(pl.multiple_of((1 - upper) * rows, rows), rows), :].astype(BF)
-
-
-def sum_kernel(*refs):
-    refs[-1][...] = total([ref[...] for ref in refs[:-1]]).astype(BF)
-
-
-def join_kernel(put, at_ref, *refs):
-    ins, outs, whole = refs[:2], refs[2:-1], refs[-1]
-    rows = whole.shape[0] // 8
-    slots = (0, 4, 2, 6, 1, 5, 3, 7)
-    for k, slot in enumerate(slots):
-        of = at_ref[0] ^ slot
-        place = (of % 2) * 4 + ((of // 2) % 2) * 2 + of // 4
-        piece = ins[k // 4][(k % 4) * rows : (k % 4 + 1) * rows, :]
-        whole[pl.ds(pl.multiple_of(place * rows, rows), rows), :] = piece.astype(F32)
-    put(whole, *outs)
+    keep_ref[...] = fix(sum_ref[pl.ds(pl.multiple_of(upper * rows, rows), rows), :])
+    send_ref[...] = fix(sum_ref[pl.ds(pl.multiple_of((1 - upper) * rows, rows), rows), :])
+
+
+def plain_sum_kernel(near_ref, far_ref, out_ref):
+    out_ref[...] = (near_ref[...].astype(F32) + far_ref[...].astype(F32)).astype(out_ref.dtype)
+
+
+def sum_kernel(fix, *refs):
+    refs[-1][...] = fix(total([ref[...] for ref in refs[:-1]]))
+
+
+def join_kernel(put, at_ref, near_ref, far_ref, *refs):
+    rows = near_ref.shape[0]
+    upper = at_ref[0] % 2
+    refs[-1][pl.ds(pl.multiple_of(upper * rows, rows), rows), :] = near_ref[...].astype(F32)
+    refs[-1][pl.ds(pl.multiple_of((1 - upper) * rows, rows), rows), :] = far_ref[...].astype(F32)
+    put(refs[-1], *refs[:-1])
 
 
 def widen_kernel(me_ref, *refs):
@@ -597,38 +712,53 @@
     return lax.ppermute(v, axis, pairs(axis, bit))
 
 
-def gather_pack(v):
-    far = swap(v, "ch", 2)
-    return [v, swap(v, "ch", 1), far, swap(far, "ch", 1)]
-
-
-def exclusive(total, rate, span, backward):
-    count, mine = lax.axis_size("seq"), lax.axis_index("seq")
+def hop_kernel(bit, span, backward, at_ref, total_ref, recv_ref, out_ref, rate_ref, next_ref, new_ref):
+    place = at_ref[0]
+    upper = (place // bit) % 2 == 1
+    inside = place % bit
+    gap = bit - 1 - inside if backward else inside
+    first = jnp.logical_not(upper) if backward else upper
+    rate = rate_ref[0 : total_ref.shape[1], :]
+    decay = jnp.exp(rate * (-float(bit * span)))
+    near = jnp.exp(-rate * (gap * span).astype(F32))
+    for k in range(total_ref.shape[0]):
+        total, recv = total_ref[k], recv_ref[k]
+        new_ref[k] = out_ref[k] + jnp.where(first, recv * near, 0.0)
+        next_ref[k] = jnp.where(first, total + decay * recv, recv + decay * total)
+
+
+def exclusive(total, par, place, span, backward, between):
+    count = lax.axis_size("seq")
     out = jnp.zeros_like(total)
     bit = 1
+    step = 0
     while bit < count:
         recv = swap(total, "seq", bit)
-        upper = (mine & bit) != 0
-        inside = mine & (bit - 1)
-        decay = jnp.exp(rate * (-float(bit * span)))
-        gap = bit - 1 - inside if backward else inside
-        near = jnp.exp(-rate * (gap * span).astype(F32))
-        first = jnp.logical_not(upper) if backward else upper
-        out = jnp.where(first, out + recv * near, out)
-        total = jnp.where(first, total + decay * recv, recv + decay * total)
+        if step < len(between):
+            between[step]()
+        total, out = small_call(
+            functools.partial(hop_kernel, bit, span, backward), "hop", [place],
+            [total, recv, out, par], [(total.shape, F32)] * 2,
+        )
         bit *= 2
+        step += 1
+    for rest in between[step:]:
+        rest()
     return out
 
 
-def block_states(local, rate, span, backward):
+def block_states(local, par, place, span, backward, between):
     per = span // BLK
+    if per == 1:
+        return exclusive(local, par, place, span, backward, between)
+    rate = par[: local.shape[1]]
     local = local.reshape((-1, per) + local.shape[1:])
     decay = jnp.exp(rate * (-float(BLK)))
     order = range(per)[::-1] if backward else range(per)
     total = 0.0
     for k in order:
         total = total * decay + local[:, k]
-    state = exclusive(total, rate, span, backward)
+    state = exclusive(total, par, place, span, backward, between)
     states = [None] * per
     for k in order:
         states[k] = state
@@ -643,7 +773,8 @@
     return acc
 
 
-def small_call(kernel, name, scalars, args, outs, scratch=(), after=()):
+def small_call(kernel, name, scalars, args, outs, scratch=()):
+    after = before()
     vmem = pl.BlockSpec(memory_space=pltpu.VMEM)
     smem = pl.BlockSpec(memory_space=pltpu.SMEM)
     n = len(scalars) + len(args)
@@ -651,7 +782,7 @@
     def body(*refs):
         kernel(*refs[:n], *refs[n + len(after) :])
 
-    return pl.pallas_call(
+    made = pl.pallas_call(
         body,
         in_specs=[smem] * len(scalars)
         + [vmem] * len(args)
@@ -663,78 +794,96 @@
         cost_estimate=cost(2),
         name=name,
     )(*scalars, *args, *after)
+    return done(made)
 
 
 class Reduction:
-    def __init__(self, name, at, keeps, sends):
-        self.name, self.at = name, at
+    def __init__(self, name, at, keeps, sends, fix=plain):
+        self.name, self.at, self.fix = name, at, fix
         self.args = list(keeps) + [swap(s, "ch", 1) for s in sends]
-        self.rows = keeps[0].shape[1]
         self.wide = lax.axis_size("seq") != 8
 
     def shards(self):
-        shape = (self.rows, 256)
-        near, far = small_call(
-            functools.partial(add_kernel, len(self.args)), self.name + "_add", [], self.args,
-            [(shape, BF), (shape, BF)],
-        )
-        self.near, self.far = near, swap(far, "ch", 2)
-        return near
+        shape = self.args[0].shape[1:]
+        self.near, far = small_call(
+            functools.partial(add_kernel, len(self.args), self.fix), self.name + "_add", [],
+            self.args, [(shape, BF), (shape, BF)],
+        )
+        self.far = swap(far, "ch", 2)
+        return [self.near]
+
+    def both(self):
+        shape = self.args[0].shape
+        (self.near,) = small_call(
+            functools.partial(sum_kernel, self.fix), self.name + "_add", [], self.args, [(shape, BF)]
+        )
+        if self.wide:
+            self.near = lax.psum(self.near.astype(F32), "seq").astype(BF)
+            self.far = jnp.zeros_like(self.near)
+        else:
+            self.far = swap(self.near, "seq", 1)
+
+    def split(self):
+        shape = self.args[0].shape[1:]
+        self.near, far = small_call(
+            functools.partial(add_kernel, 2, self.fix), self.name + "_split", [],
+            [self.near, self.far], [(shape, BF), (shape, BF)],
+        )
+        self.far = swap(far, "ch", 2)
 
     def whole_seq(self):
-        self.whole = lax.psum(total([self.near, self.far]).astype(BF), "seq").astype(F32)
-
-    def scatter(self, bit):
+        kind = F32 if self.wide else BF
+        (v,) = small_call(
+            plain_sum_kernel, self.name + "_sum", [], [self.near, self.far], [(self.near.shape, kind)]
+        )
+        self.whole = lax.psum(v, "seq")
+
+    def halve(self):
         if self.wide:
-            if bit == 1:
-                self.whole_seq()
-            return self.whole
+            return []
         rows = self.near.shape[0]
-        near, far = small_call(
-            functools.partial(cut_kernel, bit), self.name + "_cut", [self.at], [self.near, self.far],
-            [((rows // 2, 256), BF)] * 2, [((rows, 256), F32)],
-        )
-        self.near, self.far = near, swap(far, "seq", bit)
-        return near
-
-    def sums(self):
+        self.near, far = small_call(
+            functools.partial(cut_kernel, 1, self.fix), self.name + "_cut", [self.at],
+            [self.near, self.far], [((rows // 2, 256), BF)] * 2, [((rows, 256), F32)],
+        )
+        self.far = swap(far, "seq", 1)
+        return [self.near]
+
+    def hop(self, bit):
         if self.wide:
-            return self.whole
-        shape = self.near.shape
+            return []
         (self.near,) = small_call(
-            sum_kernel, self.name + "_sum", [], [self.near, self.far], [(shape, BF)]
-        )
-        self.far = swap(self.near, "seq", 4)
-        return self.near
-
-    def grow(self, bit):
-        if self.wide:
-            return self.whole
-        self.near = jnp.concatenate([self.near, self.far], axis=0)
+            functools.partial(sum_kernel, self.fix), self.name + "_sum", [], [self.near, self.far],
+            [(self.near.shape, BF)],
+        )
         self.far = swap(self.near, "seq", bit)
-        return self.near
-
-    def join(self, put, outs):
-        if self.wide:
+        return [self.near]
+
+    def join(self, put, outs, halved=True):
+        if self.wide and halved:
+            self.whole_seq()
             return small_call(put, self.name + "_join", [], [self.whole], outs)
+        if halved:
+            shape = (2 * self.near.shape[0], 256)
+            return small_call(
+                functools.partial(join_kernel, put), self.name + "_join", [self.at],
+                [self.near, self.far], outs, [(shape, F32)],
+            )
+
+        def finish(near_ref, far_ref, *refs):
+            refs[-1][...] = near_ref[...].astype(F32) + far_ref[...].astype(F32)
+            put(refs[-1], *refs[:-1])
+
         return small_call(
-            functools.partial(join_kernel, put), self.name + "_join", [self.at],
-            [self.near, self.far], outs, [((self.rows, 256), F32)],
-        )
-
-    def rest(self, put, outs, scatters=()):
-        for bit in scatters:
-            self.scatter(bit)
-        self.sums()
-        self.grow(2)
-        self.grow(1)
-        return self.join(put, outs)
+            finish, self.name + "_join", [], [self.near, self.far], outs,
+            [(self.near.shape, F32)],
+        )
 
 
 def put_ff(whole, up_ref, down_ref):
-    up_ref[...] = whole[0:512, :]
-    down_ref[:, 0:256] = whole[512:768, :]
-    down_ref[:, 256:512] = whole[768:1024, :]
+    up_ref[...] = whole[0:512, :].astype(F32)
+    down_ref[:, 0:256] = whole[512:768, :].astype(F32)
+    down_ref[:, 256:512] = whole[768:1024, :].astype(F32)
 
 
 def put_gates(whole, reset_ref, update_ref, cand_ref, out_ref):
@@ -745,54 +894,74 @@
     out_ref[:, 256:512] = whole[1280:1536, :]
 
 
-def put_mix(whole, value_ref, z_ref, small_ref):
-    value_ref[...] = whole[0:512, :]
-    z_ref[0:256, :] = whole[512:768, 0:128]
-    z_ref[256:512, :] = whole[512:768, 128:256]
-    small_ref[...] = whole[768:784, 0:128]
-
-
-def put_late(whole, emb_ref, rate_ref, beta_ref, eta_ref, small_ref):
+def put_mix(whole, value_ref, z_ref, scale_ref, offset_ref, bias_ref, gain_ref):
+    for k in range(8):
+        part = whole[k * 112 : k * 112 + 96, :]
+        if k < 5:
+            value_ref[k * 96 : k * 96 + 96, :] = part
+        elif k == 5:
+            value_ref[480:512, :] = part[0:32]
+            z_ref[0:64, :] = part[32:96, 0:128]
+            z_ref[256:320, :] = part[32:96, 128:256]
+        else:
+            first = (k - 6) * 96 + 64
+            z_ref[first : first + 96, :] = part[:, 0:128]
+            z_ref[256 + first : 256 + first + 96, :] = part[:, 128:256]
+    small = whole[96:112, 0:128] + whole[96:112, 128:256]
+    scale_ref[...] = small[0:2]
+    offset_ref[...] = small[2:4]
+    bias_ref[...] = jnp.concatenate([small[4:5], small[5:6]], axis=1)[:, :255]
+    for k in range(4):
+        gain_ref[:, k * 128 : k * 128 + 128] = small[6 + k : 7 + k]
+
+
+def put_late(whole, emb_ref, rate_ref, beta_ref, eta_ref, omega_ref, gain_ref):
     emb_ref[:, 0:256] = whole[0:64, :].astype(BF)
     emb_ref[:, 256:512] = whole[64:128, :].astype(BF)
     rate_ref[...] = whole[128:144, 0:128]
     beta_ref[...] = whole[128:144, 128:256]
     eta_ref[...] = whole[144:160, 0:128]
-    small_ref[...] = whole[160:176, 0:128]
-
-
-def spread(v, me, base, first, blocks):
+    omega_ref[...] = whole[144:145, 128:256]
+    for k in range(4):
+        gain_ref[:, k * 128 : k * 128 + 128] = whole[148 + k : 149 + k, 128:256]
+
+
+def spread(v):
     far = swap(v, "ch", 2)
-    near = swap(v, "ch", 1)
-    parts = [v, near, far, swap(far, "ch", 1)]
-    n, _, width = v.shape
+    return [v, swap(v, "ch", 1), far, swap(far, "ch", 1)]
+
+
+def widen(parts, me, base, first, blocks):
+    n, _, width = parts[0].shape
     step = n if blocks % n == 0 and first % n == 0 else 1
     inner = n // step
 
     def held(k):
         return lambda r, b, me_ref: (jnp.where(r == k, b, jnp.where(r > k, inner - 1, 0)), 0, 0)
 
-    extra = [] if base is None else [base]
-    return pl.pallas_call(
-        widen_kernel,
-        grid_spec=pltpu.PrefetchScalarGridSpec(
-            num_scalar_prefetch=1,
-            grid=(4, inner),
-            in_specs=[pl.BlockSpec((step, BLK, width), held(k)) for k in range(4)]
-            + [pl.BlockSpec(memory_space=pl.ANY)] * len(extra),
-            out_specs=pl.BlockSpec(
-                (step, BLK, width),
-                lambda r, b, me_ref: (((me_ref[0] ^ r) * blocks + first) // step + b, 0, 0),
+    extra = ([] if base is None else [base]) + before()
+    return done(
+        pl.pallas_call(
+            widen_kernel,
+            grid_spec=pltpu.PrefetchScalarGridSpec(
+                num_scalar_prefetch=1,
+                grid=(4, inner),
+                in_specs=[pl.BlockSpec((step, BLK, width), held(k)) for k in range(4)]
+                + [pl.BlockSpec(memory_space=pl.ANY)] * len(extra),
+                out_specs=pl.BlockSpec(
+                    (step, BLK, width),
+                    lambda r, b, me_ref: (((me_ref[0] ^ r) * blocks + first) // step + b, 0, 0),
+                ),
             ),
-        ),
-        out_shape=jax.ShapeDtypeStruct((4 * blocks, BLK, width), F32),
-        input_output_aliases={5: 0} if extra else {},
-        compiler_params=pltpu.CompilerParams(
-            dimension_semantics=("arbitrary", "arbitrary"), vmem_limit_bytes=VMEM
-        ),
-        cost_estimate=cost(4),
-        name="widen",
-    )(me, *parts, *extra)
+            out_shape=jax.ShapeDtypeStruct((4 * blocks, BLK, width), F32),
+            input_output_aliases={} if base is None else {5: 0},
+            compiler_params=pltpu.CompilerParams(
+                dimension_semantics=("arbitrary", "arbitrary"), vmem_limit_bytes=VMEM
+            ),
+            cost_estimate=cost(4),
+            name="widen",
+        )(me, *parts, *extra)
+    )
 
 
 def row_block(shape, first=0):
@@ -805,8 +974,9 @@
     return pl.BlockSpec(tuple(shape), lambda i, *_: zeros)
 
 
-def call(kernel, name, span, us, scalars, rows, fixed, row_outs, fixed_outs, scratch, specs=None, after=()):
+def call(kernel, name, span, us, scalars, rows, fixed, row_outs, fixed_outs, scratch, specs=None):
     first, count = span
+    after = before()
     if specs is None:
         specs = [row_block(v.shape, first if v.shape[0] > count else 0) for v in rows]
     specs = specs + [v[1] if isinstance(v, tuple) else whole_block(v.shape) for v in fixed]
@@ -818,7 +988,7 @@
         kernel(*refs[:n], *refs[n + len(after) :])
 
     row_outs = [((count,) + s[1:], t) for s, t in row_outs]
-    return pl.pallas_call(
+    made = pl.pallas_call(
         body,
         grid_spec=pltpu.PrefetchScalarGridSpec(
             num_scalar_prefetch=len(scalars),
@@ -834,6 +1004,7 @@
         cost_estimate=cost(us),
         name=name,
     )(*scalars, *rows, *fixed, *after)
+    return done(made)
 
 
 def local(
@@ -852,22 +1023,18 @@
     rows = blocks * BLK
     me = mine.astype(jnp.int32).reshape(1)
 
-    pack1 = gather_pack(jnp.concatenate([w_value, w_reset], axis=0))
-    halves = width // 2
-    pack2 = gather_pack(
-        jnp.concatenate(
-            [jnp.concatenate([w_update, w_cand], axis=1), w_out[:, :halves], w_out[:, halves:]], axis=0
-        )
-    )
-    pack3 = gather_pack(
-        jnp.concatenate([w_up, w_down[:, :halves], w_down[:, halves:]], axis=0)
-    )
-
-    par = pl.pallas_call(
-        prep_kernel, out_shape=jax.ShapeDtypeStruct((5 * dims + 8, channels), F32), name="prep"
-    )(ema_rate.T, ema_beta.T, ema_eta.T, ema_omega[None])
-    par = lax.all_gather(par, "ch", axis=1, tiled=True)
-    rate = par[:dims]
+    ORDER.clear()
+    LANDED.clear()
+    (par,) = small_call(
+        prep_kernel, "prep", [], [ema_rate.T, ema_beta.T, ema_eta.T, ema_omega[None]],
+        [((5 * dims + 8, channels), F32)],
+    )
+    pars = [par] + [swap(par, "ch", r) for r in (1, 2, 3)]
+    packs = small_call(
+        pack_kernel, "pack", [], [w_value, w_reset, w_update, w_cand, w_out, w_up, w_down],
+        [((1024, 256), BF)] * 3,
+    )
+    pack1, pack2, pack3 = (spread(v) for v in packs)
     g_one, g_two = gain_one[None], gain_two[None]
 
     ids = lax.dynamic_slice_in_dim(token_ids, mine * seqs, seqs, 0)
@@ -876,9 +1043,6 @@
     ids = jnp.where(places[None, :] < own_counts[:, None], ids, -1)
     ids_nat = ids.reshape(blocks, 1, BLK)
     ids_tm = ids.reshape(blocks, LANES, STEP).transpose(0, 2, 1).reshape(blocks, 1, BLK)
-
-    bias = jnp.concatenate([position_bias, jnp.zeros((1,), F32)])[None]
-    (bias,) = small_call(table_kernel, "table", [], [bias], [((BLK, BLK), F32)])
 
     row = (blocks, BLK, width)
     row_v = (blocks, BLK, units)
@@ -888,21 +1052,40 @@
     x, emb = call(
         embed_kernel, "embed", every, 4, [], [ids_tm], [embedding, g_one], [(row, F32), (row, BF)], [], []
     )
-    ex, lv = call(
-        enter_kernel, "enter", every, 6, [], [x], [par], [(states, F32), (edge, F32)], [], []
-    )
-    se = block_states(lv, rate, span, False)
+    ex, lv, par = call(
+        enter_kernel, "enter", every, 6, [me], [x], pars, [(states, F32), (edge, F32)],
+        [((5 * dims + 8, width), F32)], [],
+    )
+    made = {}
+
+    def slopes():
+        made["slope"] = call(
+            slope_kernel, "slope", every, 8, [], [x], [par], [(states, F32), (states, F32)], [], []
+        )
+
+    def table():
+        bias = jnp.concatenate([position_bias, jnp.zeros((1,), F32)])[None]
+        (made["bias"],) = small_call(table_kernel, "table", [], [bias], [((BLK, BLK), F32)])
+
+    at_seq = lax.axis_index("seq").astype(jnp.int32).reshape(1)
+    steps = [
+        lambda: None,
+        slopes,
+        table,
+    ]
+    se = block_states(lv, par, at_seq, span, False, steps)
+    el, ed = made["slope"]
+    bias = made["bias"]
     (es,) = call(run_kernel, "run", every, 7, [], [x, ex, se], [par], [(row, F32)], [], [])
     vp, rp, mix, zp, up, cp, res = call(
         forward_kernel, "forward", every, 12, [me], [es, x, emb],
         [bias, w_z, z_scale, z_offset, *pack1, *pack2],
-        [(row_v, BF), (row_v, BF), (row_v, BF), ((blocks, BLK, z_width), F32), (row, BF), (row, BF),
+        [(row_v, F32), (row_v, F32), (row_v, BF), ((blocks, BLK, z_width), F32), (row, BF), (row, BF),
          (row, F32)],
         [],
         [((width, units), BF), ((width, units), BF), ((width, width), BF), ((width, width), BF),
          ((units, width), BF)],
     )
-    at_seq = lax.axis_index("seq").astype(jnp.int32).reshape(1)
     cot = cotangent.reshape(batch * span // BLK, BLK, width)
 
     def pack_outs(rows):
@@ -920,7 +1103,7 @@
         ],
     )
     sum3 = Reduction("ff", at_seq, [keep3], [send3])
-    output = spread(out, me, None, 0, blocks).reshape(batch, span, width)
+    out = spread(out)
 
     def half_of(pack, k):
         return [(v, pl.BlockSpec((512, 256), lambda i, *_: (k, 0))) for v in pack]
@@ -934,76 +1117,120 @@
          ((width, units), F32), ((width, width), F32), ((width, width), F32), ((units, width), F32)],
     )
     sum2 = Reduction("gates", at_seq, [keep2], [send2])
+    land(out[1])
+    sum3.shards()
     g, gnv, ae, lb, keep1, send1 = call(
         mix_back_kernel, "mix_back", every, 24, [], [es, x, vp, zp, gm, ge],
         [bias, w_z, z_scale, z_offset, par, gg2, *half_of(pack1, 0)],
         [(row, F32), (row, BF), (states, F32), (edge, F32)],
         pack_outs(896),
         [((width, units), BF), ((width, units), F32), ((width, z_width), F32),
-         ((8, z_width), F32), ((BLK, BLK), F32)],
-        after=[sum3.shards()],
-    )
-    sum1 = Reduction("mix", at_seq, [keep1], [send1])
-    ar = block_states(lb, rate, span, True)
-    sum3.whole_seq()
-    pins = [[sum2.shards(), sum1.shards()], [sum2.scatter(1)]]
+         ((8, z_width), F32), ((BLK, BLK), F32), ((768, 256), BF)],
+    )
+    sum1 = Reduction("mix", at_seq, [keep1], [send1], repair)
+    locals_ = []
+
+    def adjoint():
+        if len(locals_) < blocks:
+            locals_.append(
+                call(
+                    adjoint_kernel, "adjoint", (len(locals_), 1), 6, [], [x, g, ae, ex, se], [par],
+                    [(row, F32), ((blocks, 2 * dims, width), F32)], [], [],
+                )
+            )
+
+    def between0():
+        land(out[2])
+        sum2.shards()
+        sum3.whole_seq()
+        adjoint()
+
+    def between1():
+        land(out[3])
+        adjoint()
+
+    def between2():
+        sum1.shards()
+        adjoint()
+        sum2.halve()
+
+    ar = block_states(lb, par, at_seq, span, True, [between0, between1, between2])
+    while len(locals_) < blocks:
+        adjoint()
+    sum2.hop(2)
+    sum1.halve()
     parts = [(0, blocks // 2), (blocks // 2, blocks // 2)]
-    keep, send = [], []
-    input_grad = None
-    for part, pin in zip(parts, pins):
+    keep, send, grads = [], [], []
+    for part in parts:
+        rows_in = [ids_tm, emb, x, g, ar, ex, se, el, ed, direct, gnv]
+        mine_in = [v for k in range(part[0], part[0] + part[1]) for v in locals_[k]]
         ig, kept, sent = call(
-            leave_kernel, "leave", part, 15, [me],
-            [ids_tm, emb, x, g, ae, ar, ex, se, direct, gnv],
-            [par, g_one],
+            functools.partial(leave_kernel, part[1]), "leave", part, 8, [me],
+            rows_in, [*mine_in, par, g_one],
             [(row, BF)],
-            pack_outs(256),
-            [((BLK, width), F32), ((dims, LANES, width), F32), ((dims, LANES, width), F32),
-             ((vocab, width), F32), ((1, width), F32), ((1, width), F32), ((3 * dims, width), F32)],
-            after=pin,
+            pack_outs(160),
+            [((BLK, width), F32), ((vocab, width), F32), ((1, width), F32), ((1, width), F32),
+             ((3 * dims, width), F32)],
         )
         keep.append(kept)
         send.append(sent)
-        input_grad = spread(ig, me, input_grad, part[0], blocks)
-    input_grad = input_grad.reshape(batch, span, width)
+        grads.append(spread(ig))
+        if len(grads) == 1:
+            sum1.hop(2)
+            sum2.hop(4)
     last = Reduction("late", at_seq, keep, send)
-    last.shards()
-    emb_part, grad_rate, grad_beta, grad_eta, late = last.rest(
+    sum1.hop(4)
+    last.both()
+    land(grads[0][1], grads[0][2])
+    output = widen(out, me, None, 0, blocks).reshape(batch, span, width)
+    land(grads[1][1])
+    last.hop(2)
+    land(grads[0][3])
+    sum2.hop(1)
+    sum1.hop(1)
+    last.hop(4)
+    land(grads[1][2])
+    input_grad = widen(grads[0], me, None, parts[0][0], blocks)
+    grad_reset, grad_update, grad_cand, grad_out = sum2.join(
+        put_gates,
+        [((width, 256), F32), ((width, 128), F32), ((width, 128), F32), ((256, width), F32)],
+    )
+    last.split()
+    grad_value, grad_z, grad_scale, grad_offset, grad_bias, grad_two = sum1.join(
+        put_mix,
+        [((width, 256), F32), ((width, z_width), F32), ((2, z_width), F32), ((2, z_width), F32),
+         ((1, 255), F32), ((1, width), F32)],
+    )
+    grad_up, grad_down = small_call(
+        put_ff, "ff_join", [], [sum3.whole], [((width, 256), F32), ((256, width), F32)]
+    )
+    emb_part, grad_rate, grad_beta, grad_eta, grad_omega, grad_one = last.join(
         put_late,
         [((64, width), BF), ((dims, channels), F32), ((dims, channels), F32),
-         ((dims, channels), F32), ((16, 128), F32)],
-        (1, 2, 4),
+         ((dims, channels), F32), ((1, channels), F32), ((1, width), F32)],
+        False,
     )
     ge = lax.all_gather(emb_part, "ch", axis=0, tiled=True).astype(F32)
-    grad_up, grad_down = small_call(
-        put_ff, "ff_join", [], [sum3.whole], [((width, 256), F32), ((256, width), F32)]
-    )
-    grad_reset, grad_update, grad_cand, grad_out = sum2.rest(
-        put_gates,
-        [((width, 256), F32), ((width, 128), F32), ((width, 128), F32), ((256, width), F32)],
-        (2, 4),
-    )
-    grad_value, grad_z, small = sum1.rest(
-        put_mix, [((width, 256), F32), ((width, z_width), F32), ((16, 128), F32)], (1, 2, 4)
-    )
+    input_grad = widen(grads[1], me, input_grad, parts[1][0], blocks).reshape(batch, span, width)
     return (
         output,
         input_grad,
         ge,
-        late[4:8].reshape(-1),
+        grad_one[0],
         grad_rate.T,
         grad_beta.T,
         grad_eta.T,
-        late[0],
+        grad_omega[0],
         grad_value,
         grad_reset,
         grad_z,
-        small[0:2],
-        small[2:4],
-        small[4:6].reshape(-1)[:-1],
+        grad_scale,
+        grad_offset,
+        grad_bias[0],
         grad_update,
         grad_cand,
         grad_out,
-        small[6:10].reshape(-1),
+        grad_two[0],
         grad_up,
         grad_down,
     )

time: 355 us -> 296 us (0.83)
  waiting for transfers between devices: 74.4 us -> 17.4 us
  Pallas kernels: 166 us -> 197 us
  starting transfers between devices: 51.2 us -> 36.1 us
  other arithmetic: 13.3 us -> 2.26 us
  blocking collectives: 16.5 us -> 5.98 us
  local copies, waits for them, and re-layouts: 17.6 us -> 22.1 us
    ppermute x51 -> x47, waiting for transfers between devices: 50.7 us -> 16.7 us  [swap(): return lax.ppermute(v, axis, pairs(axis, bit))]
    psum x1, waiting for transfers between devices: 23.7 us -> 0.01 us  [whole_seq(): self.whole = lax.psum(v, 'seq')]
    pallas_call x21 -> x29, Pallas kernels: 42.2 us -> 59.2 us  [small_call(): pl.pallas_call(body, in_specs=[smem] * len(scalars) + [vmem] * len(args)...]
    ppermute x51 -> x47, starting transfers between devices: 51.2 us -> 36.1 us  [swap(): return lax.ppermute(v, axis, pairs(axis, bit))]
    pallas_call x9 -> x14, Pallas kernels: 109 us -> 124 us  [call(): pl.pallas_call(body, grid_spec=pltpu.PrefetchScalarGridSpec(num_scalar_pr...]
    unnamed x99 -> x96, local copies, waits for them, and re-layouts: 9.33 us -> 19.9 us
    all_gather x1 -> x0, blocking collectives: 10.5 us -> none  [local(): par = lax.all_gather(par, 'ch', axis=1, tiled=True)]
    reshape x3 -> x0, local copies, waits for them, and re-layouts: 3.91 us -> none  [the longest x1 1.37 us: local(): small[4:6].reshape(-1)[:-1]]
  transfers between devices with their start and end apart: 52 -> 48, of which waited for: 22 -> 6; matrix products, arithmetic and copies ran while one was open for 6% -> 2% of each run, Pallas kernels for 42% -> 58%
where the time goes in v2:
time: 296 us; the launch traced here: 295 us
  Pallas kernels  197 us (67%)
  starting transfers between devices  36.1 us (12%)
  local copies, waits for them, and re-layouts  22.1 us (7%)
  waiting for transfers between devices  17.4 us (6%)
  between operations  14.4 us (5%)
  blocking collectives  5.98 us (2%)
    pallas_call x14, Pallas kernels, call(): pl.pallas_call(body, grid_spec=pltpu.PrefetchScalarGridSpec(num_scalar_pr...  124 us
    pallas_call x29, Pallas kernels, small_call(): pl.pallas_call(body, in_specs=[smem] * len(scalars) + [vmem] * len(args)...  59.2 us
    ppermute x47, starting transfers between devices, swap(): return lax.ppermute(v, axis, pairs(axis, bit))  36.1 us
    unnamed x96, local copies, waits for them, and re-layouts  19.9 us
    ppermute x47, waiting for transfers between devices, swap(): return lax.ppermute(v, axis, pairs(axis, bit))  16.7 us
    pallas_call x3, Pallas kernels, widen(): pl.pallas_call(widen_kernel, grid_spec=pltpu.PrefetchScalarGridSpec(num_s...  13.8 us
    all_gather x1, blocking collectives, local(): ge = lax.all_gather(emb_part, 'ch', axis=0, tiled=True).astype(F32)  5.98 us
  transfers between devices with their start and end apart: 48, of which 6 were waited for; matrix products, arithmetic and copies ran while one was open for 2% of the time, Pallas kernels for 58%

profile of v2, /device:TPU:0, one launch (start us, length us, event | category | flops | bytes accessed | tf_op | source)
XLA Modules:
  0.0 295.0 jit_solution(10854153809006511004)
XLA Ops:
  8.6 2.4 collective-permute-start.2
  13.4 2.6 pack.1
  15.9 4.0 %embed.1 = (f32[4,256,512]{2,1,0:T(8,128)}, bf16[4,256,512]{2,1,0:T(8,128)(2,1)}) custom-call(s32[4,1,256]{2,1,0:T(1,128)} %reshape.65.refs_0_.refs_1_, bf16[256,512]{1,0:T(8,128)(2,1)} %refs_1_.3, f32[1,512]{1,0:T(1,128)} %bitcast.23, bf16[1024,256]{1,0:T(8,128)(2,1)} %get-tuple-element.109.refs_3_.refs_8_.refs_12_), custom_call_target="tpu_custom_call" | custom-call | flops 4000000000 | bytes 100000 | tf_op jit(solution)/shard_map/embed/pallas_call | solution.py:991
  20.6 5.8 %enter.1 = (f32[4,16,8,512]{3,2,1,0:T(8,128)}, f32[4,16,512]{2,1,0:T(8,128)}, f32[88,512]{1,0:T(8,128)}) custom-call(s32[1]{0:T(128)} %bitcast.refs_0_.me_ref, f32[4,256,512]{2,1,0:T(8,128)} %get-tuple-element.110.refs_1_.refs_6_.refs_0_.refs_2_.refs_3_, f32[88,128]{1,0:T(8,128)} %prep.1.refs_7_.refs_2_, f32[88,128]{1,0:T(8,128)} %copy-done.46, ...), custom_call_target="tpu_custom_call" | custom-call | flops 6000000000 | bytes 100000 | tf_op jit(solution)/shard_map/enter/pallas_call | solution.py:991
  36.5 7.3 %slope.1 = (f32[4,16,8,512]{3,2,1,0:T(8,128)}, f32[4,16,8,512]{3,2,1,0:T(8,128)}) custom-call(f32[4,256,512]{2,1,0:T(8,128)} %get-tuple-element.110.refs_1_.refs_6_.refs_0_.refs_2_.refs_3_, f32[88,512]{1,0:T(8,128)} %get-tuple-element.113.refs_4_.refs_1_.refs_3_.refs_10_.refs_5_.refs_16_, f32[4,16,512]{2,1,0:T(8,128)} %get-tuple-element.114.refs_2_.refs_1_), custom_call_target="tpu_custom_call" | custom-call | flops 8000000000 | bytes 100000 | tf_op jit(solution)/shard_map/slope/pallas_call | solution.py:991
  46.3 2.6 collective-permute-start.5
  48.9 2.6 table.1.refs_5_.refs_4_.refs_6_
  51.5 3.3 %collective-permute-done.5.refs_2_ = f32[4,16,512]{2,1,0:T(8,128)S(1)} collective-permute-done((f32[4,16,512]{2,1,0:T(8,128)}, f32[4,16,512]{2,1,0:T(8,128)S(1)}, u32[]{:S(2)}, u32[]{:S(2)}) %collective-permute-start.5) | collective-permute-done | bytes 131104 | tf_op jit(solution)/shard_map/ppermute | solution.py:712
  58.7 7.6 %run.1.refs_1_.refs_16_.refs_0_ = f32[4,256,512]{2,1,0:T(8,128)} custom-call(f32[4,256,512]{2,1,0:T(8,128)} %get-tuple-element.110.refs_1_.refs_6_.refs_0_.refs_2_.refs_3_, f32[4,16,8,512]{3,2,1,0:T(8,128)} %get-tuple-element.111.refs_5_.refs_1_.refs_3_.refs_6_, f32[4,16,512]{2,1,0:T(8,128)} %get-tuple-element.119.refs_2_.refs_4_.refs_7_, ...), custom_call_target="tpu_custom_call" | custom-call | flops 7000000000 | bytes 100000 | tf_op jit(solution)/shard_map/run/pallas_call | solution.py:991
  66.3 2.3 collective-permute-done.13.refs_7_
  69.9 11.7 %forward.1 = (f32[4,256,1024]{2,1,0:T(8,128)}, f32[4,256,1024]{2,1,0:T(8,128)}, bf16[4,256,1024]{2,1,0:T(8,128)(2,1)}, f32[4,256,128]{2,1,0:T(8,128)}, bf16[4,25...) custom-call(s32[1]{0:T(128)} %bitcast.refs_0_.me_ref, ...), custom_call_target="tpu_custom_call" | custom-call | flops 12000000000 | bytes 100000 | tf_op jit(solution)/shard_map/forward/pallas_call | solution.py:991
  82.4 14.0 %ff.1 = (bf16[4,256,512]{2,1,0:T(8,128)(2,1)}, f32[4,256,512]{2,1,0:T(8,128)}, bf16[2,1024,256]{2,1,0:T(8,128)(2,1)}, bf16[2,1024,256]{2,1,0:T(8,128)(2,1)}, f32[4,128]{1,0:T(4,128)}) custom-call(s32[1]{0:T(128)} %bitcast.refs_0_.me_ref, s32[4,1,256]{2,1,0:T(1,128)} %reshape.61.refs_1_, bf16[16,256,512]{2,1,0:T(8,128)(2,1)} %refs_2_.3, ...), custom_call_target="tpu_custom_call" | custom-call | flops 14000000000 | bytes 100000 | tf_op jit(solution)/shard_map/ff/pallas_call | solution.py:991
  98.3 16.4 %gates_back.1 = (bf16[4,256,1024]{2,1,0:T(8,128)(2,1)}, f32[4,256,512]{2,1,0:T(8,128)}, bf16[4,256,512]{2,1,0:T(8,128)(2,1)}, bf16[2,1536,256]{2,1,0:T(8,128)(2,1)}, bf16[2,1536,256]{2,1,0:T(8,128)(2,1)}) custom-call(s32[1]{0:T(128)} %bitcast.refs_0_.me_ref, f32[4,256,512]{2,1,0:T(8,128)} %run.1.refs_1_.refs_16_.refs_0_, ...), custom_call_target="tpu_custom_call" | custom-call | flops 16999999488 | bytes 100000 | tf_op jit(solution)/shard_map/gates_back/pallas_call | solution.py:991
  115.8 2.6 ff_add.1
  119.1 18.8 %mix_back.1 = (f32[4,256,512]{2,1,0:T(8,128)}, bf16[4,256,512]{2,1,0:T(8,128)(2,1)}, f32[4,16,8,512]{3,2,1,0:T(8,128)}, f32[4,16,512]{2,1,0:T(8,128)}, bf16[2,89...) custom-call(f32[4,256,512]{2,1,0:T(8,128)} %run.1.refs_1_.refs_16_.refs_0_, ...), custom_call_target="tpu_custom_call" | custom-call | flops 24000000000 | bytes 100000 | tf_op jit(solution)/shard_map/mix_back/pallas_call | solution.py:991
  140.7 3.2 %gates_add.1 = (bf16[1536,256]{1,0:T(8,128)(2,1)}, bf16[1536,256]{1,0:T(8,128)(2,1)}) custom-call(bf16[2,1536,256]{2,1,0:T(8,128)(2,1)} %get-tuple-element.143.refs_0_, bf16[2,1536,256]{2,1,0:T(8,128)(2,1)} %copy-done.7, f32[4,256,512]{2,1,0:T(8,128)} %get-tuple-element.139.refs_2_.refs_1_.refs_4_, bf16[4,256,512]{2,1,0:T(8,128)(2,1)} %copy-done.8), custom_call_target="tpu_custom_call" | custom-call | flops 2000000000 | bytes 100000 | tf_op jit(solution)/shard_map/gates_add/pallas_call | solution.py:785
  146.0 5.6 %adjoint.4 = (f32[1,256,512]{2,1,0:T(8,128)}, f32[1,32,512]{2,1,0:T(8,128)}) custom-call(f32[4,256,512]{2,1,0:T(8,128)} %get-tuple-element.110.refs_1_.refs_6_.refs_0_.refs_2_.refs_3_, f32[4,256,512]{2,1,0:T(8,128)} %get-tuple-element.139.refs_2_.refs_1_.refs_4_, f32[4,16,8,512]{3,2,1,0:T(8,128)} %get-tuple-element.141.refs_2_, ...), custom_call_target="tpu_custom_call" | custom-call | flops 6000000000 | bytes 100000 | tf_op jit(solution)/shard_map/adjoint/pallas_call | solution.py:991
  157.1 5.8 %adjoint.5 = (f32[1,256,512]{2,1,0:T(8,128)}, f32[1,32,512]{2,1,0:T(8,128)}) custom-call(f32[4,256,512]{2,1,0:T(8,128)} %get-tuple-element.110.refs_1_.refs_6_.refs_0_.refs_2_.refs_3_, f32[4,256,512]{2,1,0:T(8,128)} %get-tuple-element.139.refs_2_.refs_1_.refs_4_, f32[4,16,8,512]{3,2,1,0:T(8,128)} %get-tuple-element.141.refs_2_, ...), custom_call_target="tpu_custom_call" | custom-call | flops 6000000000 | bytes 100000 | tf_op jit(solution)/shard_map/adjoint/pallas_call | solution.py:991
  167.1 2.5 mix_add.1
  171.3 5.6 %adjoint.6 = (f32[1,256,512]{2,1,0:T(8,128)}, f32[1,32,512]{2,1,0:T(8,128)}) custom-call(f32[4,256,512]{2,1,0:T(8,128)} %get-tuple-element.110.refs_1_.refs_6_.refs_0_.refs_2_.refs_3_, f32[4,256,512]{2,1,0:T(8,128)} %get-tuple-element.139.refs_2_.refs_1_.refs_4_, f32[4,16,8,512]{3,2,1,0:T(8,128)} %get-tuple-element.141.refs_2_, ...), custom_call_target="tpu_custom_call" | custom-call | flops 6000000000 | bytes 100000 | tf_op jit(solution)/shard_map/adjoint/pallas_call | solution.py:991
  177.8 2.6 gates_cut.1
  183.5 5.6 %adjoint.7 = (f32[1,256,512]{2,1,0:T(8,128)}, f32[1,32,512]{2,1,0:T(8,128)}) custom-call(f32[4,256,512]{2,1,0:T(8,128)} %get-tuple-element.110.refs_1_.refs_6_.refs_0_.refs_2_.refs_3_, f32[4,256,512]{2,1,0:T(8,128)} %get-tuple-element.139.refs_2_.refs_1_.refs_4_, f32[4,16,8,512]{3,2,1,0:T(8,128)} %get-tuple-element.141.refs_2_, ...), custom_call_target="tpu_custom_call" | custom-call | flops 6000000000 | bytes 100000 | tf_op jit(solution)/shard_map/adjoint/pallas_call | solution.py:991
  189.1 2.8 collective-permute-done.27.refs_1_
  198.3 7.7 %leave.2 = (bf16[2,256,512]{2,1,0:T(8,128)(2,1)}, bf16[2,160,256]{2,1,0:T(8,128)(2,1)}, bf16[2,160,256]{2,1,0:T(8,128)(2,1)}) custom-call(s32[1]{0:T(128)} %bitcast.refs_0_.me_ref, s32[4,1,256]{2,1,0:T(1,128)} %reshape.65.refs_0_.refs_1_, bf16[4,256,512]{2,1,0:T(8,128)(2,1)} %get-tuple-element.121.refs_3_.refs_2_, ...), custom_call_target="tpu_custom_call" | custom-call | flops 8000000000 | bytes 100000 | tf_op jit(solution)/shard_map/leave/pallas_call | solution.py:991
  216.0 7.8 %leave.3 = (bf16[2,256,512]{2,1,0:T(8,128)(2,1)}, bf16[2,160,256]{2,1,0:T(8,128)(2,1)}, bf16[2,160,256]{2,1,0:T(8,128)(2,1)}) custom-call(s32[1]{0:T(128)} %bitcast.refs_0_.me_ref, s32[4,1,256]{2,1,0:T(1,128)} %reshape.65.refs_0_.refs_1_, bf16[4,256,512]{2,1,0:T(8,128)(2,1)} %get-tuple-element.121.refs_3_.refs_2_, ...), custom_call_target="tpu_custom_call" | custom-call | flops 8000000000 | bytes 100000 | tf_op jit(solution)/shard_map/leave/pallas_call | solution.py:991
  231.0 5.8 %widen.3.refs_2_ = f32[16,256,512]{2,1,0:T(8,128)} custom-call(s32[1]{0:T(128)} %bitcast.refs_0_.me_ref, bf16[4,256,512]{2,1,0:T(8,128)(2,1)} %get-tuple-element.126.refs_16_.refs_0_, bf16[4,256,512]{2,1,0:T(8,128)(2,1)} %copy-done.9, bf16[4,256,512]{2,1,0:T(8,128)(2,1)} %copy-done.8, bf16[4,256,512]{2,1,0:T(8,128)(2,1)} %copy-done.10, ...), custom_call_target="tpu_custom_call" | custom-call | flops 4000000000 | bytes 100000 | tf_op jit(solution)/shard_map/widen/pallas_call | solution.py:944
  246.4 4.6 %collective-permute-done.41.refs_1_ = bf16[448,256]{1,0:T(8,128)(2,1)S(1)} collective-permute-done((bf16[448,256]{1,0:T(8,128)(2,1)S(1)}, bf16[448,256]{1,0:T(8,128)(2,1)S(1)}, u32[]{:S(2)}, u32[]{:S(2)}) %collective-permute-start.41) | collective-permute-done | bytes 229408 | tf_op jit(solution)/shard_map/ppermute | solution.py:712
  256.3 4.0 %widen.4.refs_3_.refs_4_ = f32[16,256,512]{2,1,0:T(8,128)} custom-call(s32[1]{0:T(128)} %bitcast.refs_0_.me_ref, bf16[2,256,512]{2,1,0:T(8,128)(2,1)} %get-tuple-element.173.refs_2_.refs_0_, bf16[2,256,512]{2,1,0:T(8,128)(2,1)} %copy-done.18, bf16[2,256,512]{2,1,0:T(8,128)(2,1)} %copy-done.17, bf16[2,256,512]{2,1,0:T(8,128)(2,1)} %copy-done.22, ...), custom_call_target="tpu_custom_call" | custom-call | flops 4000000000 | bytes 100000 | tf_op jit(solution)/shard_map/widen/pallas_call | solution.py:944
  261.0 2.4 gates_join.1
  263.4 2.8 collective-permute-done.43.refs_1_
  276.5 6.0 %all_gather.3 = bf16[256,512]{1,0:T(8,128)(2,1)S(1)} all-gather(bf16[64,512]{1,0:T(8,128)(2,1)} %get-tuple-element.183.refs_5_), channel_id=1, replica_groups=mesh['seq'=8,'ch'=4] {'ch'}, dimensions={0}, use_global_device_ids=true | all-gather | bytes 327680 | tf_op jit(solution)/shard_map/all_gather | solution.py:1213
  284.1 4.0 %widen.5 = f32[16,256,512]{2,1,0:T(8,128)} custom-call(s32[1]{0:T(128)} %bitcast.refs_0_.me_ref, bf16[2,256,512]{2,1,0:T(8,128)(2,1)} %get-tuple-element.177.refs_2_.refs_0_, bf16[2,256,512]{2,1,0:T(8,128)(2,1)} %copy-done, bf16[2,256,512]{2,1,0:T(8,128)(2,1)} %copy-done.2, bf16[2,256,512]{2,1,0:T(8,128)(2,1)} %copy-done.3, ...), custom_call_target="tpu_custom_call", output_to_operand_aliasing={{}: (5, {})} | custom-call | flops 4000000000 | bytes 100000 | tf_op jit(solution)/shard_map/widen/pallas_call | solution.py:944
  (218 shorter events, 97.9 us)
Async XLA Ops:
  28.0 30.0 %collective-permute-start.10 = (bf16[1024,256]{1,0:T(8,128)(2,1)S(1)}, bf16[1024,256]{1,0:T(8,128)(2,1)S(1)}, u32[]{:S(2)}, u32[]{:S(2)}) collective-permute-start(bf16[1024,256]{1,0:T(8,128)(2,1)S(1)} %copy-done.15), channel_id=1, source_target_pairs={{0,2},{1,3},{2,0},{3,1},{4,6},{5,7},{6,4},{7,5},{8,10},{9,11},{10,... | collective-permute-start | bytes 1572872 | tf_op jit(solution)/shard_map/ppermute | solution.py:712
  29.6 39.0 %collective-permute-start.9 = (bf16[1024,256]{1,0:T(8,128)(2,1)S(1)}, bf16[1024,256]{1,0:T(8,128)(2,1)S(1)}, u32[]{:S(2)}, u32[]{:S(2)}) collective-permute-start(bf16[1024,256]{1,0:T(8,128)(2,1)S(1)} %copy-done.15), channel_id=1, source_target_pairs={{0,1},{1,0},{2,3},{3,2},{4,5},{5,4},{6,7},{7,6},{8,9},{9,8},{10,11... | collective-permute-start | bytes 1572872 | tf_op jit(solution)/shard_map/ppermute | solution.py:712
  29.6 28.6 %collective-permute-start.7 = (bf16[1024,256]{1,0:T(8,128)(2,1)S(1)}, bf16[1024,256]{1,0:T(8,128)(2,1)S(1)}, u32[]{:S(2)}, u32[]{:S(2)}) collective-permute-start(bf16[1024,256]{1,0:T(8,128)(2,1)S(1)} %copy-done.13), channel_id=1, source_target_pairs={{0,2},{1,3},{2,0},{3,1},{4,6},{5,7},{6,4},{7,5},{8,10},{9,11},{10,... | collective-permute-start | bytes 1572872 | tf_op jit(solution)/shard_map/ppermute | solution.py:712
  30.1 39.0 %collective-permute-start.6 = (bf16[1024,256]{1,0:T(8,128)(2,1)S(1)}, bf16[1024,256]{1,0:T(8,128)(2,1)S(1)}, u32[]{:S(2)}, u32[]{:S(2)}) collective-permute-start(bf16[1024,256]{1,0:T(8,128)(2,1)S(1)} %copy-done.13), channel_id=1, source_target_pairs={{0,1},{1,0},{2,3},{3,2},{4,5},{5,4},{6,7},{7,6},{8,9},{9,8},{10,11... | collective-permute-start | bytes 1572872 | tf_op jit(solution)/shard_map/ppermute | solution.py:712
  54.8 13.8 %collective-permute-start.13 = (bf16[1024,256]{1,0:T(8,128)(2,1)S(1)}, bf16[1024,256]{1,0:T(8,128)(2,1)}, u32[]{:S(2)}, u32[]{:S(2)}) collective-permute-start(bf16[1024,256]{1,0:T(8,128)(2,1)S(1)} %copy-done.19), channel_id=1, source_target_pairs={{0,2},{1,3},{2,0},{3,1},{4,6},{5,7},{6,4},{7,5},{8,10},{9,11},{10,... | collective-permute-start | bytes 1572872 | tf_op jit(solution)/shard_map/ppermute | solution.py:712
  68.6 13.0 %collective-permute-start.12 = (bf16[1024,256]{1,0:T(8,128)(2,1)S(1)}, bf16[1024,256]{1,0:T(8,128)(2,1)}, u32[]{:S(2)}, u32[]{:S(2)}) collective-permute-start(bf16[1024,256]{1,0:T(8,128)(2,1)S(1)} %copy-done.19), channel_id=1, source_target_pairs={{0,1},{1,0},{2,3},{3,2},{4,5},{5,4},{6,7},{7,6},{8,9},{9,8},{10,11... | collective-permute-start | bytes 1572872 | tf_op jit(solution)/shard_map/ppermute | solution.py:712
  68.6 13.0 %collective-permute-start.14 = (bf16[1024,256]{1,0:T(8,128)(2,1)}, bf16[1024,256]{1,0:T(8,128)(2,1)S(1)}, u32[]{:S(2)}, u32[]{:S(2)}) collective-permute-start(bf16[1024,256]{1,0:T(8,128)(2,1)} %collective-permute-done.13.refs_7_), channel_id=1, source_target_pairs={{0,1},{1,0},{2,3},{3,2},{4,5},{5,4},{6,7},{7,6},{8,9},{9,8},{10,11... | collective-permute-start | bytes 1572872 | tf_op jit(solution)/shard_map/ppermute | solution.py:712
  96.4 42.7 %collective-permute-start.16 = (bf16[4,256,512]{2,1,0:T(8,128)(2,1)}, bf16[4,256,512]{2,1,0:T(8,128)(2,1)S(1)}, u32[]{:S(2)}, u32[]{:S(2)}) collective-permute-start(bf16[4,256,512]{2,1,0:T(8,128)(2,1)} %get-tuple-element.126.refs_16_.refs_0_), channel_id=1, source_target_pairs={{0,2},{1,3},{2,0},{3,1},{4,6},{5,7},{6,4},{7,5},{8,10},{9,11},{10,... | collective-permute-start | bytes 3145736 | tf_op jit(solution)/shard_map/ppermute | solution.py:712
  97.8 17.0 %collective-permute-start.15 = (bf16[4,256,512]{2,1,0:T(8,128)(2,1)}, bf16[4,256,512]{2,1,0:T(8,128)(2,1)S(1)}, u32[]{:S(2)}, u32[]{:S(2)}) collective-permute-start(bf16[4,256,512]{2,1,0:T(8,128)(2,1)} %get-tuple-element.126.refs_16_.refs_0_), channel_id=1, source_target_pairs={{0,1},{1,0},{2,3},{3,2},{4,5},{5,4},{6,7},{7,6},{8,9},{9,8},{10,11... | collective-permute-start | bytes 3145736 | tf_op jit(solution)/shard_map/ppermute | solution.py:712
  97.8 17.0 %collective-permute-start.18 = (bf16[2,1024,256]{2,1,0:T(8,128)(2,1)}, bf16[2,1024,256]{2,1,0:T(8,128)(2,1)}, u32[]{:S(2)}, u32[]{:S(2)}) collective-permute-start(bf16[2,1024,256]{2,1,0:T(8,128)(2,1)} %get-tuple-element.137), channel_id=1, source_target_pairs={{0,1},{1,0},{2,3},{3,2},{4,5},{5,4},{6,7},{7,6},{8,9},{9,8},{10,11... | collective-permute-start | bytes 3145736 | tf_op jit(solution)/shard_map/ppermute | solution.py:712
  114.8 24.8 %collective-permute-start.21 = (bf16[2,1536,256]{2,1,0:T(8,128)(2,1)}, bf16[2,1536,256]{2,1,0:T(8,128)(2,1)S(1)}, u32[]{:S(2)}, u32[]{:S(2)}) collective-permute-start(bf16[2,1536,256]{2,1,0:T(8,128)(2,1)} %get-tuple-element.144), channel_id=1, source_target_pairs={{0,1},{1,0},{2,3},{3,2},{4,5},{5,4},{6,7},{7,6},{8,9},{9,8},{10,11... | collective-permute-start | bytes 4718600 | tf_op jit(solution)/shard_map/ppermute | solution.py:712
  118.5 25.4 %collective-permute-start.20 = (bf16[1024,256]{1,0:T(8,128)(2,1)}, bf16[1024,256]{1,0:T(8,128)(2,1)}, u32[]{:S(2)}, u32[]{:S(2)}) collective-permute-start(bf16[1024,256]{1,0:T(8,128)(2,1)} %get-tuple-element.142), channel_id=1, source_target_pairs={{0,2},{1,3},{2,0},{3,1},{4,6},{5,7},{6,4},{7,5},{8,10},{9,11},{10,... | collective-permute-start | bytes 1572872 | tf_op jit(solution)/shard_map/ppermute | solution.py:712
  137.9 14.4 %collective-permute-start.19 = (f32[4,16,512]{2,1,0:T(8,128)}, f32[4,16,512]{2,1,0:T(8,128)S(1)}, u32[]{:S(2)}, u32[]{:S(2)}) collective-permute-start(f32[4,16,512]{2,1,0:T(8,128)} %get-tuple-element.140.refs_1_), channel_id=1, source_target_pairs={{0,4},{4,0},{8,12},{12,8},{16,20},{20,16},{24,28},{28,24},{1,5},{5... | collective-permute-start | bytes 393224 | tf_op jit(solution)/shard_map/ppermute | solution.py:712
  139.0 28.0 %collective-permute-start.25 = (bf16[2,896,256]{2,1,0:T(8,128)(2,1)}, bf16[2,896,256]{2,1,0:T(8,128)(2,1)}, u32[]{:S(2)}, u32[]{:S(2)}) collective-permute-start(bf16[2,896,256]{2,1,0:T(8,128)(2,1)} %get-tuple-element.154), channel_id=1, source_target_pairs={{0,1},{1,0},{2,3},{3,2},{4,5},{5,4},{6,7},{7,6},{8,9},{9,8},{10,11... | collective-permute-start | bytes 2752520 | tf_op jit(solution)/shard_map/ppermute | solution.py:712
  139.0 17.1 %collective-permute-start.17 = (bf16[4,256,512]{2,1,0:T(8,128)(2,1)S(1)}, bf16[4,256,512]{2,1,0:T(8,128)(2,1)S(1)}, u32[]{:S(2)}, u32[]{:S(2)}) collective-permute-start(bf16[4,256,512]{2,1,0:T(8,128)(2,1)S(1)} %collective-permute-done.16.refs_3_.refs_2_), channel_id=1, source_target_pairs={{0,1},{1,0},{2,3},{3,2},{4,5},{5,4},{6,7},{7,6},{8,9},{9,8},{10,11... | collective-permute-start | bytes 3145736 | tf_op jit(solution)/shard_map/ppermute | solution.py:712
  151.6 120.6 %all-reduce.2.cloned.1.call-start = ((), (), s32[]{:S(2)}) async-start(), calls=%async_computation | async-start | bytes 1048576 | tf_op jit(solution)/shard_map/psum | solution.py:839
  154.9 22.0 %collective-permute-start.24 = (bf16[1536,256]{1,0:T(8,128)(2,1)S(1)}, bf16[1536,256]{1,0:T(8,128)(2,1)S(1)}, u32[]{:S(2)}, u32[]{:S(2)}) collective-permute-start(bf16[1536,256]{1,0:T(8,128)(2,1)S(1)} %copy-done.11), channel_id=1, source_target_pairs={{0,2},{1,3},{2,0},{3,1},{4,6},{5,7},{6,4},{7,5},{8,10},{9,11},{10,... | collective-permute-start | bytes 2359304 | tf_op jit(solution)/shard_map/ppermute | solution.py:712
  165.5 15.5 %collective-permute-start.23 = (f32[4,16,512]{2,1,0:T(8,128)}, f32[4,16,512]{2,1,0:T(8,128)S(1)}, u32[]{:S(2)}, u32[]{:S(2)}) collective-permute-start(f32[4,16,512]{2,1,0:T(8,128)} %get-tuple-element.150.refs_2_.refs_1_), channel_id=1, source_target_pairs={{0,16},{4,20},{8,24},{12,28},{16,0},{20,4},{24,8},{28,12},{1,17},{... | collective-permute-start | bytes 393224 | tf_op jit(solution)/shard_map/ppermute | solution.py:712
  169.5 25.4 %collective-permute-start.26 = (bf16[896,256]{1,0:T(8,128)(2,1)}, bf16[896,256]{1,0:T(8,128)(2,1)S(1)}, u32[]{:S(2)}, u32[]{:S(2)}) collective-permute-start(bf16[896,256]{1,0:T(8,128)(2,1)} %get-tuple-element.164), channel_id=1, source_target_pairs={{0,2},{1,3},{2,0},{3,1},{4,6},{5,7},{6,4},{7,5},{8,10},{9,11},{10,... | collective-permute-start | bytes 1376264 | tf_op jit(solution)/shard_map/ppermute | solution.py:712
  194.6 17.7 %collective-permute-start.28 = (bf16[768,256]{1,0:T(8,128)(2,1)}, bf16[768,256]{1,0:T(8,128)(2,1)S(1)}, u32[]{:S(2)}, u32[]{:S(2)}) collective-permute-start(bf16[768,256]{1,0:T(8,128)(2,1)} %gates_sum.3.refs_3_.refs_0_), channel_id=1, source_target_pairs={{0,8},{4,12},{8,0},{12,4},{16,24},{20,28},{24,16},{28,20},{1,9},{5... | collective-permute-start | bytes 1179656 | tf_op jit(solution)/shard_map/ppermute | solution.py:712
  206.0 21.0 %collective-permute-start.34 = (bf16[2,256,512]{2,1,0:T(8,128)(2,1)}, bf16[2,256,512]{2,1,0:T(8,128)(2,1)S(1)}, u32[]{:S(2)}, u32[]{:S(2)}) collective-permute-start(bf16[2,256,512]{2,1,0:T(8,128)(2,1)} %get-tuple-element.173.refs_2_.refs_0_), channel_id=1, source_target_pairs={{0,2},{1,3},{2,0},{3,1},{4,6},{5,7},{6,4},{7,5},{8,10},{9,11},{10,... | collective-permute-start | bytes 1572872 | tf_op jit(solution)/shard_map/ppermute | solution.py:712
  207.6 22.0 %collective-permute-start.33 = (bf16[2,256,512]{2,1,0:T(8,128)(2,1)}, bf16[2,256,512]{2,1,0:T(8,128)(2,1)S(1)}, u32[]{:S(2)}, u32[]{:S(2)}) collective-permute-start(bf16[2,256,512]{2,1,0:T(8,128)(2,1)} %get-tuple-element.173.refs_2_.refs_0_), channel_id=1, source_target_pairs={{0,1},{1,0},{2,3},{3,2},{4,5},{5,4},{6,7},{7,6},{8,9},{9,8},{10,11... | collective-permute-start | bytes 1572872 | tf_op jit(solution)/shard_map/ppermute | solution.py:712
  207.6 18.7 %collective-permute-start.30 = (bf16[2,160,256]{2,1,0:T(8,128)(2,1)}, bf16[2,160,256]{2,1,0:T(8,128)(2,1)S(1)}, u32[]{:S(2)}, u32[]{:S(2)}) collective-permute-start(bf16[2,160,256]{2,1,0:T(8,128)(2,1)} %get-tuple-element.175), channel_id=1, source_target_pairs={{0,1},{1,0},{2,3},{3,2},{4,5},{5,4},{6,7},{7,6},{8,9},{9,8},{10,11... | collective-permute-start | bytes 491528 | tf_op jit(solution)/shard_map/ppermute | solution.py:712
  210.6 13.2 %collective-permute-start.32 = (bf16[448,256]{1,0:T(8,128)(2,1)}, bf16[448,256]{1,0:T(8,128)(2,1)S(1)}, u32[]{:S(2)}, u32[]{:S(2)}) collective-permute-start(bf16[448,256]{1,0:T(8,128)(2,1)} %mix_sum.3.refs_2_.refs_0_), channel_id=1, source_target_pairs={{0,8},{4,12},{8,0},{12,4},{16,24},{20,28},{24,16},{28,20},{1,9},{5... | collective-permute-start | bytes 688136 | tf_op jit(solution)/shard_map/ppermute | solution.py:712
  215.0 26.9 %collective-permute-start.42 = (bf16[768,256]{1,0:T(8,128)(2,1)}, bf16[768,256]{1,0:T(8,128)(2,1)S(1)}, u32[]{:S(2)}, u32[]{:S(2)}) collective-permute-start(bf16[768,256]{1,0:T(8,128)(2,1)} %gates_sum.4.refs_18_.refs_0_), channel_id=1, source_target_pairs={{0,16},{4,20},{8,24},{12,28},{16,0},{20,4},{24,8},{28,12},{1,17},{... | collective-permute-start | bytes 1179656 | tf_op jit(solution)/shard_map/ppermute | solution.py:712
  226.4 15.5 %collective-permute-start.36 = (bf16[2,256,512]{2,1,0:T(8,128)(2,1)S(1)}, bf16[2,256,512]{2,1,0:T(8,128)(2,1)S(1)}, u32[]{:S(2)}, u32[]{:S(2)}) collective-permute-start(bf16[2,256,512]{2,1,0:T(8,128)(2,1)S(1)} %copy-done.1), channel_id=1, source_target_pairs={{0,2},{1,3},{2,0},{3,1},{4,6},{5,7},{6,4},{7,5},{8,10},{9,11},{10,... | collective-permute-start | bytes 1572872 | tf_op jit(solution)/shard_map/ppermute | solution.py:712
  227.0 14.9 %collective-permute-start.38 = (bf16[2,256,512]{2,1,0:T(8,128)(2,1)S(1)}, bf16[2,256,512]{2,1,0:T(8,128)(2,1)S(1)}, u32[]{:S(2)}, u32[]{:S(2)}) collective-permute-start(bf16[2,256,512]{2,1,0:T(8,128)(2,1)S(1)} %collective-permute-done.34.refs_6_.refs_2_), channel_id=1, source_target_pairs={{0,1},{1,0},{2,3},{3,2},{4,5},{5,4},{6,7},{7,6},{8,9},{9,8},{10,11... | collective-permute-start | bytes 1572872 | tf_op jit(solution)/shard_map/ppermute | solution.py:712
  236.8 14.1 %collective-permute-start.41 = (bf16[448,256]{1,0:T(8,128)(2,1)S(1)}, bf16[448,256]{1,0:T(8,128)(2,1)S(1)}, u32[]{:S(2)}, u32[]{:S(2)}) collective-permute-start(bf16[448,256]{1,0:T(8,128)(2,1)S(1)} %copy-done.28), channel_id=1, source_target_pairs={{0,16},{4,20},{8,24},{12,28},{16,0},{20,4},{24,8},{28,12},{1,17},{... | collective-permute-start | bytes 688136 | tf_op jit(solution)/shard_map/ppermute | solution.py:712
  241.6 12.4 %collective-permute-start.40 = (bf16[2,160,256]{2,1,0:T(8,128)(2,1)}, bf16[2,160,256]{2,1,0:T(8,128)(2,1)S(1)}, u32[]{:S(2)}, u32[]{:S(2)}) collective-permute-start(bf16[2,160,256]{2,1,0:T(8,128)(2,1)} %late_sum.2.refs_2_.refs_0_), channel_id=1, source_target_pairs={{0,8},{4,12},{8,0},{12,4},{16,24},{20,28},{24,16},{28,20},{1,9},{5... | collective-permute-start | bytes 491528 | tf_op jit(solution)/shard_map/ppermute | solution.py:712
  241.9 41.4 %collective-permute-start.37 = (bf16[2,256,512]{2,1,0:T(8,128)(2,1)S(1)}, bf16[2,256,512]{2,1,0:T(8,128)(2,1)S(1)}, u32[]{:S(2)}, u32[]{:S(2)}) collective-permute-start(bf16[2,256,512]{2,1,0:T(8,128)(2,1)S(1)} %collective-permute-done.36.refs_5_.refs_2_), channel_id=1, source_target_pairs={{0,1},{1,0},{2,3},{3,2},{4,5},{5,4},{6,7},{7,6},{8,9},{9,8},{10,11... | collective-permute-start | bytes 1572872 | tf_op jit(solution)/shard_map/ppermute | solution.py:712
  245.5 14.8 %collective-permute-start.44 = (bf16[768,256]{1,0:T(8,128)(2,1)}, bf16[768,256]{1,0:T(8,128)(2,1)S(1)}, u32[]{:S(2)}, u32[]{:S(2)}) collective-permute-start(bf16[768,256]{1,0:T(8,128)(2,1)} %gates_sum.5.refs_2_.refs_1_), channel_id=1, source_target_pairs={{0,4},{4,0},{8,12},{12,8},{16,20},{20,16},{24,28},{28,24},{1,5},{5... | collective-permute-start | bytes 1179656 | tf_op jit(solution)/shard_map/ppermute | solution.py:712
  253.4 16.1 %collective-permute-start.46 = (bf16[448,256]{1,0:T(8,128)(2,1)}, bf16[448,256]{1,0:T(8,128)(2,1)S(1)}, u32[]{:S(2)}, u32[]{:S(2)}) collective-permute-start(bf16[448,256]{1,0:T(8,128)(2,1)} %mix_sum.5.refs_2_.refs_1_), channel_id=1, source_target_pairs={{0,4},{4,0},{8,12},{12,8},{16,20},{20,16},{24,28},{28,24},{1,5},{5... | collective-permute-start | bytes 688136 | tf_op jit(solution)/shard_map/ppermute | solution.py:712
  (64 other events, 242.7 us)
Sparse Core Ops, SparseCore 0:
  156.4 85.9 all-reduce.1
